TPU v7x, 256 devices: a whole 4x4x8 slice. The times are simulated.
256 devices in a mesh: dp: 2 (over core), ctx: 4 (over x), expert: 32 (over z, y).
Axes of the slice: x: 4, y: 4, z: 8, core: 2. Of those that a mesh axis runs over, the one named last changes fastest.
Arguments:
- tokens: bfloat16 [2, 16384, 2048], P('dp', ('ctx', 'expert')), may hold values from -6 to 6
- out_grad: bfloat16 [2, 16384, 2048], P('dp', ('ctx', 'expert')), may hold values from -6 to 6
- w_in: bfloat16 [32, 2048, 512], P('expert'), may hold values from -0.125 to 0.125
- w_out: bfloat16 [32, 512, 2048], P('expert'), may hold values from -0.25 to 0.25
- picks: int32 [2, 32, 1024], P('dp'), may hold values from 0 to 16383, as said below
- gates: float32 [2, 32, 1024], P('dp', 'expert', 'ctx'), may hold values from 0.1 to 1
Outputs:
- tok_grad: bfloat16 [2, 16384, 2048], P('dp', ('ctx', 'expert'))
- w_in_grad: bfloat16 [32, 2048, 512], P('expert')
- w_out_grad: bfloat16 [32, 512, 2048], P('expert')
- gate_grad: float32 [2, 32, 1024], P('dp', 'expert', 'ctx')
Inputs may be any that keep to these rules, and one draw needn't show every extreme that they name: `picks`: for every group and expert the 1024 entries are distinct. Within each quarter of an expert's list (entries q * 256 to (q + 1) * 256 - 1) at most 4 entries fall into any one block of 128 consecutive tokens, and some block holds exactly 4.
All inputs are finite; a program needn't handle non-finite values.
Results may differ from a plain program's by a relative error of at most 0.017.
Values may be sent and summed in bfloat16 or wider, within the bound.
No kernel may reach another device: no remote copies, remote signals or barrier semaphores. Data moves between devices by JAX's collectives and lax.ppermute only.
A program may use at most 128 MiB of HBM per device.

v0:
```python
import jax
import jax.numpy as jnp
from jax import lax
from jax.sharding import PartitionSpec as P


def silu_slope(pre_act):
    sigmoid_v = jax.nn.sigmoid(pre_act)
    return sigmoid_v * (1.0 + pre_act * (1.0 - sigmoid_v))


def expert_pass(rows_in, rows_grad, gate_rows, weight_in, weight_out):
    pre_act = jnp.dot(rows_in, weight_in, preferred_element_type=jnp.float32)
    activation = jax.nn.silu(pre_act).astype(jnp.bfloat16)
    expert_out = jnp.dot(activation, weight_out, preferred_element_type=jnp.float32)
    gate_part = jnp.sum(rows_grad.astype(jnp.float32) * expert_out, axis=-1)
    scaled = (gate_rows[:, None] * rows_grad.astype(jnp.float32)).astype(jnp.bfloat16)
    act_grad = lax.dot_general(
        scaled, weight_out, (((1,), (1,)), ((), ())), preferred_element_type=jnp.float32
    )
    pre_grad = (act_grad * silu_slope(pre_act)).astype(jnp.bfloat16)
    row_grads = lax.dot_general(
        pre_grad, weight_in, (((1,), (1,)), ((), ())), preferred_element_type=jnp.float32
    ).astype(jnp.bfloat16)
    return (activation, scaled, pre_grad, row_grads, gate_part)


def shards(tokens, out_grad, w_in, w_out, picks, gates):
    ctx_count = lax.axis_size("ctx")
    exp_count = lax.axis_size("expert")
    blocks = ctx_count * exp_count
    ctx_index = lax.axis_index("ctx")
    exp_index = lax.axis_index("expert")
    my_block = ctx_index * exp_count + exp_index
    tok_dev = tokens.shape[1]
    feat_width = tokens.shape[2]
    pick_total = picks.shape[2]
    share_len = pick_total // ctx_count
    slot_cap = 2 * (share_len // blocks)
    slot_rows = blocks * slot_cap
    grad_scale = (lax.axis_size("dp") * pick_total) ** (-0.5)
    pick_lists = jnp.transpose(
        picks[0].reshape(exp_count, ctx_count, share_len), (1, 0, 2)
    ).reshape(blocks, share_len)
    is_mine = pick_lists // tok_dev == my_block
    pick_rank = jnp.cumsum(is_mine.astype(jnp.int32), axis=1) - 1
    local_row = pick_lists - my_block * tok_dev
    chosen = is_mine[:, :, None] & (pick_rank[:, :, None] == jnp.arange(slot_cap)[None, None, :])
    row_table = jnp.sum(jnp.where(chosen, local_row[:, :, None], 0), axis=1)
    filled = jnp.any(chosen, axis=1)
    stacked = jnp.stack((tokens[0], out_grad[0]))
    outgoing = jnp.where(
        filled[None, :, :, None], stacked[:, row_table], jnp.zeros((), jnp.bfloat16)
    )
    arrived = lax.all_to_all(outgoing, ("ctx", "expert"), split_axis=1, concat_axis=1, tiled=True)
    arrived = arrived.reshape(2, slot_rows, feat_width)
    expert_row = lax.dynamic_index_in_dim(picks[0], exp_index, 0, keepdims=False)
    own_list = lax.dynamic_slice_in_dim(expert_row, ctx_index * share_len, share_len)
    source = own_list // tok_dev
    source_hits = (source[:, None] == jnp.arange(blocks)[None, :]).astype(jnp.int32)
    order_in = jnp.sum((jnp.cumsum(source_hits, axis=0) - 1) * source_hits, axis=1)
    position = source * slot_cap + order_in
    weight_in = w_in[0]
    weight_out = w_out[0]
    gate_now = gates[0, 0]
    rows_in = arrived[0]
    rows_grad = arrived[1]
    slot_gate = jnp.zeros((slot_rows,), jnp.float32).at[position].set(gate_now)
    activation, scaled, pre_grad, row_grads, gate_part = expert_pass(
        rows_in, rows_grad, slot_gate, weight_in, weight_out
    )
    gate_grad = gate_part[position]
    in_term = (
        lax.dot_general(
            rows_in, pre_grad, (((0,), (0,)), ((), ())), preferred_element_type=jnp.float32
        )
        * grad_scale
    )
    out_term = (
        lax.dot_general(
            activation, scaled, (((0,), (0,)), ((), ())), preferred_element_type=jnp.float32
        )
        * grad_scale
    )
    in_total, out_total = (
        lax.psum(in_term.astype(jnp.bfloat16), ("dp", "ctx")).astype(jnp.float32),
        lax.psum(out_term.astype(jnp.bfloat16), ("dp", "ctx")).astype(jnp.float32),
    )
    returned = lax.all_to_all(
        row_grads.reshape(blocks, slot_cap, feat_width),
        ("ctx", "expert"),
        split_axis=0,
        concat_axis=0,
        tiled=True,
    )
    returned = returned.reshape(slot_rows, feat_width).astype(jnp.float32)
    token_total = (
        jnp.zeros((tok_dev, feat_width), jnp.float32).at[row_table.reshape(slot_rows)].add(returned)
    )
    return (
        token_total.astype(jnp.bfloat16)[None],
        in_total.astype(jnp.bfloat16)[None],
        out_total.astype(jnp.bfloat16)[None],
        gate_grad[None, None],
    )


def solution(mesh):
    placed = (
        P("dp", ("ctx", "expert"), None),
        P("dp", ("ctx", "expert"), None),
        P("expert", None, None),
        P("expert", None, None),
        P("dp", None, None),
        P("dp", "expert", "ctx"),
    )
    return jax.shard_map(
        shards,
        mesh=mesh,
        in_specs=placed,
        out_specs=(
            P("dp", ("ctx", "expert"), None),
            P("expert", None, None),
            P("expert", None, None),
            P("dp", "expert", "ctx"),
        ),
        check_vma=False,
    )
```

profile of v0, /device:TPU:6, one launch (start us, length us, event | category | flops | bytes accessed | tf_op | source)
XLA Modules:
  0.0 295.9 jit_solution(14968755299943214022)
XLA Ops:
  7.2 1.1 reshape_squeeze.3
  8.4 0.1 fusion.21
  8.6 0.1 copy.49
  8.7 0.3 fusion.22
  9.2 0.1 copy.54
  9.3 0.2 fusion.19
  9.4 0.2 select_reduce_fusion
  9.6 0.1 copy.58
  9.8 0.1 copy.61
  9.9 0.1 reshape.276
  10.0 0.8 copy.59
  10.8 1.9 copy.60
  12.7 2.4 pad_maximum_fusion
  15.1 18.5 %gather_fusion = bf16[512,2,2048]{2,1,0:T(2,128)(2,1)} fusion(bf16[2,128,2048]{2,0,1:T(2,128)(2,1)S(1)} %pad_maximum_fusion, s32[1024]{0:T(1024)S(1)} %pad_clamp_fusion.1), kind=kCustom, calls=%fused_computation | custom fusion | bytes 8390656 | tf_op jit(solution)/shard_map/gather | solution.py:53
  33.6 6.7 %fusion = bf16[2,128,4,2048]{3,2,0,1:T(4,128)(2,1)} fusion(bf16[128,4,2,2048]{3,2,1,0:T(2,128)(2,1)} %bitcast.71, pred[128,4]{1,0:T(8,128)(4,1)S(1)} %copy.58), kind=kLoop, calls=%fused_computation.5 | loop fusion | flops 2097152 | bytes 8389120 | tf_op jit(solution)/shard_map/jit(_where)/select_n | solution.py:52
  40.3 16.5 %all-to-all-start = ((bf16[2,128,4,2048]{3,2,0,1:T(4,128)(2,1)}), bf16[2,128,4,2048]{3,2,0,1:T(4,128)(2,1)}, u32[]{:S(2)}, u32[]{:S(2)}) async-start(bf16[2,128,4,2048]{3,2,0,1:T(4,128)(2,1)} %fusion), calls=%async_computation | async-start | bytes 8388608 | tf_op jit(solution)/shard_map/all_to_all | solution.py:55
  56.9 0.8 constant_dynamic-slice_fusion
  57.7 0.1 copy.56
  57.8 0.2 fusion.23
  58.1 0.2 fusion.24
  58.3 0.8 compare_select_fusion.1
  59.1 1.6 scatter_custom_fusion
  60.7 0.1 mul.74
  60.8 90.5 %all-to-all-done = bf16[2,128,4,2048]{3,2,0,1:T(4,128)(2,1)} async-done(((bf16[2,128,4,2048]{3,2,0,1:T(4,128)(2,1)}), bf16[2,128,4,2048]{3,2,0,1:T(4,128)(2,1)}, u32[]{:S(2)}, u32[]{:S(2)}) %all-to-all-start) | async-done | bytes 4194336 | tf_op jit(solution)/shard_map/all_to_all | solution.py:55
  151.2 3.8 %multiply_convert_fusion.3 = bf16[1,128,4,2048]{3,2,0,1:T(4,128)(2,1)} fusion(f32[128,4]{1,0:T(8,128)S(1)} %mul.74, bf16[2,128,4,2048]{3,2,0,1:T(4,128)(2,1)} %all-to-all-done), kind=kLoop, calls=%fused_computation.10 | loop fusion | flops 3145728 | bytes 4196352 | tf_op jit(solution)/shard_map/convert_element_type | solution.py:17
  155.0 3.9 %convert_element_type.59 = bf16[512,2048]{1,0:T(8,128)(2,1)} reshape(bf16[1,128,4,2048]{3,2,0,1:T(4,128)(2,1)} %multiply_convert_fusion.3) | data formatting | bytes 4194304 | tf_op jit(solution)/shard_map/convert_element_type | solution.py:17
  159.0 5.1 %slice_convert_fusion = (f32[1,128,4,2048]{3,2,0,1:T(4,128)}, bf16[1,128,4,2048]{3,2,0,1:T(4,128)(2,1)}) fusion(bf16[2,128,4,2048]{3,2,0,1:T(4,128)(2,1)} %all-to-all-done), kind=kLoop, calls=%fused_computation.14 | loop fusion | flops 1048576 | bytes 10485760 | tf_op jit(solution)/shard_map/convert_element_type | solution.py:17
  164.1 4.0 %squeeze.18 = bf16[512,2048]{1,0:T(8,128)(2,1)} reshape(bf16[1,128,4,2048]{3,2,0,1:T(4,128)(2,1)} %get-tuple-element.7) | data formatting | bytes 4194304 | tf_op jit(solution)/shard_map/squeeze | solution.py:66
  168.1 3.0 %fusion.4 = f32[512,512]{1,0:T(8,128)S(1)} fusion(bf16[512,2048]{1,0:T(8,128)(2,1)} %squeeze.18, bf16[1,2048,512]{2,1,0:T(8,128)(2,1)S(1)} %copy-done), kind=kOutput, calls=%fused_computation.16 | convolution fusion | flops 1073741824 | bytes 5242880 | tf_op jit(solution)/shard_map/dot_general | solution.py:13
  171.1 1.5 fusion.13
  172.6 2.6 convolution_convert_fusion
  175.2 4.1 %reshape.271 = bf16[128,4,2048]{2,1,0:T(4,128)(2,1)} reshape(bf16[512,2048]{1,0:T(8,128)(2,1)} %convolution_convert_fusion) | data formatting | bytes 4194304 | tf_op jit(solution)/shard_map/reshape | solution.py:90
  179.3 10.3 %all-to-all-start.1 = ((bf16[128,4,2048]{2,1,0:T(4,128)(2,1)}), bf16[128,4,2048]{2,1,0:T(4,128)(2,1)}, u32[]{:S(2)}, u32[]{:S(2)}) async-start(bf16[128,4,2048]{2,1,0:T(4,128)(2,1)} %reshape.271), calls=%async_computation.1 | async-start | bytes 4194304 | tf_op jit(solution)/shard_map/all_to_all | solution.py:89
  189.5 0.3 all-reduce.3.cloned.1.call-start
  189.8 5.3 %reshape.273 = f32[512,2048]{1,0:T(8,128)} reshape(f32[1,128,4,2048]{3,2,0,1:T(4,128)} %get-tuple-element.6) | data formatting | bytes 8388608 | tf_op jit(solution)/shard_map/convert_element_type | solution.py:17
  195.1 4.4 %fusion.1 = bf16[1,2048,512]{2,1,0:T(8,128)(2,1)} fusion(bf16[512,2048]{1,0:T(8,128)(2,1)} %squeeze.18, bf16[512,512]{1,0:T(8,128)(2,1)S(1)} %fusion.13), kind=kOutput, calls=%fused_computation.12 | convolution fusion | flops 1075838976 | bytes 4718592 | tf_op jit(solution)/shard_map/dot_general | solution.py:74
  199.4 2.8 fusion.2
  202.2 0.1 copy.55
  202.3 0.1 reshape.269
  202.5 4.5 %multiply_reduce_fusion = f32[512]{0:T(512)S(1)} fusion(f32[512,2048]{1,0:T(8,128)} %reshape.273, bf16[1,512,2048]{2,1,0:T(8,128)(2,1)} %param.9, f32[512,512]{1,0:T(8,128)} %copy-done.6), kind=kOutput, calls=%fused_computation.6 | convolution fusion | flops 1077149184 | bytes 7342080 | tf_op jit(solution)/shard_map/dot_general | solution.py:15
  207.0 2.5 gather_fusion.1
  209.5 29.2 %all-to-all-done.1 = bf16[128,4,2048]{2,1,0:T(4,128)(2,1)} async-done(((bf16[128,4,2048]{2,1,0:T(4,128)(2,1)}), bf16[128,4,2048]{2,1,0:T(4,128)(2,1)}, u32[]{:S(2)}, u32[]{:S(2)}) %all-to-all-start.1) | async-done | bytes 2097184 | tf_op jit(solution)/shard_map/all_to_all | solution.py:89
  238.7 4.2 %reshape.302 = f32[512,2048]{1,0:T(8,128)} reshape(bf16[128,4,2048]{2,1,0:T(4,128)(2,1)} %all-to-all-done.1) | data formatting | bytes 6291456 | tf_op jit(solution)/shard_map/convert_element_type | solution.py:96
  243.0 8.8 %scatter_custom_fusion.1 = f32[128,2048]{1,0:T(8,128)S(1)} fusion(s32[512]{0:T(512)S(1)} %bitcast.79, f32[512,2048]{1,0:T(8,128)} %reshape.302, f32[]{:T(128)} %constant.79.clone.1), kind=kCustom, calls=%fused_computation.30 | custom fusion | flops 1048576 | bytes 1049088 | tf_op jit(solution)/shard_map/scatter-add | solution.py:98
  251.8 0.9 convert_bitcast_fusion
  252.6 32.0 %all-reduce.3.cloned.1.call-done = (bf16[1,2048,512]{2,1,0:T(8,128)(2,1)}, bf16[1,512,2048]{2,1,0:T(8,128)(2,1)}) async-done(((bf16[1,2048,512]{2,1,0:T(8,128)(2,1)}, bf16[1,512,2048]{2,1,0:T(8,128)(2,1)}), (bf16[1,2048,512]{2,1,0:T(8,128)(2,1)}, bf16[1,512,2048]{2,1,0:T(8,128)(2,1)})) %all-reduce.3.cloned.1.call-update) | async-done | bytes 4194320 | tf_op jit(solution)/shard_map/psum | solution.py:86
  284.6 3.2 %copy.68 = bf16[1,2048,512]{2,1,0:T(8,128)(2,1)} copy(bf16[1,2048,512]{2,1,0:T(8,128)(2,1)} %get-tuple-element.9) | data formatting | bytes 4194304
  287.8 1.3 copy.69
  (36 shorter events, 0.4 us)
Async XLA Ops:
  7.2 160.9 %copy-start = (bf16[1,2048,512]{2,1,0:T(8,128)(2,1)S(1)}, bf16[1,2048,512]{2,1,0:T(8,128)(2,1)}, u32[]{:S(2)}) copy-start(bf16[1,2048,512]{2,1,0:T(8,128)(2,1)} %param.8) | copy-start | bytes 6291460
  7.2 2.8 copy-start.4
  40.3 110.9 %all-to-all-start = ((bf16[2,128,4,2048]{3,2,0,1:T(4,128)(2,1)}), bf16[2,128,4,2048]{3,2,0,1:T(4,128)(2,1)}, u32[]{:S(2)}, u32[]{:S(2)}) async-start(bf16[2,128,4,2048]{3,2,0,1:T(4,128)(2,1)} %fusion), calls=%async_computation | async-start | bytes 8388608 | tf_op jit(solution)/shard_map/all_to_all | solution.py:55
  168.1 3.0 %copy-start.3 = (bf16[512,2048]{1,0:T(8,128)(2,1)S(1)}, bf16[512,2048]{1,0:T(8,128)(2,1)}, u32[]{:S(2)}) copy-start(bf16[512,2048]{1,0:T(8,128)(2,1)} %convert_element_type.59) | copy-start | bytes 6291460
  168.1 3.0 %copy-start.5 = (bf16[1,512,2048]{2,1,0:T(8,128)(2,1)S(1)}, bf16[1,512,2048]{2,1,0:T(8,128)(2,1)}, u32[]{:S(2)}) copy-start(bf16[1,512,2048]{2,1,0:T(8,128)(2,1)} %param.9) | copy-start | bytes 6291460
  171.1 1.5 copy-start.6
  179.3 59.5 %all-to-all-start.1 = ((bf16[128,4,2048]{2,1,0:T(4,128)(2,1)}), bf16[128,4,2048]{2,1,0:T(4,128)(2,1)}, u32[]{:S(2)}, u32[]{:S(2)}) async-start(bf16[128,4,2048]{2,1,0:T(4,128)(2,1)} %reshape.271), calls=%async_computation.1 | async-start | bytes 4194304 | tf_op jit(solution)/shard_map/all_to_all | solution.py:89
  189.5 95.1 %all-reduce.3.cloned.1.call-start = ((), (), s32[]{:S(2)}) async-start(), calls=%async_computation.2 | async-start | bytes 8388608 | tf_op jit(solution)/shard_map/psum | solution.py:86
  195.1 4.4 %copy-start.1 = (f32[512,2048]{1,0:T(8,128)S(1)}, f32[512,2048]{1,0:T(8,128)}, u32[]{:S(2)}) copy-start(f32[512,2048]{1,0:T(8,128)} %reshape.273) | copy-start | bytes 12582916
  195.1 4.4 %copy-start.7 = (f32[512,512]{1,0:T(8,128)S(1)}, f32[512,512]{1,0:T(8,128)}, u32[]{:S(2)}) copy-start(f32[512,512]{1,0:T(8,128)} %copy-done.6) | copy-start | bytes 3145732
  284.6 3.2 %copy-start.2 = (bf16[1,512,2048]{2,1,0:T(8,128)(2,1)S(1)}, bf16[1,512,2048]{2,1,0:T(8,128)(2,1)}, u32[]{:S(2)}) copy-start(bf16[1,512,2048]{2,1,0:T(8,128)(2,1)} %get-tuple-element.10) | copy-start | bytes 6291460
Sparse Core Ops, SparseCore 0:
  202.4 82.1 all-reduce.2
where the time goes:
time: 300 us; the launch traced here: 296 us
  waiting for transfers between devices  152 us (51%)
  local copies, waits for them, and re-layouts  54.4 us (18%)
  other arithmetic  29.8 us (10%)
  starting transfers between devices  27 us (9%)
  matrix products  18.7 us (6%)
  between operations  14.3 us (5%)
    all_to_all x1, waiting for transfers between devices, shards(): lax.all_to_all(outgoing, ('ctx', 'expert'), split_axis=1, concat_axis=1,...  90.5 us
    psum x1, waiting for transfers between devices, shards(): lax.psum(in_term.astype(jnp.bfloat16), ('dp', 'ctx')).astype(jnp.float32)  32 us
    all_to_all x1, waiting for transfers between devices, shards(): lax.all_to_all(row_grads.reshape(blocks, slot_cap, feat_width), ('ctx', '...  29.2 us
    gather x1, local copies, waits for them, and re-layouts, shards(): stacked[:, row_table]  18.5 us
    all_to_all x1, starting transfers between devices, shards(): lax.all_to_all(outgoing, ('ctx', 'expert'), split_axis=1, concat_axis=1,...  16.5 us
    all_to_all x1, starting transfers between devices, shards(): lax.all_to_all(row_grads.reshape(blocks, slot_cap, feat_width), ('ctx', '...  10.3 us
    scatter-add x1, other arithmetic, shards(): jnp.zeros((tok_dev, feat_width), jnp.float32)  8.77 us
    unnamed x20, local copies, waits for them, and re-layouts  7.21 us
  transfers between devices with their start and end apart: 3, of which 3 were waited for; matrix products, arithmetic and copies ran while one was open for 13% of the time, Pallas kernels for 0%

commit v1 on v0

v1 whole, which is shorter than its diff:
```python
import jax
import jax.numpy as jnp
from jax import lax
from jax.sharding import PartitionSpec as P

BF = jnp.bfloat16
F32 = jnp.float32


def dot(left, right, dims):
    return lax.dot_general(left, right, (dims, ((), ())), preferred_element_type=F32)


def ring(count, step):
    return [(i, (i + step) % count) for i in range(count)]


def earlier(count):
    rows = lax.broadcasted_iota(jnp.int32, (count, count), 0)
    cols = lax.broadcasted_iota(jnp.int32, (count, count), 1)
    return (rows < cols).astype(BF)


def reduce_dp(part):
    core = lax.axis_index("dp")
    half = part.shape[0] // 2
    mine = lax.dynamic_slice_in_dim(part, core * half, half)
    other = lax.dynamic_slice_in_dim(part, (1 - core) * half, half)
    got = lax.ppermute(other, "dp", ring(2, 1))
    return (mine.astype(F32) + got.astype(F32)).astype(BF)


def gather_dp(part):
    core = lax.axis_index("dp")
    other = lax.ppermute(part, "dp", ring(2, 1))
    return jnp.where(
        core == 0, jnp.concatenate((part, other), 0), jnp.concatenate((other, part), 0)
    )


def reduce_ctx(part):
    count = lax.axis_size("ctx")
    index = lax.axis_index("ctx")
    size = part.shape[0] // count

    def piece(step):
        return lax.dynamic_slice_in_dim(part, ((index + step) % count) * size, size)

    steps = (2, 1, 3)
    got = [lax.ppermute(piece(step), "ctx", ring(count, step)) for step in steps]
    total = piece(0).astype(F32)
    for term in got:
        total = total + term.astype(F32)
    total = total.astype(BF)
    whole = jnp.zeros_like(part)
    whole = lax.dynamic_update_slice_in_dim(whole, total, index * size, 0)
    for step in steps:
        term = lax.ppermute(total, "ctx", ring(count, step))
        whole = lax.dynamic_update_slice_in_dim(whole, term, ((index - step) % count) * size, 0)
    return whole


def shards(tokens, out_grad, w_in, w_out, picks, gates):
    ctx_count = lax.axis_size("ctx")
    exp_count = lax.axis_size("expert")
    ctx_index = lax.axis_index("ctx")
    exp_index = lax.axis_index("expert")
    tok_dev, feat = tokens.shape[1], tokens.shape[2]
    pick_total = picks.shape[2]
    share = pick_total // ctx_count
    slots = ctx_count * 4
    slot_rows = exp_count * slots
    grad_scale = (lax.axis_size("dp") * pick_total) ** (-0.5)
    lists = picks[0]
    before = earlier(tok_dev)
    tok_ids = jnp.arange(tok_dev, dtype=jnp.int32)
    slot_ids = jnp.arange(slots, dtype=jnp.int32)

    local = lists - (ctx_index * exp_count + exp_index) * tok_dev
    picked = jnp.any(local[:, :, None] == tok_ids[None, None, :], axis=1)
    rank = dot(picked.astype(BF), before, ((1,), (0,))).astype(jnp.int32)
    spread = picked[:, None, :] & (rank[:, None, :] == slot_ids[None, :, None])
    spread = spread.astype(BF).reshape(slot_rows, tok_dev)

    def send(rows):
        out = dot(spread, rows, ((1,), (0,))).astype(BF)
        out = lax.all_to_all(
            out.reshape(exp_count, slots, feat), "expert", split_axis=0, concat_axis=0, tiled=True
        )
        return out.reshape(slot_rows, feat)

    rows_in = send(tokens[0])
    rows_grad = send(out_grad[0])

    own = lax.dynamic_index_in_dim(lists, exp_index, 0, keepdims=False)
    offset = own - ctx_index * (exp_count * tok_dev)
    block = offset // tok_dev
    inside = (block >= 0) & (block < exp_count)
    token = offset % tok_dev
    in_block = (inside[:, None] & (block[:, None] == jnp.arange(exp_count)[None, :])).astype(BF)
    at_token = (token[:, None] == tok_ids[None, :]).astype(BF)
    held = dot(in_block, at_token, ((0,), (0,))).astype(BF)
    rank_own = dot(held, before, ((1,), (0,))).astype(BF)
    rank_pick = jnp.sum(
        dot(in_block, rank_own, ((1,), (0,))) * at_token.astype(F32), axis=1
    ).astype(jnp.int32)
    place = jnp.where(inside, block * slots + rank_pick, -1)
    at_slot = place[:, None] == jnp.arange(slot_rows, dtype=jnp.int32)[None, :]
    gate_all = lax.all_gather(gates[0, 0], "ctx", tiled=True)
    slot_gate = jnp.sum(jnp.where(at_slot, gate_all[:, None], 0.0), axis=0)

    weight_in = w_in[0]
    weight_out = w_out[0]
    pre_act = dot(rows_in, weight_in, ((1,), (0,)))
    sig = jax.nn.sigmoid(pre_act)
    activation = (pre_act * sig).astype(BF)
    slope = sig * (1.0 + pre_act * (1.0 - sig))
    back = dot(rows_grad, weight_out, ((1,), (1,)))
    pre_grad = (slot_gate[:, None] * back * slope).astype(BF)
    row_grads = dot(pre_grad, weight_in, ((1,), (1,))).astype(BF)
    returned = lax.all_to_all(
        row_grads.reshape(exp_count, slots, feat), "expert", split_axis=0, concat_axis=0, tiled=True
    ).reshape(slot_rows, feat)

    gated = (slot_gate[:, None] * activation.astype(F32)).astype(BF)
    out_part = (dot(gated, rows_grad, ((0,), (0,))) * grad_scale).astype(BF)
    in_part = (dot(rows_in, pre_grad, ((0,), (0,))) * grad_scale).astype(BF)
    out_total = gather_dp(reduce_ctx(reduce_dp(out_part)))
    in_total = gather_dp(reduce_ctx(reduce_dp(in_part)))

    gate_slot = jnp.sum(activation.astype(F32) * back, axis=1)
    gate_pick = jnp.sum(jnp.where(at_slot, gate_slot[None, :], 0.0), axis=1)
    gate_grad = lax.psum_scatter(gate_pick, "ctx", tiled=True)

    token_total = dot(spread, returned, ((0,), (0,))).astype(BF)
    return (
        token_total[None],
        in_total[None],
        out_total[None],
        gate_grad.reshape(1, 1, share),
    )


def solution(mesh):
    placed = (
        P("dp", ("ctx", "expert"), None),
        P("dp", ("ctx", "expert"), None),
        P("expert", None, None),
        P("expert", None, None),
        P("dp", None, None),
        P("dp", "expert", "ctx"),
    )
    return jax.shard_map(
        shards,
        mesh=mesh,
        in_specs=placed,
        out_specs=(
            P("dp", ("ctx", "expert"), None),
            P("expert", None, None),
            P("expert", None, None),
            P("dp", "expert", "ctx"),
        ),
        check_vma=False,
    )
```

time: 300 us -> 226 us (0.75)
  local copies, waits for them, and re-layouts: 54.4 us -> 7.82 us
  waiting for transfers between devices: 152 us -> 113 us
  blocking collectives: 0 us -> 14.6 us
  between operations: 14.3 us -> 1.68 us
  starting transfers between devices: 27 us -> 39 us
  other arithmetic: 29.8 us -> 22.8 us
  matrix products: 18.7 us -> 24.1 us
    all_to_all x2 -> x3, waiting for transfers between devices: 120 us -> 85.6 us  [the longest x2 85.6 us: send(): lax.all_to_all(out.reshape(exp_count, slots, feat), 'expert', split_axis=...]
    psum x1 -> x0, waiting for transfers between devices: 32 us -> none  [shards(): lax.psum(in_term.astype(jnp.bfloat16), ('dp', 'ctx')).astype(jnp.float32)]
    ppermute x0 -> x16, waiting for transfers between devices: none -> 27.5 us  [the longest x6 17.5 us: reduce_ctx(): lax.ppermute(piece(step), 'ctx', ring(count, step))]
    gather x2 -> x0, local copies, waits for them, and re-layouts: 21 us -> none  [the longest x1 18.5 us: shards(): stacked[:, row_table]]
    ppermute x0 -> x16, starting transfers between devices: none -> 15 us  [the longest x6 8.28 us: reduce_ctx(): lax.ppermute(piece(step), 'ctx', ring(count, step))]
    convert_element_type x3 -> x0, local copies, waits for them, and re-layouts: 13.5 us -> none  [the longest x1 5.29 us: expert_pass(): rows_grad.astype(jnp.float32)]
    scatter-add x1 -> x0, other arithmetic: 8.77 us -> none  [shards(): jnp.zeros((tok_dev, feat_width), jnp.float32)]
    unnamed x0 -> x1, blocking collectives: none -> 7.83 us
  transfers between devices with their start and end apart: 3 -> 19, of which waited for: 3 -> 10; matrix products, arithmetic and copies ran while one was open for 13% -> 14% of each run, Pallas kernels for 0% -> 0%
where the time goes in v1:
time: 226 us; the launch traced here: 223 us
  waiting for transfers between devices  113 us (50%)
  starting transfers between devices  39 us (17%)
  matrix products  24.1 us (11%)
  other arithmetic  22.8 us (10%)
  blocking collectives  14.6 us (6%)
  local copies, waits for them, and re-layouts  7.82 us (3%)
    all_to_all x2, waiting for transfers between devices, send(): lax.all_to_all(out.reshape(exp_count, slots, feat), 'expert', split_axis=...  85.6 us
    dot_general x11, matrix products, dot(): lax.dot_general(left, right, (dims, ((), ())), preferred_element_type=F32)  24.1 us
    all_to_all x2, starting transfers between devices, send(): lax.all_to_all(out.reshape(exp_count, slots, feat), 'expert', split_axis=...  17.9 us
    ppermute x6, waiting for transfers between devices, reduce_ctx(): lax.ppermute(piece(step), 'ctx', ring(count, step))  17.5 us
    ppermute x6, waiting for transfers between devices, reduce_ctx(): term = lax.ppermute(total, 'ctx', ring(count, step))  9.96 us
    ppermute x6, starting transfers between devices, reduce_ctx(): lax.ppermute(piece(step), 'ctx', ring(count, step))  8.28 us
    select_n x2, other arithmetic, gather_dp(): jnp.where(core == 0, jnp.concatenate((part, other), 0), jnp.concatenate((...  8.27 us
    unnamed x1, blocking collectives  7.83 us
  transfers between devices with their start and end apart: 19, of which 10 were waited for; matrix products, arithmetic and copies ran while one was open for 14% of the time, Pallas kernels for 0%

profile of v1, /device:TPU:6, one launch (start us, length us, event | category | flops | bytes accessed | tf_op | source)
XLA Modules:
  0.0 223.1 jit_solution(10995141401725550495)
XLA Ops:
  0.7 1.1 subtract_bitcast_fusion
  1.7 5.7 %fusion = pred[32,128]{1,0:T(8,128)(4,1)S(1)} fusion(s32[32,1024]{1,0:T(8,128)S(1)} %subtract_bitcast_fusion), kind=kLoop, calls=%fused_computation.1 | loop fusion | flops 8384512 | bytes 135168 | tf_op jit(solution)/shard_map/reduce_or | solution.py:80
  7.6 3.1 %convolution_convert_fusion.1 = bf16[512,2048]{1,0:T(8,128)(2,1)} fusion(pred[512,128]{1,0:T(8,128)(4,1)S(1)} %bitcast.55, bf16[1,128,2048]{2,1,0:T(8,128)(2,1)} %param.6), kind=kOutput, calls=%fused_computation.5 | convolution fusion | flops 269484032 | bytes 2686976 | tf_op jit(solution)/shard_map/dot_general | solution.py:11
  10.7 11.7 %all-to-all-start.1 = ((bf16[32,16,2048]{2,1,0:T(8,128)(2,1)}), bf16[32,16,2048]{2,1,0:T(8,128)(2,1)}, u32[]{:S(2)}, u32[]{:S(2)}) async-start(bf16[32,16,2048]{2,1,0:T(8,128)(2,1)} %bitcast.52), calls=%async_computation.1 | async-start | bytes 4194304 | tf_op jit(solution)/shard_map/all_to_all | solution.py:87
  22.4 2.0 convolution_convert_fusion.2
  24.5 48.1 %all-to-all-done.1 = bf16[32,16,2048]{2,1,0:T(8,128)(2,1)} async-done(((bf16[32,16,2048]{2,1,0:T(8,128)(2,1)}), bf16[32,16,2048]{2,1,0:T(8,128)(2,1)}, u32[]{:S(2)}, u32[]{:S(2)}) %all-to-all-start.1) | async-done | bytes 2097184 | tf_op jit(solution)/shard_map/all_to_all | solution.py:87
  72.6 6.2 %all-to-all-start = ((bf16[32,16,2048]{2,1,0:T(8,128)(2,1)}), bf16[32,16,2048]{2,1,0:T(8,128)(2,1)}, u32[]{:S(2)}, u32[]{:S(2)}) async-start(bf16[32,16,2048]{2,1,0:T(8,128)(2,1)} %bitcast.51), calls=%async_computation | async-start | bytes 4194304 | tf_op jit(solution)/shard_map/all_to_all | solution.py:87
  78.9 6.7 %all-gather = f32[1,1,1024]{2,1,0:T(1,128)S(1)} all-gather(f32[1,1,256]{2,1,0:T(1,128)S(1)} %copy-done.7), channel_id=2, replica_groups=mesh['dp'=2,'ctx'=4,'expert'=32] {'ctx'}, dimensions={2}, use_global_device_ids=true | all-gather | bytes 5120 | tf_op jit(solution)/shard_map/all_gather | solution.py:109
  85.6 0.8 fusion.26
  87.5 2.9 %fusion.4 = f32[512,512]{0,1:T(8,128)S(1)} fusion(bf16[512,2048]{1,0:T(8,128)(2,1)} %bitcast.10, bf16[1,2048,512]{2,1,0:T(8,128)(2,1)S(1)} %copy-done), kind=kOutput, calls=%fused_computation.13 | convolution fusion | flops 1073741824 | bytes 5242880 | tf_op jit(solution)/shard_map/dot_general | solution.py:11
  90.4 37.5 %all-to-all-done = bf16[32,16,2048]{2,1,0:T(8,128)(2,1)} async-done(((bf16[32,16,2048]{2,1,0:T(8,128)(2,1)}), bf16[32,16,2048]{2,1,0:T(8,128)(2,1)}, u32[]{:S(2)}, u32[]{:S(2)}) %all-to-all-start) | async-done | bytes 2097184 | tf_op jit(solution)/shard_map/all_to_all | solution.py:87
  127.9 3.6 %fusion.10 = (f32[512]{0:T(512)S(1)}, f32[512,512]{0,1:T(8,128)S(1)}) fusion(f32[512,512]{0,1:T(8,128)S(1)} %fusion.4, bf16[512,2048]{1,0:T(8,128)(2,1)} %bitcast.6, bf16[1,512,2048]{2,1,0:T(8,128)(2,1)} %param.9), kind=kOutput, calls=%fused_computation.30 | convolution fusion | flops 1075838464 | bytes 6293504 | tf_op jit(solution)/shard_map/dot_general | solution.py:11
  131.5 0.7 select_reduce_fusion
  132.2 2.9 %multiply_convert_fusion = bf16[512,2048]{1,0:T(8,128)(2,1)S(1)} fusion(bf16[512,2048]{1,0:T(8,128)(2,1)} %bitcast.6, f32[512]{0:T(512)S(1)} %get-tuple-element.5, f32[512,512]{0,1:T(8,128)S(1)} %fusion.4), kind=kOutput, calls=%fused_computation.2 | convolution fusion | flops 1077936128 | bytes 5244928 | tf_op jit(solution)/shard_map/dot_general | solution.py:11
  135.1 1.1 constant_dynamic-slice_fusion.3
  137.2 2.9 %multiply_convert_fusion.1 = bf16[2048,512]{1,0:T(8,128)(2,1)S(1)} fusion(bf16[512,2048]{1,0:T(8,128)(2,1)} %bitcast.10, bf16[512,512]{0,1:T(8,128)(2,1)S(1)} %multiply_convert_fusion.3), kind=kOutput, calls=%fused_computation.3 | convolution fusion | flops 1075838976 | bytes 4718592 | tf_op jit(solution)/shard_map/dot_general | solution.py:11
  140.1 1.3 copy-done.2
  141.7 2.6 %convolution_convert_fusion = bf16[512,2048]{1,0:T(8,128)(2,1)} fusion(bf16[512,512]{0,1:T(8,128)(2,1)S(1)} %multiply_convert_fusion.3, bf16[1,2048,512]{2,1,0:T(8,128)(2,1)S(1)} %copy-done), kind=kOutput, calls=%fused_computation.4 | convolution fusion | flops 1074790400 | bytes 4718592 | tf_op jit(solution)/shard_map/dot_general | solution.py:11
  144.4 6.1 %all-to-all-start.2 = ((bf16[32,16,2048]{2,1,0:T(8,128)(2,1)}), bf16[32,16,2048]{2,1,0:T(8,128)(2,1)}, u32[]{:S(2)}, u32[]{:S(2)}) async-start(bf16[32,16,2048]{2,1,0:T(8,128)(2,1)} %bitcast.54), calls=%async_computation.2 | async-start | bytes 4194304 | tf_op jit(solution)/shard_map/all_to_all | solution.py:121
  150.5 2.1 add_convert_fusion
  153.2 1.5 collective-permute-start.11
  154.8 1.4 collective-permute-start.9
  156.2 1.5 add_convert_fusion.1
  157.8 2.2 collective-permute-start.1
  160.0 1.7 collective-permute-start.2
  161.9 0.9 collective-permute-start.3
  162.7 10.5 %collective-permute-done.11 = bf16[64,2048]{1,0:T(8,128)(2,1)S(1)} collective-permute-done((bf16[64,2048]{1,0:T(8,128)(2,1)S(1)}, bf16[64,2048]{1,0:T(8,128)(2,1)S(1)}, u32[]{:S(2)}, u32[]{:S(2)}) %collective-permute-start.11) | collective-permute-done | bytes 262176 | tf_op jit(solution)/shard_map/ppermute | solution.py:50
  173.2 1.1 broadcast_in_dim.30
  174.3 0.9 constant_dynamic-update-slice_fusion.3
  175.3 2.0 collective-permute-start.14
  177.3 1.6 collective-permute-done.2
  178.9 5.3 %collective-permute-done.3 = bf16[256,512]{1,0:T(8,128)(2,1)} collective-permute-done((bf16[256,512]{1,0:T(8,128)(2,1)S(1)}, bf16[256,512]{1,0:T(8,128)(2,1)}, u32[]{:S(2)}, u32[]{:S(2)}) %collective-permute-start.3) | collective-permute-done | bytes 262176 | tf_op jit(solution)/shard_map/ppermute | solution.py:50
  184.2 1.3 constant_dynamic-update-slice_fusion.7
  185.6 2.1 collective-permute-start.4
  187.7 2.0 collective-permute-start.6
  189.7 0.7 constant_dynamic-update-slice_fusion.2
  190.4 0.7 constant_dynamic-update-slice_fusion.1
  191.2 4.5 %collective-permute-done.14 = bf16[64,2048]{1,0:T(8,128)(2,1)S(1)} collective-permute-done((bf16[64,2048]{1,0:T(8,128)(2,1)}, bf16[64,2048]{1,0:T(8,128)(2,1)S(1)}, u32[]{:S(2)}, u32[]{:S(2)}) %collective-permute-start.14) | collective-permute-done | bytes 262176 | tf_op jit(solution)/shard_map/ppermute | solution.py:58
  195.6 0.7 constant_dynamic-update-slice_fusion
  196.4 0.8 collective-permute-done.4
  197.2 3.5 %collective-permute-done.5 = bf16[256,512]{1,0:T(8,128)(2,1)S(1)} collective-permute-done((bf16[256,512]{1,0:T(8,128)(2,1)S(1)}, bf16[256,512]{1,0:T(8,128)(2,1)S(1)}, u32[]{:S(2)}, u32[]{:S(2)}) %collective-permute-start.5) | collective-permute-done | bytes 262176 | tf_op jit(solution)/shard_map/ppermute | solution.py:58
  200.6 1.3 collective-permute-done.6
  202.3 0.6 dynamic-slice.1
  203.5 7.8 %all-reduce = f32[1024]{0:T(1024)S(1)} all-reduce(f32[1024]{0:T(1024)S(1)} %get-tuple-element.4), channel_id=3, replica_groups=mesh['dp'=2,'ctx'=4,'expert'=32] {'ctx'}, use_global_device_ids=true, to_apply=%region_5.6.clone | all-reduce | flops 1024 | bytes 8192
  211.3 0.6 dynamic-slice.2
  212.0 4.8 %maximum_select_fusion.1 = bf16[1,512,2048]{2,1,0:T(8,128)(2,1)} fusion(bf16[1,256,2048]{2,1,0:T(8,128)(2,1)} %bitcast.18, bf16[1,256,2048]{2,1,0:T(8,128)(2,1)} %bitcast.17, pred[]{:T(512)S(6)} %eq.113), kind=kLoop, calls=%fused_computation.11 | loop fusion | flops 9437184 | bytes 4194305 | tf_op jit(solution)/shard_map/jit(_where)/select_n | solution.py:36
  216.8 3.4 %maximum_select_fusion = bf16[1,2048,512]{2,1,0:T(8,128)(2,1)} fusion(bf16[1,1024,512]{2,1,0:T(8,128)(2,1)} %bitcast.16, bf16[1,1024,512]{2,1,0:T(8,128)(2,1)S(1)} %bitcast.53, pred[]{:T(512)S(6)} %eq.113), kind=kLoop, calls=%fused_computation.10 | loop fusion | flops 9437184 | bytes 4194305 | tf_op jit(solution)/shard_map/jit(_where)/select_n | solution.py:36
  220.3 2.9 %fusion.2 = bf16[1,128,2048]{2,1,0:T(8,128)(2,1)} fusion(bf16[32,16,2048]{2,1,0:T(8,128)(2,1)} %all-to-all-done.2, s32[32,128]{1,0:T(8,128)S(1)} %convolution_convert_fusion.3, pred[32,128]{1,0:T(8,128)(4,1)S(1)} %fusion), kind=kOutput, calls=%fused_computation.9 | convolution fusion | flops 268828672 | bytes 2641920 | tf_op jit(solution)/shard_map/dot_general | solution.py:11
  (50 shorter events, 4.0 us)
Async XLA Ops:
  0.6 86.9 %copy-start = (bf16[1,2048,512]{2,1,0:T(8,128)(2,1)S(1)}, bf16[1,2048,512]{2,1,0:T(8,128)(2,1)}, u32[]{:S(2)}) copy-start(bf16[1,2048,512]{2,1,0:T(8,128)(2,1)} %param.8) | copy-start | bytes 6291460
  10.7 11.8 %copy-start.5 = (bf16[1,128,2048]{2,1,0:T(8,128)(2,1)S(1)}, bf16[1,128,2048]{2,1,0:T(8,128)(2,1)}, u32[]{:S(2)}) copy-start(bf16[1,128,2048]{2,1,0:T(8,128)(2,1)} %param.7) | copy-start | bytes 1572868
  10.7 61.9 %all-to-all-start.1 = ((bf16[32,16,2048]{2,1,0:T(8,128)(2,1)}), bf16[32,16,2048]{2,1,0:T(8,128)(2,1)}, u32[]{:S(2)}, u32[]{:S(2)}) async-start(bf16[32,16,2048]{2,1,0:T(8,128)(2,1)} %bitcast.52), calls=%async_computation.1 | async-start | bytes 4194304 | tf_op jit(solution)/shard_map/all_to_all | solution.py:87
  72.6 6.3 %copy-start.7 = (f32[1,1,256]{2,1,0:T(1,128)S(1)}, f32[1,1,256]{2,1,0:T(1,128)}, u32[]{:S(2)}) copy-start(f32[1,1,256]{2,1,0:T(1,128)} %param.11) | copy-start | bytes 3076
  72.6 55.3 %all-to-all-start = ((bf16[32,16,2048]{2,1,0:T(8,128)(2,1)}), bf16[32,16,2048]{2,1,0:T(8,128)(2,1)}, u32[]{:S(2)}, u32[]{:S(2)}) async-start(bf16[32,16,2048]{2,1,0:T(8,128)(2,1)} %bitcast.51), calls=%async_computation | async-start | bytes 4194304 | tf_op jit(solution)/shard_map/all_to_all | solution.py:87
  135.1 1.7 copy-start.4
  136.3 14.2 %collective-permute-start.8 = (bf16[256,2048]{1,0:T(8,128)(2,1)}, bf16[256,2048]{1,0:T(8,128)(2,1)}, u32[]{:S(2)}, u32[]{:S(2)}) collective-permute-start(bf16[256,2048]{1,0:T(8,128)(2,1)} %constant_dynamic-slice_fusion.3), channel_id=1, source_target_pairs={{0,128},{128,0},{1,129},{129,1},{2,130},{130,2},{3,131},{131,3},{4... | collective-permute-start | bytes 3145736 | tf_op jit(solution)/shard_map/ppermute | solution.py:29
  140.1 1.3 copy-start.2
  141.5 14.7 %collective-permute-start = (bf16[1024,512]{1,0:T(8,128)(2,1)S(1)}, bf16[1024,512]{1,0:T(8,128)(2,1)}, u32[]{:S(2)}, u32[]{:S(2)}) collective-permute-start(bf16[1024,512]{1,0:T(8,128)(2,1)S(1)} %constant_dynamic-slice_fusion.7), channel_id=1, source_target_pairs={{0,128},{128,0},{1,129},{129,1},{2,130},{130,2},{3,131},{131,3},{4... | collective-permute-start | bytes 3145736 | tf_op jit(solution)/shard_map/ppermute | solution.py:29
  144.4 75.9 %all-to-all-start.2 = ((bf16[32,16,2048]{2,1,0:T(8,128)(2,1)}), bf16[32,16,2048]{2,1,0:T(8,128)(2,1)}, u32[]{:S(2)}, u32[]{:S(2)}) async-start(bf16[32,16,2048]{2,1,0:T(8,128)(2,1)} %bitcast.54), calls=%async_computation.2 | async-start | bytes 4194304 | tf_op jit(solution)/shard_map/all_to_all | solution.py:121
  150.5 5.7 %copy-start.3 = (bf16[2048,512]{1,0:T(8,128)(2,1)S(1)}, bf16[2048,512]{1,0:T(8,128)(2,1)}, u32[]{:S(2)}) copy-start(bf16[2048,512]{1,0:T(8,128)(2,1)} %copy-done.2) | copy-start | bytes 6291460
  152.7 9.2 %collective-permute-start.10 = (bf16[64,2048]{1,0:T(8,128)(2,1)S(1)}, bf16[64,2048]{1,0:T(8,128)(2,1)S(1)}, u32[]{:S(2)}, u32[]{:S(2)}) collective-permute-start(bf16[64,2048]{1,0:T(8,128)(2,1)S(1)} %get-tuple-element.14), channel_id=1, source_target_pairs={{0,32},{32,64},{64,96},{96,0},{1,33},{33,65},{65,97},{97,1},{2,34}... | collective-permute-start | bytes 786440 | tf_op jit(solution)/shard_map/ppermute | solution.py:50
  153.2 20.0 %collective-permute-start.11 = (bf16[64,2048]{1,0:T(8,128)(2,1)S(1)}, bf16[64,2048]{1,0:T(8,128)(2,1)S(1)}, u32[]{:S(2)}, u32[]{:S(2)}) collective-permute-start(bf16[64,2048]{1,0:T(8,128)(2,1)S(1)} %get-tuple-element.13), channel_id=1, source_target_pairs={{0,96},{32,0},{64,32},{96,64},{1,97},{33,1},{65,33},{97,65},{2,98}... | collective-permute-start | bytes 786440 | tf_op jit(solution)/shard_map/ppermute | solution.py:50
  154.8 18.5 %collective-permute-start.9 = (bf16[64,2048]{1,0:T(8,128)(2,1)S(1)}, bf16[64,2048]{1,0:T(8,128)(2,1)S(1)}, u32[]{:S(2)}, u32[]{:S(2)}) collective-permute-start(bf16[64,2048]{1,0:T(8,128)(2,1)S(1)} %get-tuple-element.12), channel_id=1, source_target_pairs={{0,64},{32,96},{64,0},{96,32},{1,65},{33,97},{65,1},{97,33},{2,66}... | collective-permute-start | bytes 786440 | tf_op jit(solution)/shard_map/ppermute | solution.py:50
  157.7 17.6 %copy-start.1 = (bf16[1024,512]{1,0:T(8,128)(2,1)}, bf16[1024,512]{1,0:T(8,128)(2,1)S(1)}, u32[]{:S(2)}) copy-start(bf16[1024,512]{1,0:T(8,128)(2,1)S(1)} %add_convert_fusion.1) | copy-start | bytes 3145732
  157.8 17.5 %collective-permute-start.1 = (bf16[256,512]{1,0:T(8,128)(2,1)S(1)}, bf16[256,512]{1,0:T(8,128)(2,1)S(1)}, u32[]{:S(2)}, u32[]{:S(2)}) collective-permute-start(bf16[256,512]{1,0:T(8,128)(2,1)S(1)} %get-tuple-element.15), channel_id=1, source_target_pairs={{0,64},{32,96},{64,0},{96,32},{1,65},{33,97},{65,1},{97,33},{2,66}... | collective-permute-start | bytes 786440 | tf_op jit(solution)/shard_map/ppermute | solution.py:50
  160.0 18.9 %collective-permute-start.2 = (bf16[256,512]{1,0:T(8,128)(2,1)S(1)}, bf16[256,512]{1,0:T(8,128)(2,1)}, u32[]{:S(2)}, u32[]{:S(2)}) collective-permute-start(bf16[256,512]{1,0:T(8,128)(2,1)S(1)} %get-tuple-element.17), channel_id=1, source_target_pairs={{0,32},{32,64},{64,96},{96,0},{1,33},{33,65},{65,97},{97,1},{2,34}... | collective-permute-start | bytes 786440 | tf_op jit(solution)/shard_map/ppermute | solution.py:50
  161.9 22.3 %collective-permute-start.3 = (bf16[256,512]{1,0:T(8,128)(2,1)S(1)}, bf16[256,512]{1,0:T(8,128)(2,1)}, u32[]{:S(2)}, u32[]{:S(2)}) collective-permute-start(bf16[256,512]{1,0:T(8,128)(2,1)S(1)} %get-tuple-element.16), channel_id=1, source_target_pairs={{0,96},{32,0},{64,32},{96,64},{1,97},{33,1},{65,33},{97,65},{2,98}... | collective-permute-start | bytes 786440 | tf_op jit(solution)/shard_map/ppermute | solution.py:50
  175.3 12.4 %collective-permute-start.12 = (bf16[64,2048]{1,0:T(8,128)(2,1)}, bf16[64,2048]{1,0:T(8,128)(2,1)S(1)}, u32[]{:S(2)}, u32[]{:S(2)}) collective-permute-start(bf16[64,2048]{1,0:T(8,128)(2,1)} %get-tuple-element.7), channel_id=1, source_target_pairs={{0,64},{32,96},{64,0},{96,32},{1,65},{33,97},{65,1},{97,33},{2,66}... | collective-permute-start | bytes 786440 | tf_op jit(solution)/shard_map/ppermute | solution.py:58
  175.3 15.2 %collective-permute-start.13 = (bf16[64,2048]{1,0:T(8,128)(2,1)}, bf16[64,2048]{1,0:T(8,128)(2,1)S(1)}, u32[]{:S(2)}, u32[]{:S(2)}) collective-permute-start(bf16[64,2048]{1,0:T(8,128)(2,1)} %get-tuple-element.7), channel_id=1, source_target_pairs={{0,32},{32,64},{64,96},{96,0},{1,33},{33,65},{65,97},{97,1},{2,34}... | collective-permute-start | bytes 786440 | tf_op jit(solution)/shard_map/ppermute | solution.py:58
  175.3 3.6 %copy-start.6 = (bf16[256,512]{1,0:T(8,128)(2,1)}, bf16[256,512]{1,0:T(8,128)(2,1)S(1)}, u32[]{:S(2)}) copy-start(bf16[256,512]{1,0:T(8,128)(2,1)S(1)} %collective-permute-done.1) | copy-start | bytes 786436
  175.3 20.3 %collective-permute-start.14 = (bf16[64,2048]{1,0:T(8,128)(2,1)}, bf16[64,2048]{1,0:T(8,128)(2,1)S(1)}, u32[]{:S(2)}, u32[]{:S(2)}) collective-permute-start(bf16[64,2048]{1,0:T(8,128)(2,1)} %get-tuple-element.7), channel_id=1, source_target_pairs={{0,96},{32,0},{64,32},{96,64},{1,97},{33,1},{65,33},{97,65},{2,98}... | collective-permute-start | bytes 786440 | tf_op jit(solution)/shard_map/ppermute | solution.py:58
  184.2 18.0 %copy-start.8 = (u32[256]{0:T(256)S(1)}, u32[256]{0:T(256)}, u32[]{:S(2)}) copy-start(u32[256]{0:T(256)} %constant.147) | copy-start | bytes 3076
  185.6 11.6 %collective-permute-start.4 = (bf16[256,512]{1,0:T(8,128)(2,1)S(1)}, bf16[256,512]{1,0:T(8,128)(2,1)S(1)}, u32[]{:S(2)}, u32[]{:S(2)}) collective-permute-start(bf16[256,512]{1,0:T(8,128)(2,1)S(1)} %get-tuple-element.9), channel_id=1, source_target_pairs={{0,64},{32,96},{64,0},{96,32},{1,65},{33,97},{65,1},{97,33},{2,66}... | collective-permute-start | bytes 786440 | tf_op jit(solution)/shard_map/ppermute | solution.py:58
  187.7 12.9 %collective-permute-start.5 = (bf16[256,512]{1,0:T(8,128)(2,1)S(1)}, bf16[256,512]{1,0:T(8,128)(2,1)S(1)}, u32[]{:S(2)}, u32[]{:S(2)}) collective-permute-start(bf16[256,512]{1,0:T(8,128)(2,1)S(1)} %get-tuple-element.9), channel_id=1, source_target_pairs={{0,32},{32,64},{64,96},{96,0},{1,33},{33,65},{65,97},{97,1},{2,34}... | collective-permute-start | bytes 786440 | tf_op jit(solution)/shard_map/ppermute | solution.py:58
  187.7 14.2 %collective-permute-start.6 = (bf16[256,512]{1,0:T(8,128)(2,1)S(1)}, bf16[256,512]{1,0:T(8,128)(2,1)S(1)}, u32[]{:S(2)}, u32[]{:S(2)}) collective-permute-start(bf16[256,512]{1,0:T(8,128)(2,1)S(1)} %get-tuple-element.9), channel_id=1, source_target_pairs={{0,96},{32,0},{64,32},{96,64},{1,97},{33,1},{65,33},{97,65},{2,98}... | collective-permute-start | bytes 786440 | tf_op jit(solution)/shard_map/ppermute | solution.py:58
  196.4 15.6 %collective-permute-start.15 = (bf16[256,2048]{1,0:T(8,128)(2,1)}, bf16[256,2048]{1,0:T(8,128)(2,1)}, u32[]{:S(2)}, u32[]{:S(2)}) collective-permute-start(bf16[256,2048]{1,0:T(8,128)(2,1)} %constant_dynamic-update-slice_fusion), channel_id=1, source_target_pairs={{0,128},{128,0},{1,129},{129,1},{2,130},{130,2},{3,131},{131,3},{4... | collective-permute-start | bytes 3145736 | tf_op jit(solution)/shard_map/ppermute | solution.py:35
  201.9 14.9 %collective-permute-start.7 = (bf16[1024,512]{1,0:T(8,128)(2,1)S(1)}, bf16[1024,512]{1,0:T(8,128)(2,1)}, u32[]{:S(2)}, u32[]{:S(2)}) collective-permute-start(bf16[1024,512]{1,0:T(8,128)(2,1)S(1)} %constant_dynamic-update-slice_fusion.4), channel_id=1, source_target_pairs={{0,128},{128,0},{1,129},{129,1},{2,130},{130,2},{3,131},{131,3},{4... | collective-permute-start | bytes 3145736 | tf_op jit(solution)/shard_map/ppermute | solution.py:35

commit v2 on v1

v2 whole, which is shorter than its diff:
```python
import jax
import jax.numpy as jnp
from jax import lax
from jax.experimental import pallas as pl
from jax.experimental.pallas import tpu as pltpu
from jax.sharding import PartitionSpec as P

BF = jnp.bfloat16
F32 = jnp.float32
I32 = jnp.int32
NEAR = ((0, 1), (1, 0), (2, 3), (3, 2))
FAR = ((0, 3), (3, 0), (1, 2), (2, 1))
SWAP = ((0, 1), (1, 0))


def dot(left, right, dims):
    return lax.dot_general(left, right, (dims, ((), ())), preferred_element_type=F32)


def ring(count, step):
    return [(i, (i + step) % count) for i in range(count)]


def earlier(count):
    rows = lax.broadcasted_iota(I32, (count, count), 0)
    cols = lax.broadcasted_iota(I32, (count, count), 1)
    return (rows < cols).astype(BF)


def bits(ctx_index):
    high = ctx_index // 2
    return (ctx_index % 2 + high) % 2, high


def halve(part, keep, pairs):
    size = part.shape[0] // 2
    sent = lax.ppermute(lax.dynamic_slice_in_dim(part, (1 - keep) * size, size), "ctx", pairs)
    mine = lax.dynamic_slice_in_dim(part, keep * size, size)
    return (mine.astype(F32) + sent.astype(F32)).astype(BF)


def reduce_ctx(part, first, second):
    (keep_a, pairs_a), (keep_b, pairs_b) = first, second
    piece = halve(halve(part, keep_a, pairs_a), keep_b, pairs_b)
    side = lax.ppermute(piece, "ctx", pairs_b)
    across = lax.ppermute(piece, "ctx", pairs_a)
    corner = lax.ppermute(side, "ctx", pairs_a)
    own = (piece, side, across, corner)
    return own + tuple(lax.ppermute(term, "dp", SWAP) for term in own)


def assemble_kernel(where, *refs):
    out_pieces, in_pieces = refs[:8], refs[8:16]
    out_ref, in_ref, sems = refs[16], refs[17], refs[18]
    core, near, far = where[0], where[1], where[2]
    out_rows, in_rows, in_cols = out_pieces[0].shape[0], in_pieces[0].shape[0], in_pieces[0].shape[1]
    copies = []
    for k in range(8):
        half = core if k < 4 else 1 - core
        flip_b, flip_a = k % 2, (k // 2) % 2
        a = 1 - near if flip_a else near
        b = 1 - far if flip_b else far
        row = pl.multiple_of(((half * 2 + a) * 2 + b) * out_rows, out_rows)
        copies.append(
            pltpu.make_async_copy(out_pieces[k], out_ref.at[pl.ds(row, out_rows), :], sems.at[k])
        )
        a = 1 - far if flip_a else far
        b = 1 - near if flip_b else near
        row = pl.multiple_of((a * 2 + b) * in_rows, in_rows)
        col = pl.multiple_of(half * in_cols, in_cols)
        copies.append(
            pltpu.make_async_copy(
                in_pieces[k],
                in_ref.at[pl.ds(row, in_rows), pl.ds(col, in_cols)],
                sems.at[8 + k],
            )
        )
    for copy in copies:
        copy.start()
    for copy in copies:
        copy.wait()


def assemble(where, out_pieces, in_pieces, out_shape, in_shape):
    moved = 4 * (out_shape[0] * out_shape[1] + in_shape[0] * in_shape[1])
    return pl.pallas_call(
        assemble_kernel,
        in_specs=[pl.BlockSpec(memory_space=pltpu.SMEM)]
        + [pl.BlockSpec(memory_space=pl.ANY)] * 16,
        out_specs=[pl.BlockSpec(memory_space=pl.ANY)] * 2,
        out_shape=[jax.ShapeDtypeStruct(out_shape, BF), jax.ShapeDtypeStruct(in_shape, BF)],
        scratch_shapes=[pltpu.SemaphoreType.DMA((16,))],
        cost_estimate=pl.CostEstimate(flops=0, bytes_accessed=moved, transcendentals=0),
    )(where, *out_pieces, *in_pieces)


def shards(tokens, out_grad, w_in, w_out, picks, gates):
    ctx_count = lax.axis_size("ctx")
    exp_count = lax.axis_size("expert")
    core = lax.axis_index("dp")
    ctx_index = lax.axis_index("ctx")
    exp_index = lax.axis_index("expert")
    tok_dev, feat = tokens.shape[1], tokens.shape[2]
    hid = w_in.shape[2]
    pick_total = picks.shape[2]
    share = pick_total // ctx_count
    slots = ctx_count * 4
    low = slots // 2
    cuts = ((0, low), (low, slots))
    grad_scale = (lax.axis_size("dp") * pick_total) ** (-0.5)
    lists = picks[0]
    before = earlier(tok_dev)
    tok_ids = jnp.arange(tok_dev, dtype=I32)

    local = lists - (ctx_index * exp_count + exp_index) * tok_dev
    picked = jnp.any(local[:, :, None] == tok_ids[None, None, :], axis=1)
    rank = dot(picked.astype(BF), before, ((1,), (0,))).astype(I32)
    both = jnp.concatenate((tokens[0], out_grad[0]), axis=1)

    def spread_of(cut):
        start, end = cut
        slot_ids = jnp.arange(start, end, dtype=I32)
        spread = picked[:, None, :] & (rank[:, None, :] == slot_ids[None, :, None])
        return spread.astype(BF).reshape(exp_count * (end - start), tok_dev)

    def swap(rows):
        out = rows.reshape(exp_count, -1, rows.shape[1])
        out = lax.all_to_all(out, "expert", split_axis=0, concat_axis=0, tiled=True)
        return out.reshape(rows.shape)

    spreads = [spread_of(cut) for cut in cuts]
    arrived = [swap(dot(spread, both, ((1,), (0,))).astype(BF)) for spread in spreads]

    own = lax.dynamic_index_in_dim(lists, exp_index, 0, keepdims=False)
    offset = own - ctx_index * (exp_count * tok_dev)
    block = offset // tok_dev
    inside = (block >= 0) & (block < exp_count)
    token = offset % tok_dev
    in_block = (inside[:, None] & (block[:, None] == jnp.arange(exp_count)[None, :])).astype(BF)
    at_token = (token[:, None] == tok_ids[None, :]).astype(BF)
    held = dot(in_block, at_token, ((0,), (0,))).astype(BF)
    rank_own = dot(held, before, ((1,), (0,))).astype(BF)
    rank_pick = jnp.sum(
        dot(in_block, rank_own, ((1,), (0,))) * at_token.astype(F32), axis=1
    ).astype(I32)
    gate_mine = gates[0, 0]
    gate_all = jnp.zeros((ctx_count, share), F32)
    gate_all = lax.dynamic_update_slice_in_dim(gate_all, gate_mine[None], ctx_index, 0)
    for step in range(1, ctx_count):
        got = lax.ppermute(gate_mine, "ctx", ring(ctx_count, step))
        gate_all = lax.dynamic_update_slice_in_dim(
            gate_all, got[None], (ctx_index - step) % ctx_count, 0
        )
    gate_all = gate_all.reshape(pick_total)

    weight_in = w_in[0]
    weight_out = w_out[0]
    other = (1 - core) * (hid // 2)
    mine = core * (hid // 2)
    sums = {"out_other": 0.0, "out_mine": 0.0, "in_other": 0.0, "in_mine": 0.0}
    gate_pick = jnp.zeros((pick_total,), F32)
    returned = []
    for (start, end), rows in zip(cuts, arrived):
        width = end - start
        rows_in, rows_grad = rows[:, :feat], rows[:, feat:]
        fits = inside & (rank_pick >= start) & (rank_pick < end)
        place = jnp.where(fits, block * width + rank_pick - start, -1)
        at_slot = place[:, None] == jnp.arange(exp_count * width, dtype=I32)[None, :]
        slot_gate = jnp.sum(jnp.where(at_slot, gate_all[:, None], 0.0), axis=0)[:, None]
        pre_act = dot(rows_in, weight_in, ((1,), (0,)))
        sig = jax.nn.sigmoid(pre_act)
        activation = (pre_act * sig).astype(BF)
        slope = sig * (1.0 + pre_act * (1.0 - sig))
        back = dot(rows_grad, weight_out, ((1,), (1,)))
        pre_grad = (slot_gate * back * slope).astype(BF)
        gated = (slot_gate * activation.astype(F32)).astype(BF)
        row_grads = dot(pre_grad, weight_in, ((1,), (1,))).astype(BF)
        returned.append(swap(row_grads))
        gate_slot = jnp.sum(activation.astype(F32) * back, axis=1)
        gate_pick += jnp.sum(jnp.where(at_slot, gate_slot[None, :], 0.0), axis=1)
        for name, at in (("other", other), ("mine", mine)):
            cols = lax.dynamic_slice_in_dim(gated, at, hid // 2, 1)
            sums["out_" + name] += dot(cols, rows_grad, ((0,), (0,)))
            cols = lax.dynamic_slice_in_dim(pre_grad, at, hid // 2, 1)
            sums["in_" + name] += dot(rows_in, cols, ((0,), (0,)))

    near, far = bits(ctx_index)
    pieces = []
    for name, order in (
        ("out_", ((near, NEAR), (far, FAR))),
        ("in_", ((far, FAR), (near, NEAR))),
    ):
        sent = lax.ppermute((sums[name + "other"] * grad_scale).astype(BF), "dp", SWAP)
        half = (sums[name + "mine"] * grad_scale + sent.astype(F32)).astype(BF)
        pieces.append(reduce_ctx(half, *order))
    out_total, in_total = assemble(
        jnp.stack((core, near, far)).astype(I32), *pieces, (hid, feat), (feat, hid)
    )

    gate_rows = gate_pick.reshape(ctx_count, share)
    gate_grad = lax.dynamic_index_in_dim(gate_rows, ctx_index, 0, keepdims=False)
    for step in range(1, ctx_count):
        term = lax.dynamic_index_in_dim(
            gate_rows, (ctx_index + step) % ctx_count, 0, keepdims=False
        )
        gate_grad = gate_grad + lax.ppermute(term, "ctx", ring(ctx_count, step))

    token_total = sum(dot(spread, rows, ((0,), (0,))) for spread, rows in zip(spreads, returned))
    return (
        token_total.astype(BF)[None],
        in_total[None],
        out_total[None],
        gate_grad.reshape(1, 1, share),
    )


def solution(mesh):
    placed = (
        P("dp", ("ctx", "expert"), None),
        P("dp", ("ctx", "expert"), None),
        P("expert", None, None),
        P("expert", None, None),
        P("dp", None, None),
        P("dp", "expert", "ctx"),
    )
    return jax.shard_map(
        shards,
        mesh=mesh,
        in_specs=placed,
        out_specs=(
            P("dp", ("ctx", "expert"), None),
            P("expert", None, None),
            P("expert", None, None),
            P("dp", "expert", "ctx"),
        ),
        check_vma=False,
    )
```

time: 226 us -> 370 us (1.64)
  Pallas kernels: 0 us -> 129 us
  starting transfers between devices: 39 us -> 55.6 us
  blocking collectives: 14.6 us -> 0 us
  matrix products: 24.1 us -> 37 us
  waiting for transfers between devices: 113 us -> 125 us
  other arithmetic: 22.8 us -> 14.7 us
  local copies, waits for them, and re-layouts: 7.82 us -> 2.46 us
    pallas_call x0 -> x1, Pallas kernels: none -> 129 us  [assemble(): pl.pallas_call(assemble_kernel, in_specs=[pl.BlockSpec(memory_space=pltpu...]
    dot_general x11 -> x21, matrix products: 24.1 us -> 37 us  [dot(): lax.dot_general(left, right, (dims, ((), ())), preferred_element_type=F32)]
    all_to_all x3 -> x4, starting transfers between devices: 24 us -> 33.7 us  [swap(): out = lax.all_to_all(out, 'expert', split_axis=0, concat_axis=0, tiled=True)]
    ppermute x16 -> x26, waiting for transfers between devices: 27.5 us -> 35.9 us  [the longest x3 13.6 us: shards(): gate_grad = gate_grad + lax.ppermute(term, 'ctx', ring(ctx_count, step))]
    select_n x3 -> x1, other arithmetic: 8.28 us -> 0.01 us  [shards(): place = jnp.where(fits, block * width + rank_pick - start, -1)]
    unnamed x1 -> x0, blocking collectives: 7.83 us -> none
    ppermute x16 -> x26, starting transfers between devices: 15 us -> 21.9 us  [the longest x3 5.42 us: shards(): gate_grad = gate_grad + lax.ppermute(term, 'ctx', ring(ctx_count, step))]
    all_gather x1 -> x0, blocking collectives: 6.72 us -> none  [shards(): gate_all = lax.all_gather(gates[0, 0], 'ctx', tiled=True)]
  transfers between devices with their start and end apart: 19 -> 30, of which waited for: 10 -> 10; matrix products, arithmetic and copies ran while one was open for 14% -> 9% of each run, Pallas kernels for 0% -> 0%
where the time goes in v2:
time: 370 us; the launch traced here: 365 us
  Pallas kernels  129 us (35%)
  waiting for transfers between devices  125 us (34%)
  starting transfers between devices  55.6 us (15%)
  matrix products  37 us (10%)
  other arithmetic  14.7 us (4%)
    pallas_call x1, Pallas kernels, assemble(): pl.pallas_call(assemble_kernel, in_specs=[pl.BlockSpec(memory_space=pltpu...  129 us
    all_to_all x4, waiting for transfers between devices, swap(): out = lax.all_to_all(out, 'expert', split_axis=0, concat_axis=0, tiled=True)  88.8 us
    dot_general x21, matrix products, dot(): lax.dot_general(left, right, (dims, ((), ())), preferred_element_type=F32)  37 us
    all_to_all x4, starting transfers between devices, swap(): out = lax.all_to_all(out, 'expert', split_axis=0, concat_axis=0, tiled=True)  33.7 us
    ppermute x3, waiting for transfers between devices, shards(): gate_grad = gate_grad + lax.ppermute(term, 'ctx', ring(ctx_count, step))  13.6 us
    ppermute x4, waiting for transfers between devices, halve(): lax.ppermute(lax.dynamic_slice_in_dim(part, (1 - keep) * size, size), 'ct...  13 us
  transfers between devices with their start and end apart: 30, of which 10 were waited for; matrix products, arithmetic and copies ran while one was open for 9% of the time, Pallas kernels for 0%

profile of v2, /device:TPU:6, one launch (start us, length us, event | category | flops | bytes accessed | tf_op | source)
XLA Modules:
  0.0 364.8 jit_solution(9461359459151007982)
XLA Ops:
  0.8 1.0 subtract_bitcast_fusion
  1.8 5.7 %fusion = pred[32,128]{1,0:T(8,128)(4,1)S(1)} fusion(s32[32,1024]{1,0:T(8,128)S(1)} %subtract_bitcast_fusion), kind=kLoop, calls=%fused_computation.1 | loop fusion | flops 8384512 | bytes 135168 | tf_op jit(solution)/shard_map/reduce_or | solution.py:116
  7.6 3.3 fusion.1
  10.9 11.7 %all-to-all-start = ((bf16[32,8,4096]{2,1,0:T(8,128)(2,1)}), bf16[32,8,4096]{2,1,0:T(8,128)(2,1)}, u32[]{:S(2)}, u32[]{:S(2)}) async-start(bf16[32,8,4096]{2,1,0:T(8,128)(2,1)} %fusion.1), calls=%async_computation | async-start | bytes 4194304 | tf_op jit(solution)/shard_map/all_to_all | solution.py:128
  22.8 2.1 fusion.2
  24.9 47.9 %all-to-all-done = bf16[32,8,4096]{2,1,0:T(8,128)(2,1)} async-done(((bf16[32,8,4096]{2,1,0:T(8,128)(2,1)}), bf16[32,8,4096]{2,1,0:T(8,128)(2,1)}, u32[]{:S(2)}, u32[]{:S(2)}) %all-to-all-start) | async-done | bytes 2097184 | tf_op jit(solution)/shard_map/all_to_all | solution.py:128
  72.8 6.1 %all-to-all-start.2 = ((bf16[32,8,4096]{2,1,0:T(8,128)(2,1)}), bf16[32,8,4096]{2,1,0:T(8,128)(2,1)}, u32[]{:S(2)}, u32[]{:S(2)}) async-start(bf16[32,8,4096]{2,1,0:T(8,128)(2,1)} %fusion.2), calls=%async_computation.2 | async-start | bytes 4194304 | tf_op jit(solution)/shard_map/all_to_all | solution.py:128
  79.8 1.1 collective-permute-start.1
  80.9 2.1 collective-permute-start
  85.2 1.9 fusion.18
  87.2 40.9 %all-to-all-done.2 = bf16[32,8,4096]{2,1,0:T(8,128)(2,1)} async-done(((bf16[32,8,4096]{2,1,0:T(8,128)(2,1)}), bf16[32,8,4096]{2,1,0:T(8,128)(2,1)}, u32[]{:S(2)}, u32[]{:S(2)}) %all-to-all-start.2) | async-done | bytes 2097184 | tf_op jit(solution)/shard_map/all_to_all | solution.py:128
  128.0 2.1 fusion.15
  130.1 2.9 fusion.42
  133.0 2.1 fusion.44
  135.0 1.1 select_reduce_fusion
  137.0 1.7 fusion.10
  138.8 6.0 %all-to-all-start.3 = ((bf16[32,8,2048]{2,1,0:T(8,128)(2,1)}), bf16[32,8,2048]{2,1,0:T(8,128)(2,1)S(1)}, u32[]{:S(2)}, u32[]{:S(2)}) async-start(bf16[32,8,2048]{2,1,0:T(8,128)(2,1)} %fusion.10), calls=%async_computation.3 | async-start | bytes 2097152 | tf_op jit(solution)/shard_map/all_to_all | solution.py:128
  144.7 1.5 fusion.41
  146.3 1.7 fusion.36
  148.0 1.7 fusion.7
  150.0 1.7 fusion.31
  151.7 1.8 fusion.8
  154.1 1.7 fusion.38
  155.8 1.7 fusion.33
  157.5 1.8 add_convert_fusion.1
  160.3 1.7 fusion.9
  162.0 1.9 add_convert_fusion
  164.8 1.2 collective-permute-start.14
  165.9 7.4 %collective-permute-done.4 = bf16[128,2048]{1,0:T(8,128)(2,1)S(1)} collective-permute-done((bf16[128,2048]{1,0:T(8,128)(2,1)S(1)}, bf16[128,2048]{1,0:T(8,128)(2,1)S(1)}, u32[]{:S(2)}, u32[]{:S(2)}) %collective-permute-start.4) | collective-permute-done | bytes 524320 | tf_op jit(solution)/shard_map/ppermute | solution.py:37
  174.2 9.9 %all-to-all-start.1 = ((bf16[32,8,2048]{2,1,0:T(8,128)(2,1)}), bf16[32,8,2048]{2,1,0:T(8,128)(2,1)}, u32[]{:S(2)}, u32[]{:S(2)}) async-start(bf16[32,8,2048]{2,1,0:T(8,128)(2,1)} %fusion.9), calls=%async_computation.1 | async-start | bytes 2097152 | tf_op jit(solution)/shard_map/all_to_all | solution.py:128
  184.2 1.0 constant_dynamic-slice_fusion.6
  185.8 1.3 add_convert_fusion.2
  187.1 1.0 collective-permute-start.15
  188.1 5.6 %collective-permute-done.5 = bf16[64,2048]{1,0:T(8,128)(2,1)S(1)} collective-permute-done((bf16[64,2048]{1,0:T(8,128)(2,1)S(1)}, bf16[64,2048]{1,0:T(8,128)(2,1)S(1)}, u32[]{:S(2)}, u32[]{:S(2)}) %collective-permute-start.5) | collective-permute-done | bytes 262176 | tf_op jit(solution)/shard_map/ppermute | solution.py:37
  194.8 1.4 collective-permute-start.16
  197.0 9.0 %collective-permute-done.25 = f32[256]{0:T(256)S(1)} collective-permute-done((f32[256]{0:T(256)S(1)}, f32[256]{0:T(256)S(1)}, u32[]{:S(2)}, u32[]{:S(2)}) %collective-permute-start.25) | collective-permute-done | bytes 1056 | tf_op jit(solution)/shard_map/ppermute | solution.py:206
  206.1 2.8 collective-permute-start.23
  208.8 1.3 collective-permute-done.23
  210.2 1.8 collective-permute-start.24
  212.0 3.3 collective-permute-done.24
  215.3 3.8 %collective-permute-start.17 = (bf16[512,256]{1,0:T(8,128)(2,1)S(1)}, bf16[512,256]{1,0:T(8,128)(2,1)}, u32[]{:S(2)}, u32[]{:S(2)}) collective-permute-start(bf16[512,256]{1,0:T(8,128)(2,1)S(1)} %add_convert_fusion.4.refs_8_), channel_id=1, source_target_pairs={{0,96},{96,0},{32,64},{64,32},{1,97},{97,1},{33,65},{65,33},{2,98}... | collective-permute-start | bytes 786440 | tf_op jit(solution)/shard_map/ppermute | solution.py:46
  219.1 1.2 collective-permute-start.18
  221.6 4.6 %collective-permute-done.17.refs_10_ = bf16[512,256]{1,0:T(8,128)(2,1)} collective-permute-done((bf16[512,256]{1,0:T(8,128)(2,1)S(1)}, bf16[512,256]{1,0:T(8,128)(2,1)}, u32[]{:S(2)}, u32[]{:S(2)}) %collective-permute-start.17) | collective-permute-done | bytes 262176 | tf_op jit(solution)/shard_map/ppermute | solution.py:46
  226.7 1.4 collective-permute-done.8.refs_3_
  228.1 3.3 collective-permute-done.18.refs_11_
  231.5 1.6 convolution_bitcast_fusion
  233.2 2.4 fusion.13
  235.6 129.0 %shard_map.93 = (bf16[512,2048]{1,0:T(8,128)(2,1)}, bf16[2048,512]{1,0:T(8,128)(2,1)}) custom-call(s32[3]{0:T(128)} %pad_add_fusion.where, bf16[64,2048]{1,0:T(8,128)(2,1)} %copy-done.7, bf16[64,2048]{1,0:T(8,128)(2,1)} %collective-permute-done.6.refs_1_, bf16[64,2048]{1,0:T(8,128)(2,1)} %copy-done.11, bf16[64,2048]{1,0:T(8,128)(2,1)} %collective-permute-done.8.refs_3_, ...), custom_call_target="tpu_custom_call" | custom-call | bytes 8388608 | tf_op jit(solution)/shard_map/pallas_call | solution.py:86
  (99 shorter events, 12.4 us)
Async XLA Ops:
  0.6 84.6 %copy-start = (bf16[1,2048,512]{2,1,0:T(8,128)(2,1)S(1)}, bf16[1,2048,512]{2,1,0:T(8,128)(2,1)}, u32[]{:S(2)}) copy-start(bf16[1,2048,512]{2,1,0:T(8,128)(2,1)} %param.8) | copy-start | bytes 6291460
  10.9 11.9 %copy-start.4 = (bf16[1,128,2048]{2,1,0:T(8,128)(2,1)S(1)}, bf16[1,128,2048]{2,1,0:T(8,128)(2,1)}, u32[]{:S(2)}) copy-start(bf16[1,128,2048]{2,1,0:T(8,128)(2,1)} %param.7) | copy-start | bytes 1572868
  10.9 11.9 %copy-start.5 = (bf16[1,128,2048]{2,1,0:T(8,128)(2,1)S(1)}, bf16[1,128,2048]{2,1,0:T(8,128)(2,1)}, u32[]{:S(2)}) copy-start(bf16[1,128,2048]{2,1,0:T(8,128)(2,1)} %param.6) | copy-start | bytes 1572868
  10.9 61.9 %all-to-all-start = ((bf16[32,8,4096]{2,1,0:T(8,128)(2,1)}), bf16[32,8,4096]{2,1,0:T(8,128)(2,1)}, u32[]{:S(2)}, u32[]{:S(2)}) async-start(bf16[32,8,4096]{2,1,0:T(8,128)(2,1)} %fusion.1), calls=%async_computation | async-start | bytes 4194304 | tf_op jit(solution)/shard_map/all_to_all | solution.py:128
  24.9 54.0 %copy-start.14 = (f32[1,1,256]{2,1,0:T(1,128)S(1)}, f32[1,1,256]{2,1,0:T(1,128)}, u32[]{:S(2)}) copy-start(f32[1,1,256]{2,1,0:T(1,128)} %param.11) | copy-start | bytes 3076
  72.8 55.2 %all-to-all-start.2 = ((bf16[32,8,4096]{2,1,0:T(8,128)(2,1)}), bf16[32,8,4096]{2,1,0:T(8,128)(2,1)}, u32[]{:S(2)}, u32[]{:S(2)}) async-start(bf16[32,8,4096]{2,1,0:T(8,128)(2,1)} %fusion.2), calls=%async_computation.2 | async-start | bytes 4194304 | tf_op jit(solution)/shard_map/all_to_all | solution.py:128
  78.9 6.3 %collective-permute-start.2 = (f32[256]{0:T(256)S(1)}, f32[256]{0:T(256)S(1)}, u32[]{:S(2)}, u32[]{:S(2)}) collective-permute-start(f32[256]{0:T(256)S(1)} %bitcast.91), channel_id=1, source_target_pairs={{0,96},{32,0},{64,32},{96,64},{1,97},{33,1},{65,33},{97,65},{2,98}... | collective-permute-start | bytes 3080 | tf_op jit(solution)/shard_map/ppermute | solution.py:150
  79.8 5.3 %collective-permute-start.1 = (f32[256]{0:T(256)S(1)}, f32[256]{0:T(256)S(1)}, u32[]{:S(2)}, u32[]{:S(2)}) collective-permute-start(f32[256]{0:T(256)S(1)} %bitcast.92), channel_id=1, source_target_pairs={{0,64},{32,96},{64,0},{96,32},{1,65},{33,97},{65,1},{97,33},{2,66}... | collective-permute-start | bytes 3080 | tf_op jit(solution)/shard_map/ppermute | solution.py:150
  80.9 4.1 %collective-permute-start = (f32[256]{0:T(256)S(1)}, f32[256]{0:T(256)S(1)}, u32[]{:S(2)}, u32[]{:S(2)}) collective-permute-start(f32[256]{0:T(256)S(1)} %bitcast.93), channel_id=1, source_target_pairs={{0,32},{32,64},{64,96},{96,0},{1,33},{33,65},{65,97},{97,1},{2,34}... | collective-permute-start | bytes 3080 | tf_op jit(solution)/shard_map/ppermute | solution.py:150
  87.1 45.8 %copy-start.9 = (f32[256,512]{1,0:T(8,128)}, f32[256,512]{1,0:T(8,128)S(1)}, u32[]{:S(2)}) copy-start(f32[256,512]{1,0:T(8,128)S(1)} %fusion.18) | copy-start | bytes 1572868
  128.0 2.1 copy-start.15
  138.8 35.5 %all-to-all-start.3 = ((bf16[32,8,2048]{2,1,0:T(8,128)(2,1)}), bf16[32,8,2048]{2,1,0:T(8,128)(2,1)S(1)}, u32[]{:S(2)}, u32[]{:S(2)}) async-start(bf16[32,8,2048]{2,1,0:T(8,128)(2,1)} %fusion.10), calls=%async_computation.3 | async-start | bytes 2097152 | tf_op jit(solution)/shard_map/all_to_all | solution.py:128
  146.2 1.7 copy-start.6
  149.7 7.8 %collective-permute-start.3 = (bf16[256,2048]{1,0:T(8,128)(2,1)S(1)}, bf16[256,2048]{1,0:T(8,128)(2,1)S(1)}, u32[]{:S(2)}, u32[]{:S(2)}) collective-permute-start(bf16[256,2048]{1,0:T(8,128)(2,1)S(1)} %fusion.7), channel_id=1, source_target_pairs={{0,128},{128,0},{1,129},{129,1},{2,130},{130,2},{3,131},{131,3},{4... | collective-permute-start | bytes 3145736 | tf_op jit(solution)/shard_map/ppermute | solution.py:193
  153.5 8.5 %collective-permute-start.13 = (bf16[2048,256]{1,0:T(8,128)(2,1)S(1)}, bf16[2048,256]{1,0:T(8,128)(2,1)S(1)}, u32[]{:S(2)}, u32[]{:S(2)}) collective-permute-start(bf16[2048,256]{1,0:T(8,128)(2,1)S(1)} %fusion.8), channel_id=1, source_target_pairs={{0,128},{128,0},{1,129},{129,1},{2,130},{130,2},{3,131},{131,3},{4... | collective-permute-start | bytes 3145736 | tf_op jit(solution)/shard_map/ppermute | solution.py:193
  159.4 13.9 %collective-permute-start.4 = (bf16[128,2048]{1,0:T(8,128)(2,1)S(1)}, bf16[128,2048]{1,0:T(8,128)(2,1)S(1)}, u32[]{:S(2)}, u32[]{:S(2)}) collective-permute-start(bf16[128,2048]{1,0:T(8,128)(2,1)S(1)} %constant_dynamic-slice_fusion.7), channel_id=1, source_target_pairs={{0,32},{32,0},{64,96},{96,64},{1,33},{33,1},{65,97},{97,65},{2,34}... | collective-permute-start | bytes 1572872 | tf_op jit(solution)/shard_map/ppermute | solution.py:37
  163.9 9.4 %copy-start.2 = (bf16[2048,256]{1,0:T(8,128)(2,1)}, bf16[2048,256]{1,0:T(8,128)(2,1)S(1)}, u32[]{:S(2)}) copy-start(bf16[2048,256]{1,0:T(8,128)(2,1)S(1)} %add_convert_fusion) | copy-start | bytes 3145732
  164.8 21.0 %collective-permute-start.14 = (bf16[1024,256]{1,0:T(8,128)(2,1)}, bf16[1024,256]{1,0:T(8,128)(2,1)}, u32[]{:S(2)}, u32[]{:S(2)}) collective-permute-start(bf16[1024,256]{1,0:T(8,128)(2,1)} %constant_dynamic-slice_fusion.5), channel_id=1, source_target_pairs={{0,96},{96,0},{32,64},{64,32},{1,97},{97,1},{33,65},{65,33},{2,98}... | collective-permute-start | bytes 1572872 | tf_op jit(solution)/shard_map/ppermute | solution.py:37
  174.2 12.9 %copy-start.1 = (bf16[32,8,2048]{2,1,0:T(8,128)(2,1)}, bf16[32,8,2048]{2,1,0:T(8,128)(2,1)S(1)}, u32[]{:S(2)}) copy-start(bf16[32,8,2048]{2,1,0:T(8,128)(2,1)S(1)} %all-to-all-done.3) | copy-start | bytes 3145732
  174.2 58.9 %all-to-all-start.1 = ((bf16[32,8,2048]{2,1,0:T(8,128)(2,1)}), bf16[32,8,2048]{2,1,0:T(8,128)(2,1)}, u32[]{:S(2)}, u32[]{:S(2)}) async-start(bf16[32,8,2048]{2,1,0:T(8,128)(2,1)} %fusion.9), calls=%async_computation.1 | async-start | bytes 2097152 | tf_op jit(solution)/shard_map/all_to_all | solution.py:128
  184.2 9.6 %copy-start.3 = (bf16[128,2048]{1,0:T(8,128)(2,1)S(1)}, bf16[128,2048]{1,0:T(8,128)(2,1)}, u32[]{:S(2)}) copy-start(bf16[128,2048]{1,0:T(8,128)(2,1)} %add_convert_fusion.3) | copy-start | bytes 1572868
  185.2 8.5 %collective-permute-start.5 = (bf16[64,2048]{1,0:T(8,128)(2,1)S(1)}, bf16[64,2048]{1,0:T(8,128)(2,1)S(1)}, u32[]{:S(2)}, u32[]{:S(2)}) collective-permute-start(bf16[64,2048]{1,0:T(8,128)(2,1)S(1)} %constant_dynamic-slice_fusion.6), channel_id=1, source_target_pairs={{0,96},{96,0},{32,64},{64,32},{1,97},{97,1},{33,65},{65,33},{2,98}... | collective-permute-start | bytes 786440 | tf_op jit(solution)/shard_map/ppermute | solution.py:37
  187.1 7.6 %collective-permute-start.15 = (bf16[512,256]{1,0:T(8,128)(2,1)S(1)}, bf16[512,256]{1,0:T(8,128)(2,1)S(1)}, u32[]{:S(2)}, u32[]{:S(2)}) collective-permute-start(bf16[512,256]{1,0:T(8,128)(2,1)S(1)} %constant_dynamic-slice_fusion.4), channel_id=1, source_target_pairs={{0,32},{32,0},{64,96},{96,64},{1,33},{33,1},{65,97},{97,65},{2,34}... | collective-permute-start | bytes 786440 | tf_op jit(solution)/shard_map/ppermute | solution.py:37
  193.8 41.8 %copy-start.7 = (bf16[64,2048]{1,0:T(8,128)(2,1)}, bf16[64,2048]{1,0:T(8,128)(2,1)S(1)}, u32[]{:S(2)}) copy-start(bf16[64,2048]{1,0:T(8,128)(2,1)S(1)} %add_convert_fusion.5.refs_0_) | copy-start | bytes 786436
  193.8 21.5 %collective-permute-start.9 = (bf16[64,2048]{1,0:T(8,128)(2,1)S(1)}, bf16[64,2048]{1,0:T(8,128)(2,1)S(1)}, u32[]{:S(2)}, u32[]{:S(2)}) collective-permute-start(bf16[64,2048]{1,0:T(8,128)(2,1)S(1)} %add_convert_fusion.5.refs_0_), channel_id=1, source_target_pairs={{0,128},{128,0},{1,129},{129,1},{2,130},{130,2},{3,131},{131,3},{4... | collective-permute-start | bytes 786440 | tf_op jit(solution)/shard_map/ppermute | solution.py:49
  193.9 25.1 %collective-permute-start.7 = (bf16[64,2048]{1,0:T(8,128)(2,1)S(1)}, bf16[64,2048]{1,0:T(8,128)(2,1)S(1)}, u32[]{:S(2)}, u32[]{:S(2)}) collective-permute-start(bf16[64,2048]{1,0:T(8,128)(2,1)S(1)} %add_convert_fusion.5.refs_0_), channel_id=1, source_target_pairs={{0,32},{32,0},{64,96},{96,64},{1,33},{33,1},{65,97},{97,65},{2,34}... | collective-permute-start | bytes 786440 | tf_op jit(solution)/shard_map/ppermute | solution.py:46
  194.0 25.0 %collective-permute-start.6 = (bf16[64,2048]{1,0:T(8,128)(2,1)S(1)}, bf16[64,2048]{1,0:T(8,128)(2,1)}, u32[]{:S(2)}, u32[]{:S(2)}) collective-permute-start(bf16[64,2048]{1,0:T(8,128)(2,1)S(1)} %add_convert_fusion.5.refs_0_), channel_id=1, source_target_pairs={{0,96},{96,0},{32,64},{64,32},{1,97},{97,1},{33,65},{65,33},{2,98}... | collective-permute-start | bytes 786440 | tf_op jit(solution)/shard_map/ppermute | solution.py:45
  194.8 36.6 %copy-start.8 = (bf16[512,256]{1,0:T(8,128)(2,1)}, bf16[512,256]{1,0:T(8,128)(2,1)S(1)}, u32[]{:S(2)}) copy-start(bf16[512,256]{1,0:T(8,128)(2,1)S(1)} %add_convert_fusion.4.refs_8_) | copy-start | bytes 786436
  194.8 24.3 %collective-permute-start.16 = (bf16[512,256]{1,0:T(8,128)(2,1)S(1)}, bf16[512,256]{1,0:T(8,128)(2,1)}, u32[]{:S(2)}, u32[]{:S(2)}) collective-permute-start(bf16[512,256]{1,0:T(8,128)(2,1)S(1)} %add_convert_fusion.4.refs_8_), channel_id=1, source_target_pairs={{0,32},{32,0},{64,96},{96,64},{1,33},{33,1},{65,97},{97,65},{2,34}... | collective-permute-start | bytes 786440 | tf_op jit(solution)/shard_map/ppermute | solution.py:45
  196.2 9.8 %collective-permute-start.25 = (f32[256]{0:T(256)S(1)}, f32[256]{0:T(256)S(1)}, u32[]{:S(2)}, u32[]{:S(2)}) collective-permute-start(f32[256]{0:T(256)S(1)} %bitcast.101), channel_id=1, source_target_pairs={{0,96},{32,0},{64,32},{96,64},{1,97},{33,1},{65,33},{97,65},{2,98}... | collective-permute-start | bytes 3080 | tf_op jit(solution)/shard_map/ppermute | solution.py:206
  206.1 4.1 %collective-permute-start.23 = (f32[256]{0:T(256)S(1)}, f32[256]{0:T(256)S(1)}, u32[]{:S(2)}, u32[]{:S(2)}) collective-permute-start(f32[256]{0:T(256)S(1)} %bitcast.100), channel_id=1, source_target_pairs={{0,32},{32,64},{64,96},{96,0},{1,33},{33,65},{65,97},{97,1},{2,34}... | collective-permute-start | bytes 3080 | tf_op jit(solution)/shard_map/ppermute | solution.py:206
  210.2 5.1 %collective-permute-start.24 = (f32[256]{0:T(256)S(1)}, f32[256]{0:T(256)S(1)}, u32[]{:S(2)}, u32[]{:S(2)}) collective-permute-start(f32[256]{0:T(256)S(1)} %bitcast.99), channel_id=1, source_target_pairs={{0,64},{32,96},{64,0},{96,32},{1,65},{33,97},{65,1},{97,33},{2,66}... | collective-permute-start | bytes 3080 | tf_op jit(solution)/shard_map/ppermute | solution.py:206
  215.2 6.3 %collective-permute-start.19 = (bf16[512,256]{1,0:T(8,128)(2,1)S(1)}, bf16[512,256]{1,0:T(8,128)(2,1)S(1)}, u32[]{:S(2)}, u32[]{:S(2)}) collective-permute-start(bf16[512,256]{1,0:T(8,128)(2,1)S(1)} %add_convert_fusion.4.refs_8_), channel_id=1, source_target_pairs={{0,128},{128,0},{1,129},{129,1},{2,130},{130,2},{3,131},{131,3},{4... | collective-permute-start | bytes 786440 | tf_op jit(solution)/shard_map/ppermute | solution.py:49
  215.2 16.2 %copy-start.10 = (bf16[64,2048]{1,0:T(8,128)(2,1)}, bf16[64,2048]{1,0:T(8,128)(2,1)S(1)}, u32[]{:S(2)}) copy-start(bf16[64,2048]{1,0:T(8,128)(2,1)S(1)} %collective-permute-done.9.refs_4_) | copy-start | bytes 786436
  215.3 10.9 %collective-permute-start.17 = (bf16[512,256]{1,0:T(8,128)(2,1)S(1)}, bf16[512,256]{1,0:T(8,128)(2,1)}, u32[]{:S(2)}, u32[]{:S(2)}) collective-permute-start(bf16[512,256]{1,0:T(8,128)(2,1)S(1)} %add_convert_fusion.4.refs_8_), channel_id=1, source_target_pairs={{0,96},{96,0},{32,64},{64,32},{1,97},{97,1},{33,65},{65,33},{2,98}... | collective-permute-start | bytes 786440 | tf_op jit(solution)/shard_map/ppermute | solution.py:46
  219.0 12.4 %copy-start.11 = (bf16[64,2048]{1,0:T(8,128)(2,1)}, bf16[64,2048]{1,0:T(8,128)(2,1)S(1)}, u32[]{:S(2)}) copy-start(bf16[64,2048]{1,0:T(8,128)(2,1)S(1)} %collective-permute-done.7.refs_2_) | copy-start | bytes 786436
  219.0 7.2 %collective-permute-start.11 = (bf16[64,2048]{1,0:T(8,128)(2,1)S(1)}, bf16[64,2048]{1,0:T(8,128)(2,1)S(1)}, u32[]{:S(2)}, u32[]{:S(2)}) collective-permute-start(bf16[64,2048]{1,0:T(8,128)(2,1)S(1)} %collective-permute-done.7.refs_2_), channel_id=1, source_target_pairs={{0,128},{128,0},{1,129},{129,1},{2,130},{130,2},{3,131},{131,3},{4... | collective-permute-start | bytes 786440 | tf_op jit(solution)/shard_map/ppermute | solution.py:49
  219.0 9.0 %collective-permute-start.8 = (bf16[64,2048]{1,0:T(8,128)(2,1)}, bf16[64,2048]{1,0:T(8,128)(2,1)}, u32[]{:S(2)}, u32[]{:S(2)}) collective-permute-start(bf16[64,2048]{1,0:T(8,128)(2,1)} %collective-permute-done.6.refs_1_), channel_id=1, source_target_pairs={{0,32},{32,0},{64,96},{96,64},{1,33},{33,1},{65,97},{97,65},{2,34}... | collective-permute-start | bytes 786440 | tf_op jit(solution)/shard_map/ppermute | solution.py:47
  219.1 12.3 %collective-permute-start.18 = (bf16[512,256]{1,0:T(8,128)(2,1)}, bf16[512,256]{1,0:T(8,128)(2,1)}, u32[]{:S(2)}, u32[]{:S(2)}) collective-permute-start(bf16[512,256]{1,0:T(8,128)(2,1)} %collective-permute-done.16.refs_9_), channel_id=1, source_target_pairs={{0,96},{96,0},{32,64},{64,32},{1,97},{97,1},{33,65},{65,33},{2,98}... | collective-permute-start | bytes 786440 | tf_op jit(solution)/shard_map/ppermute | solution.py:47
  221.5 9.9 %copy-start.12 = (bf16[512,256]{1,0:T(8,128)(2,1)}, bf16[512,256]{1,0:T(8,128)(2,1)S(1)}, u32[]{:S(2)}) copy-start(bf16[512,256]{1,0:T(8,128)(2,1)S(1)} %collective-permute-done.19.refs_12_) | copy-start | bytes 786436
  221.6 14.0 %collective-permute-start.10 = (bf16[64,2048]{1,0:T(8,128)(2,1)}, bf16[64,2048]{1,0:T(8,128)(2,1)}, u32[]{:S(2)}, u32[]{:S(2)}) collective-permute-start(bf16[64,2048]{1,0:T(8,128)(2,1)} %collective-permute-done.6.refs_1_), channel_id=1, source_target_pairs={{0,128},{128,0},{1,129},{129,1},{2,130},{130,2},{3,131},{131,3},{4... | collective-permute-start | bytes 786440 | tf_op jit(solution)/shard_map/ppermute | solution.py:49
  226.2 9.4 %collective-permute-start.20 = (bf16[512,256]{1,0:T(8,128)(2,1)}, bf16[512,256]{1,0:T(8,128)(2,1)}, u32[]{:S(2)}, u32[]{:S(2)}) collective-permute-start(bf16[512,256]{1,0:T(8,128)(2,1)} %collective-permute-done.16.refs_9_), channel_id=1, source_target_pairs={{0,128},{128,0},{1,129},{129,1},{2,130},{130,2},{3,131},{131,3},{4... | collective-permute-start | bytes 786440 | tf_op jit(solution)/shard_map/ppermute | solution.py:49
  226.2 5.2 %copy-start.13 = (bf16[64,2048]{1,0:T(8,128)(2,1)}, bf16[64,2048]{1,0:T(8,128)(2,1)S(1)}, u32[]{:S(2)}) copy-start(bf16[64,2048]{1,0:T(8,128)(2,1)S(1)} %collective-permute-done.11.refs_6_) | copy-start | bytes 786436
  226.2 9.4 %collective-permute-start.21 = (bf16[512,256]{1,0:T(8,128)(2,1)}, bf16[512,256]{1,0:T(8,128)(2,1)}, u32[]{:S(2)}, u32[]{:S(2)}) collective-permute-start(bf16[512,256]{1,0:T(8,128)(2,1)} %collective-permute-done.17.refs_10_), channel_id=1, source_target_pairs={{0,128},{128,0},{1,129},{129,1},{2,130},{130,2},{3,131},{131,3},{4... | collective-permute-start | bytes 786440 | tf_op jit(solution)/shard_map/ppermute | solution.py:49
  228.1 7.5 %collective-permute-start.12 = (bf16[64,2048]{1,0:T(8,128)(2,1)}, bf16[64,2048]{1,0:T(8,128)(2,1)}, u32[]{:S(2)}, u32[]{:S(2)}) collective-permute-start(bf16[64,2048]{1,0:T(8,128)(2,1)} %collective-permute-done.8.refs_3_), channel_id=1, source_target_pairs={{0,128},{128,0},{1,129},{129,1},{2,130},{130,2},{3,131},{131,3},{4... | collective-permute-start | bytes 786440 | tf_op jit(solution)/shard_map/ppermute | solution.py:49
  231.4 4.2 %collective-permute-start.22 = (bf16[512,256]{1,0:T(8,128)(2,1)}, bf16[512,256]{1,0:T(8,128)(2,1)}, u32[]{:S(2)}, u32[]{:S(2)}) collective-permute-start(bf16[512,256]{1,0:T(8,128)(2,1)} %collective-permute-done.18.refs_11_), channel_id=1, source_target_pairs={{0,128},{128,0},{1,129},{129,1},{2,130},{130,2},{3,131},{131,3},{4... | collective-permute-start | bytes 786440 | tf_op jit(solution)/shard_map/ppermute | solution.py:49

commit v3 on v2

v3 whole, which is shorter than its diff:
```python
import functools

import jax
import jax.numpy as jnp
from jax import lax
from jax.experimental import pallas as pl
from jax.experimental.pallas import tpu as pltpu
from jax.sharding import PartitionSpec as P

BF = jnp.bfloat16
F32 = jnp.float32
I32 = jnp.int32
SWAP = ((0, 1), (1, 0))
NEAR = ((0, 1), (1, 0), (2, 3), (3, 2))
FAR = ((0, 3), (3, 0), (1, 2), (2, 1))


def dot(left, right, dims):
    return lax.dot_general(left, right, (dims, ((), ())), preferred_element_type=F32)


def ring(count, step):
    return [(i, (i + step) % count) for i in range(count)]


def earlier(count):
    rows = lax.broadcasted_iota(I32, (count, count), 0)
    cols = lax.broadcasted_iota(I32, (count, count), 1)
    return (rows < cols).astype(BF)


def bits(ctx_index):
    high = ctx_index // 2
    return (ctx_index % 2 + high) % 2, high


def reduce_ctx(parts, near, far, beside):
    join = lax.optimization_barrier
    plans = (((near, NEAR), (far, FAR)), ((far, FAR), (near, NEAR)))
    for step in range(2):
        sent, kept = [], []
        for part, plan in zip(parts, plans):
            keep = plan[step][0]
            size = part.shape[0] // 2
            sent.append(lax.dynamic_slice_in_dim(part, (1 - keep) * size, size))
            kept.append(lax.dynamic_slice_in_dim(part, keep * size, size))
        sent, kept = join((sent, kept))
        got = [lax.ppermute(part, "ctx", plan[step][1]) for part, plan in zip(sent, plans)]
        got, kept, beside = join((got, kept, beside))
        parts = [(a.astype(F32) + b.astype(F32)).astype(BF) for a, b in zip(kept, got)]
    parts = join(parts)
    side = [lax.ppermute(part, "ctx", plan[1][1]) for part, plan in zip(parts, plans)]
    across = [lax.ppermute(part, "ctx", plan[0][1]) for part, plan in zip(parts, plans)]
    side = join(side)
    corner = [lax.ppermute(part, "ctx", plan[0][1]) for part, plan in zip(side, plans)]
    return [tuple(four) for four in zip(parts, side, across, corner)], beside


def dispatch_kernel(base, picks, tokens, out_grad, sent, spread, high_ref, low_ref, code_ref):
    exp_count, tok_dev = code_ref.shape
    highs, lows = high_ref.shape[0] // exp_count, low_ref.shape[0] // exp_count
    rows = spread.shape[0]
    slots = rows * pl.num_programs(0) // exp_count
    iota = lax.broadcasted_iota

    @pl.when(pl.program_id(0) == 0)
    def _():
        for e in range(exp_count):
            local = picks[0, e : e + 1, :] - base[0]
            wide = (highs, local.shape[1])
            high_ref[e * highs : (e + 1) * highs, :] = (
                iota(I32, wide, 0) == jnp.broadcast_to(local >> (lows.bit_length() - 1), wide)
            ).astype(F32)
            wide = (lows, local.shape[1])
            low_ref[e * lows : (e + 1) * lows, :] = (
                iota(I32, wide, 0) == jnp.broadcast_to(local & (lows - 1), wide)
            ).astype(F32)
        pairs = dot(high_ref[...].astype(BF), low_ref[...].astype(BF), ((1,), (1,)))
        same = iota(I32, pairs.shape, 0) // highs == iota(I32, pairs.shape, 1) // lows
        pairs = jnp.where(same, pairs, 0.0).astype(BF)
        wide = (exp_count * lows, tok_dev)
        fold = (iota(I32, wide, 0) % lows == iota(I32, wide, 1) % lows).astype(BF)
        by_high = dot(pairs, fold, ((1,), (0,)))
        same = iota(I32, by_high.shape, 0) % highs == iota(I32, by_high.shape, 1) // lows
        by_high = jnp.where(same, by_high, 0.0).astype(BF)
        wide = (exp_count, exp_count * highs)
        fold = (iota(I32, wide, 0) == iota(I32, wide, 1) // highs).astype(BF)
        picked = dot(fold, by_high, ((1,), (0,)))
        rank = dot(picked.astype(BF), earlier(tok_dev), ((1,), (0,)))
        code_ref[...] = picked * (rank + 1.0)

    wide = (rows, exp_count)
    at = pl.program_id(0) * (rows // slots)
    repeat = (iota(I32, wide, 0) // slots + at == iota(I32, wide, 1)).astype(BF)
    code = dot(repeat, code_ref[...].astype(BF), ((1,), (0,)))
    slot = (iota(I32, code.shape, 0) % slots + 1).astype(F32)
    chosen = (code == slot).astype(F32).astype(BF)
    spread[...] = chosen
    feat = tokens.shape[2]
    sent[:, :feat] = dot(chosen, tokens[0], ((1,), (0,))).astype(BF)
    sent[:, feat:] = dot(chosen, out_grad[0], ((1,), (0,))).astype(BF)


def dispatch(base, picks, tokens, out_grad, slots):
    exp_count, pick_total = picks.shape[1:]
    tok_dev, feat = tokens.shape[1:]
    lows = 16
    steps = 4
    rows = exp_count * slots // steps

    def whole(shape):
        return pl.BlockSpec(shape, lambda i: (0,) * len(shape))

    return pl.pallas_call(
        dispatch_kernel,
        grid=(steps,),
        in_specs=[
            pl.BlockSpec(memory_space=pltpu.SMEM),
            whole(picks.shape),
            whole(tokens.shape),
            whole(out_grad.shape),
        ],
        out_specs=[
            pl.BlockSpec((rows, 2 * feat), lambda i: (i, 0)),
            pl.BlockSpec((rows, tok_dev), lambda i: (i, 0)),
        ],
        out_shape=[
            jax.ShapeDtypeStruct((exp_count * slots, 2 * feat), BF),
            jax.ShapeDtypeStruct((exp_count * slots, tok_dev), BF),
        ],
        scratch_shapes=[
            pltpu.VMEM((exp_count * tok_dev // lows, pick_total), F32),
            pltpu.VMEM((exp_count * lows, pick_total), F32),
            pltpu.VMEM((exp_count, tok_dev), F32),
        ],
        compiler_params=pltpu.CompilerParams(vmem_limit_bytes=32 * 1024 * 1024),
        cost_estimate=pl.CostEstimate(
            flops=4 * exp_count * slots * tok_dev * feat,
            bytes_accessed=4 * exp_count * slots * feat,
            transcendentals=0,
        ),
    )(jnp.reshape(base, (1,)).astype(I32), picks, tokens, out_grad)


def pass_kernel(rows_in, rows_grad, weight_in, weight_out, gate, grads, pre, gated, gate_slot):
    pre_act = dot(rows_in[...], weight_in[...], ((1,), (0,)))
    back = dot(rows_grad[...], weight_out[...], ((1,), (1,)))
    sig = 1.0 / (1.0 + jnp.exp(-pre_act))
    activation = (pre_act * sig).astype(BF).astype(F32)
    pre_grad = (gate[...] * back * (sig * (1.0 + pre_act * (1.0 - sig)))).astype(BF)
    gate_slot[...] = jnp.sum(activation * back, axis=1, keepdims=True)
    gated[...] = (gate[...] * activation).astype(BF)
    pre[...] = pre_grad
    grads[...] = dot(pre_grad, weight_in[...], ((1,), (1,))).astype(BF)


def expert_pass(rows, weight_in, weight_out, gate):
    count, feat, hid = rows.shape[0], weight_in.shape[0], weight_in.shape[1]
    size = min(256, count)

    def block(cols, at=0):
        return pl.BlockSpec((size, cols), lambda i: (i, at))

    def whole(shape):
        return pl.BlockSpec(shape, lambda i: (0, 0))

    return pl.pallas_call(
        pass_kernel,
        grid=(count // size,),
        in_specs=[
            block(feat),
            block(feat, 1),
            whole((feat, hid)),
            whole((hid, feat)),
            block(1),
        ],
        out_specs=[block(feat), block(hid), block(hid), block(1)],
        out_shape=[
            jax.ShapeDtypeStruct((count, feat), BF),
            jax.ShapeDtypeStruct((count, hid), BF),
            jax.ShapeDtypeStruct((count, hid), BF),
            jax.ShapeDtypeStruct((count, 1), F32),
        ],
        compiler_params=pltpu.CompilerParams(vmem_limit_bytes=48 * 1024 * 1024),
        cost_estimate=pl.CostEstimate(
            flops=6 * count * feat * hid,
            bytes_accessed=2 * (3 * count * feat + 2 * feat * hid),
            transcendentals=count * hid,
        ),
    )(rows, rows, weight_in, weight_out, gate)


def outer_kernel(scale, where, rows_in, rows_grad, pre_a, pre_b, gated_a, gated_b, *refs):
    half = pre_a.shape[1]
    gated = jnp.concatenate((gated_a[...], gated_b[...]), axis=1)
    pre = jnp.concatenate((pre_a[...], pre_b[...]), axis=1)
    out = (dot(gated, rows_grad[...], ((0,), (0,))) * scale).astype(BF)
    inn = (dot(rows_in[...], pre, ((0,), (0,))) * scale).astype(BF)
    refs[0][...], refs[2][...] = out[:half], out[half:]
    refs[1][...], refs[3][...] = inn[:, :half], inn[:, half:]


def outer(rows, pre, gated, core, scale):
    count, feat, hid = rows.shape[0], rows.shape[1] // 2, pre.shape[1] // 2
    steps = 4
    size = feat // steps
    out_block = pl.BlockSpec((hid, size), lambda i, at: (0, i))
    in_block = pl.BlockSpec((size, hid), lambda i, at: (i, 0))
    theirs = pl.BlockSpec((count, hid), lambda i, at: (0, 1 - at[0]))
    mine = pl.BlockSpec((count, hid), lambda i, at: (0, at[0]))
    out_type = jax.ShapeDtypeStruct((hid, feat), BF)
    in_type = jax.ShapeDtypeStruct((feat, hid), BF)
    parts = pl.pallas_call(
        functools.partial(outer_kernel, scale),
        grid_spec=pltpu.PrefetchScalarGridSpec(
            num_scalar_prefetch=1,
            grid=(steps,),
            in_specs=[
                pl.BlockSpec((count, size), lambda i, at: (0, i)),
                pl.BlockSpec((count, size), lambda i, at: (0, i + steps)),
                theirs,
                mine,
                theirs,
                mine,
            ],
            out_specs=[out_block, in_block] * 2,
        ),
        out_shape=[out_type, in_type] * 2,
        compiler_params=pltpu.CompilerParams(vmem_limit_bytes=48 * 1024 * 1024),
        cost_estimate=pl.CostEstimate(
            flops=8 * count * feat * hid,
            bytes_accessed=4 * (count * feat + 2 * feat * hid),
            transcendentals=0,
        ),
    )(jnp.reshape(core, (1,)).astype(I32), rows, rows, pre, pre, gated, gated)
    return parts[:2], parts[2:]


def assemble_kernel(where, *refs):
    out_pieces, in_pieces = refs[:8], refs[8:16]
    out_ref, in_ref = refs[16], refs[17]
    core, near, far = where[0], where[1], where[2]
    out_rows, in_rows, in_cols = out_pieces[0].shape[0], in_pieces[0].shape[0], in_pieces[0].shape[1]
    for k in range(8):
        half = core if k < 4 else 1 - core
        flip_b, flip_a = k % 2, (k // 2) % 2
        a = 1 - near if flip_a else near
        b = 1 - far if flip_b else far
        row = pl.multiple_of(((half * 2 + a) * 2 + b) * out_rows, out_rows)
        out_ref[pl.ds(row, out_rows), :] = out_pieces[k][...]
        a = 1 - far if flip_a else far
        b = 1 - near if flip_b else near
        row = pl.multiple_of((a * 2 + b) * in_rows, in_rows)
        col = pl.multiple_of(half * in_cols, in_cols)
        in_ref[pl.ds(row, in_rows), pl.ds(col, in_cols)] = in_pieces[k][...]


def assemble(where, out_pieces, in_pieces, out_shape, in_shape):
    moved = 4 * (out_shape[0] * out_shape[1] + in_shape[0] * in_shape[1])
    return pl.pallas_call(
        assemble_kernel,
        in_specs=[pl.BlockSpec(memory_space=pltpu.SMEM)]
        + [pl.BlockSpec(memory_space=pltpu.VMEM)] * 16,
        out_specs=[pl.BlockSpec(memory_space=pltpu.VMEM)] * 2,
        out_shape=[jax.ShapeDtypeStruct(out_shape, BF), jax.ShapeDtypeStruct(in_shape, BF)],
        compiler_params=pltpu.CompilerParams(vmem_limit_bytes=24 * 1024 * 1024),
        cost_estimate=pl.CostEstimate(flops=0, bytes_accessed=moved, transcendentals=0),
    )(where, *out_pieces, *in_pieces)


def shards(tokens, out_grad, w_in, w_out, picks, gates):
    ctx_count = lax.axis_size("ctx")
    exp_count = lax.axis_size("expert")
    core = lax.axis_index("dp")
    ctx_index = lax.axis_index("ctx")
    exp_index = lax.axis_index("expert")
    tok_dev, feat = tokens.shape[1], tokens.shape[2]
    hid = w_in.shape[2]
    pick_total = picks.shape[2]
    share = pick_total // ctx_count
    slots = ctx_count * 4
    grad_scale = (lax.axis_size("dp") * pick_total) ** (-0.5)
    lists = picks[0]
    before = earlier(tok_dev)
    tok_ids = jnp.arange(tok_dev, dtype=I32)

    def swap(rows):
        out = rows.reshape(exp_count, -1, rows.shape[1])
        out = lax.all_to_all(out, "expert", split_axis=0, concat_axis=0, tiled=True)
        return out.reshape(rows.shape)

    base = (ctx_index * exp_count + exp_index) * tok_dev
    sent, spread = dispatch(base, picks, tokens, out_grad, slots)
    arrived = swap(sent)

    own = lax.dynamic_index_in_dim(lists, exp_index, 0, keepdims=False)
    offset = own - ctx_index * (exp_count * tok_dev)
    block = offset // tok_dev
    inside = (block >= 0) & (block < exp_count)
    token = offset % tok_dev
    in_block = (inside[:, None] & (block[:, None] == jnp.arange(exp_count)[None, :])).astype(BF)
    at_token = (token[:, None] == tok_ids[None, :]).astype(BF)
    held = dot(in_block, at_token, ((0,), (0,))).astype(BF)
    rank_own = dot(held, before, ((1,), (0,))).astype(BF)
    rank_pick = jnp.sum(
        dot(in_block, rank_own, ((1,), (0,))) * at_token.astype(F32), axis=1
    ).astype(I32)
    gate_mine = gates[0, 0]
    gate_all = jnp.zeros((ctx_count, share), F32)
    gate_all = lax.dynamic_update_slice_in_dim(gate_all, gate_mine[None], ctx_index, 0)
    for step in range(1, ctx_count):
        got = lax.ppermute(gate_mine, "ctx", ring(ctx_count, step))
        gate_all = lax.dynamic_update_slice_in_dim(
            gate_all, got[None], (ctx_index - step) % ctx_count, 0
        )
    gate_all = gate_all.reshape(pick_total)

    place = jnp.where(inside, block * slots + rank_pick, -1)
    at_slot = place[:, None] == jnp.arange(exp_count * slots, dtype=I32)[None, :]
    slot_gate = jnp.sum(jnp.where(at_slot, gate_all[:, None], 0.0), axis=0)[:, None]

    row_grads, pre_grad, gated, gate_slot = expert_pass(arrived, w_in[0], w_out[0], slot_gate)
    theirs, mine = outer(arrived, pre_grad, gated, core, grad_scale)
    got = [lax.ppermute(part, "dp", SWAP) for part in theirs]
    row_grads, _ = lax.optimization_barrier((row_grads, theirs))
    returned = swap(row_grads)
    halves = [(a.astype(F32) + b.astype(F32)).astype(BF) for a, b in zip(mine, got)]

    gate_pick = jnp.sum(jnp.where(at_slot, gate_slot[:, 0][None, :], 0.0), axis=1)
    gate_rows = gate_pick.reshape(ctx_count, share)
    gate_grad = lax.dynamic_index_in_dim(gate_rows, ctx_index, 0, keepdims=False)
    for step in range(1, ctx_count):
        term = lax.dynamic_index_in_dim(
            gate_rows, (ctx_index + step) % ctx_count, 0, keepdims=False
        )
        gate_grad = gate_grad + lax.ppermute(term, "ctx", ring(ctx_count, step))

    near, far = bits(ctx_index)
    pieces, gate_grad = reduce_ctx(halves, near, far, gate_grad)
    pieces = [four + tuple(lax.ppermute(term, "dp", SWAP) for term in four) for four in pieces]
    token_total = dot(spread, returned, ((0,), (0,))).astype(BF)
    pieces, token_total = lax.optimization_barrier((pieces, token_total))
    out_total, in_total = assemble(
        jnp.stack((core, near, far)).astype(I32), *pieces, (hid, feat), (feat, hid)
    )

    return (
        token_total[None],
        in_total[None],
        out_total[None],
        gate_grad.reshape(1, 1, share),
    )


def solution(mesh):
    placed = (
        P("dp", ("ctx", "expert"), None),
        P("dp", ("ctx", "expert"), None),
        P("expert", None, None),
        P("expert", None, None),
        P("dp", None, None),
        P("dp", "expert", "ctx"),
    )
    return jax.shard_map(
        shards,
        mesh=mesh,
        in_specs=placed,
        out_specs=(
            P("dp", ("ctx", "expert"), None),
            P("expert", None, None),
            P("expert", None, None),
            P("dp", "expert", "ctx"),
        ),
        check_vma=False,
    )
```

time: 370 us -> 195 us (0.53)
  Pallas kernels: 129 us -> 19.7 us
  matrix products: 37 us -> 3.96 us
  starting transfers between devices: 55.6 us -> 37.8 us
  other arithmetic: 14.7 us -> 5.89 us
  waiting for transfers between devices: 125 us -> 117 us
  local copies, waits for them, and re-layouts: 2.46 us -> 7.19 us
    pallas_call x1, Pallas kernels: 129 us -> 3.43 us  [assemble(): pl.pallas_call(assemble_kernel, in_specs=[pl.BlockSpec(memory_space=pltpu...]
    dot_general x21 -> x3, matrix products: 37 us -> 3.96 us  [dot(): lax.dot_general(left, right, (dims, ((), ())), preferred_element_type=F32)]
    pallas_call x0 -> x3, Pallas kernels: none -> 16.3 us  [the longest x1 7.62 us: expert_pass(): pl.pallas_call(pass_kernel, grid=(count // size,), in_specs=[block(feat),...]
    all_to_all x4 -> x2, starting transfers between devices: 33.7 us -> 18.7 us  [swap(): out = lax.all_to_all(out, 'expert', split_axis=0, concat_axis=0, tiled=True)]
    reduce_or x1 -> x0, other arithmetic: 5.69 us -> none  [shards(): picked = jnp.any(local[:, :, None] == tok_ids[None, None, :], axis=1)]
    unnamed x33 -> x13, local copies, waits for them, and re-layouts: 0.08 us -> 5.01 us
    ppermute x3, waiting for transfers between devices: 13.6 us -> 9.17 us  [shards(): gate_grad = gate_grad + lax.ppermute(term, 'ctx', ring(ctx_count, step))]
    all_to_all x4 -> x2, waiting for transfers between devices: 88.8 us -> 86 us  [swap(): out = lax.all_to_all(out, 'expert', split_axis=0, concat_axis=0, tiled=True)]
  transfers between devices with their start and end apart: 30 -> 28, of which waited for: 10 -> 10; matrix products, arithmetic and copies ran while one was open for 9% -> 6% of each run, Pallas kernels for 0% -> 0%
where the time goes in v3:
time: 195 us; the launch traced here: 193 us
  waiting for transfers between devices  117 us (60%)
  starting transfers between devices  37.8 us (19%)
  Pallas kernels  19.7 us (10%)
  local copies, waits for them, and re-layouts  7.19 us (4%)
  other arithmetic  5.89 us (3%)
  matrix products  3.96 us (2%)
    all_to_all x2, waiting for transfers between devices, swap(): out = lax.all_to_all(out, 'expert', split_axis=0, concat_axis=0, tiled=True)  86 us
    all_to_all x2, starting transfers between devices, swap(): out = lax.all_to_all(out, 'expert', split_axis=0, concat_axis=0, tiled=True)  18.7 us
    ppermute x3, waiting for transfers between devices, shards(): gate_grad = gate_grad + lax.ppermute(term, 'ctx', ring(ctx_count, step))  9.17 us
    pallas_call x1, Pallas kernels, expert_pass(): pl.pallas_call(pass_kernel, grid=(count // size,), in_specs=[block(feat),...  7.62 us
    ppermute x4, waiting for transfers between devices, reduce_ctx(): lax.ppermute(part, 'ctx', plan[0][1])  7.6 us
    ppermute x4, waiting for transfers between devices, reduce_ctx(): lax.ppermute(part, 'ctx', plan[step][1])  6.89 us
    pallas_call x1, Pallas kernels, outer(): pl.pallas_call(functools.partial(outer_kernel, scale), grid_spec=pltpu.Pr...  5.62 us
    ppermute x4, starting transfers between devices, reduce_ctx(): lax.ppermute(part, 'ctx', plan[0][1])  5.54 us
  transfers between devices with their start and end apart: 28, of which 10 were waited for; matrix products, arithmetic and copies ran while one was open for 6% of the time, Pallas kernels for 0%

profile of v3, /device:TPU:6, one launch (start us, length us, event | category | flops | bytes accessed | tf_op | source)
XLA Modules:
  0.0 192.5 jit_solution(3366708978135654461)
XLA Ops:
  0.7 0.9 copy-done.2
  1.5 1.0 copy-done.3
  2.6 1.0 copy-done.4
  3.6 3.0 %shard_map.93 = (bf16[512,4096]{1,0:T(8,128)(2,1)S(1)}, bf16[512,128]{1,0:T(8,128)(2,1)S(1)}) custom-call(s32[1]{0:T(128)} %bitcast.1.base, s32[1,32,1024]{2,1,0:T(8,128)S(1)} %copy-done.2, bf16[1,128,2048]{2,1,0:T(8,128)(2,1)S(1)} %copy-done.3, bf16[1,128,2048]{2,1,0:T(8,128)(2,1)S(1)} %copy-done.4), custom_call_target="tpu_custom_call" | custom-call | flops 536870912 | bytes 4194304 | tf_op jit(solution)/shard_map/pallas_call | solution.py:114
  6.7 2.0 %copy-done = bf16[512,4096]{1,0:T(8,128)(2,1)} copy-done((bf16[512,4096]{1,0:T(8,128)(2,1)}, bf16[512,4096]{1,0:T(8,128)(2,1)S(1)}, u32[]{:S(2)}) %copy-start) | copy-done | bytes 4194328
  8.7 11.8 %all-to-all-start = ((bf16[32,16,4096]{2,1,0:T(8,128)(2,1)}), bf16[32,16,4096]{2,1,0:T(8,128)(2,1)}, u32[]{:S(2)}, u32[]{:S(2)}) async-start(bf16[32,16,4096]{2,1,0:T(8,128)(2,1)} %bitcast.30), calls=%async_computation | async-start | bytes 8388608 | tf_op jit(solution)/shard_map/all_to_all | solution.py:289
  20.4 0.6 collective-permute-start
  21.0 2.4 %collective-permute-start.1 = (f32[256]{0:T(256)S(1)}, f32[256]{0:T(256)S(1)}, u32[]{:S(2)}, u32[]{:S(2)}) collective-permute-start(f32[256]{0:T(256)S(1)} %bitcast.41), channel_id=1, source_target_pairs={{0,64},{32,96},{64,0},{96,32},{1,65},{33,97},{65,1},{97,33},{2,66}... | collective-permute-start | bytes 3080 | tf_op jit(solution)/shard_map/ppermute | solution.py:312
  23.4 0.8 dynamic-slice_subtract_fusion
  24.2 0.5 convolution_convert_fusion.2
  24.8 0.6 fusion
  25.5 0.6 collective-permute-done.1
  26.1 2.1 %collective-permute-done.2 = f32[256]{0:T(256)S(1)} collective-permute-done((f32[256]{0:T(256)S(1)}, f32[256]{0:T(256)S(1)}, u32[]{:S(2)}, u32[]{:S(2)}) %collective-permute-start.2) | collective-permute-done | bytes 1056 | tf_op jit(solution)/shard_map/ppermute | solution.py:312
  28.3 0.3 select_reduce_fusion.1
  28.6 0.2 copy.11.gate
  28.8 86.0 %all-to-all-done = bf16[32,16,4096]{2,1,0:T(8,128)(2,1)} async-done(((bf16[32,16,4096]{2,1,0:T(8,128)(2,1)}), bf16[32,16,4096]{2,1,0:T(8,128)(2,1)}, u32[]{:S(2)}, u32[]{:S(2)}) %all-to-all-start) | async-done | bytes 4194336 | tf_op jit(solution)/shard_map/all_to_all | solution.py:289
  114.8 7.6 %shard_map.94 = (bf16[512,2048]{1,0:T(8,128)(2,1)}, bf16[512,512]{1,0:T(8,128)(2,1)S(1)}, bf16[512,512]{1,0:T(8,128)(2,1)S(1)}, f32[512,1]{1,0:T(8,128)S(1)}) custom-call(bf16[512,4096]{1,0:T(8,128)(2,1)} %bitcast.3.rows_in.rows_grad, bf16[512,4096]{1,0:T(8,128)(2,1)} %bitcast.3.rows_in.rows_grad, bf16[2048,512]{1,0:T(8,128)(2,1)S(1)} %bitcast.31, ...), custom_call_target="tpu_custom_call" | custom-call | flops 3221225472 | bytes 10485760 | tf_op jit(solution)/shard_map/pallas_call | solution.py:167
  122.4 5.6 %shard_map.95 = (bf16[256,2048]{1,0:T(8,128)(2,1)}, bf16[2048,256]{1,0:T(8,128)(2,1)}, bf16[256,2048]{1,0:T(8,128)(2,1)S(1)}, bf16[2048,256]{1,0:T(8,128)(2,1)S(1)}) custom-call(s32[1]{0:T(128)} %bitcast.where, bf16[512,4096]{1,0:T(8,128)(2,1)} %bitcast.3.rows_in.rows_grad, bf16[512,4096]{1,0:T(8,128)(2,1)} %bitcast.3.rows_in.rows_grad, ...), custom_call_target="tpu_custom_call" | custom-call | flops 2147483648 | bytes 8388608 | tf_op jit(solution)/shard_map/pallas_call | solution.py:213
  128.0 0.5 collective-permute-start.3
  128.5 6.9 %all-to-all-start.1 = ((bf16[32,16,2048]{2,1,0:T(8,128)(2,1)}), bf16[32,16,2048]{2,1,0:T(8,128)(2,1)}, u32[]{:S(2)}, u32[]{:S(2)}) async-start(bf16[32,16,2048]{2,1,0:T(8,128)(2,1)} %bitcast.17), calls=%async_computation.1 | async-start | bytes 4194304 | tf_op jit(solution)/shard_map/all_to_all | solution.py:289
  135.5 1.5 add_convert_fusion
  137.0 0.9 constant_dynamic-slice_fusion.8
  137.9 1.6 add_convert_fusion.1
  139.5 0.9 constant_dynamic-slice_fusion.9
  140.4 0.8 collective-permute-start.5
  141.2 1.2 collective-permute-start.6
  142.5 0.5 select_reduce_fusion
  143.0 2.3 %collective-permute-start.7 = (f32[256]{0:T(256)S(1)}, f32[256]{0:T(256)S(1)}, u32[]{:S(2)}, u32[]{:S(2)}) collective-permute-start(f32[256]{0:T(256)S(1)} %bitcast.50), channel_id=1, source_target_pairs={{0,32},{32,64},{64,96},{96,0},{1,33},{33,65},{65,97},{97,1},{2,34}... | collective-permute-start | bytes 3080 | tf_op jit(solution)/shard_map/ppermute | solution.py:336
  145.3 0.2 collective-permute-start.8
  145.5 1.3 collective-permute-start.9
  146.8 7.4 %collective-permute-done.7 = f32[256]{0:T(256)S(1)} collective-permute-done((f32[256]{0:T(256)S(1)}, f32[256]{0:T(256)S(1)}, u32[]{:S(2)}, u32[]{:S(2)}) %collective-permute-start.7) | collective-permute-done | bytes 1056 | tf_op jit(solution)/shard_map/ppermute | solution.py:336
  154.2 1.8 collective-permute-done.9
  156.0 0.6 add_add_fusion
  156.9 1.2 collective-permute-start.10
  158.2 6.9 %collective-permute-done.10 = bf16[64,2048]{1,0:T(8,128)(2,1)S(1)} collective-permute-done((bf16[64,2048]{1,0:T(8,128)(2,1)S(1)}, bf16[64,2048]{1,0:T(8,128)(2,1)S(1)}, u32[]{:S(2)}, u32[]{:S(2)}) %collective-permute-start.10) | collective-permute-done | bytes 262176 | tf_op jit(solution)/shard_map/ppermute | solution.py:48
  165.2 1.8 collective-permute-start.12
  167.0 2.0 %collective-permute-start.14 = (bf16[64,2048]{1,0:T(8,128)(2,1)S(1)}, bf16[64,2048]{1,0:T(8,128)(2,1)S(1)}, u32[]{:S(2)}, u32[]{:S(2)}) collective-permute-start(bf16[64,2048]{1,0:T(8,128)(2,1)S(1)} %add_convert_fusion.5.refs_0_), channel_id=1, source_target_pairs={{0,32},{32,0},{64,96},{96,64},{1,33},{33,1},{65,97},{97,65},{2,34}... | collective-permute-start | bytes 786440 | tf_op jit(solution)/shard_map/ppermute | solution.py:53
  169.1 1.5 collective-permute-start.20
  170.6 4.8 %collective-permute-done.12.refs_1_ = bf16[64,2048]{1,0:T(8,128)(2,1)S(1)} collective-permute-done((bf16[64,2048]{1,0:T(8,128)(2,1)S(1)}, bf16[64,2048]{1,0:T(8,128)(2,1)S(1)}, u32[]{:S(2)}, u32[]{:S(2)}) %collective-permute-start.12) | collective-permute-done | bytes 262176 | tf_op jit(solution)/shard_map/ppermute | solution.py:52
  175.3 0.2 collective-permute-start.15
  175.6 2.5 %collective-permute-done.14.refs_2_ = bf16[64,2048]{1,0:T(8,128)(2,1)S(1)} collective-permute-done((bf16[64,2048]{1,0:T(8,128)(2,1)S(1)}, bf16[64,2048]{1,0:T(8,128)(2,1)S(1)}, u32[]{:S(2)}, u32[]{:S(2)}) %collective-permute-start.14) | collective-permute-done | bytes 262176 | tf_op jit(solution)/shard_map/ppermute | solution.py:53
  178.1 1.8 collective-permute-start.21
  180.0 0.5 collective-permute-start.23
  180.6 3.4 %collective-permute-done.15.refs_3_ = bf16[64,2048]{1,0:T(8,128)(2,1)S(1)} collective-permute-done((bf16[64,2048]{1,0:T(8,128)(2,1)S(1)}, bf16[64,2048]{1,0:T(8,128)(2,1)S(1)}, u32[]{:S(2)}, u32[]{:S(2)}) %collective-permute-start.15) | collective-permute-done | bytes 262176 | tf_op jit(solution)/shard_map/ppermute | solution.py:55
  184.0 1.6 collective-permute-done.21.refs_11_
  185.7 0.5 collective-permute-start.25
  186.2 2.9 %convolution_convert_fusion = bf16[128,2048]{1,0:T(8,128)(2,1)} fusion(bf16[512,128]{1,0:T(8,128)(2,1)S(1)} %get-tuple-element.85, bf16[512,2048]{1,0:T(8,128)(2,1)} %bitcast.18), kind=kOutput, calls=%fused_computation | convolution fusion | flops 268697600 | bytes 2752512 | tf_op jit(solution)/shard_map/dot_general | solution.py:19
  189.1 3.4 %shard_map.96 = (bf16[512,2048]{1,0:T(8,128)(2,1)}, bf16[2048,512]{1,0:T(8,128)(2,1)}) custom-call(s32[3]{0:T(128)S(1)} %pad_add_fusion.where, bf16[64,2048]{1,0:T(8,128)(2,1)S(1)} %add_convert_fusion.5.refs_0_, bf16[64,2048]{1,0:T(8,128)(2,1)S(1)} %collective-permute-done.12.refs_1_, bf16[64,2048]{1,0:T(8,128)(2,1)S(1)} %collective-permute-done.14.refs_2_, ...), custom_call_target="tpu_custom_call" | custom-call | bytes 8388608 | tf_op jit(solution)/shard_map/pallas_call | solution.py:260
  (55 shorter events, 1.1 us)
Async XLA Ops:
  0.6 0.9 copy-start.2
  1.5 1.0 copy-start.3
  2.6 1.0 copy-start.4
  6.7 2.0 %copy-start = (bf16[512,4096]{1,0:T(8,128)(2,1)}, bf16[512,4096]{1,0:T(8,128)(2,1)S(1)}, u32[]{:S(2)}) copy-start(bf16[512,4096]{1,0:T(8,128)(2,1)S(1)} %get-tuple-element.56) | copy-start | bytes 12582916
  8.7 11.8 %copy-start.5 = (f32[1,1,256]{2,1,0:T(1,128)S(1)}, f32[1,1,256]{2,1,0:T(1,128)}, u32[]{:S(2)}) copy-start(f32[1,1,256]{2,1,0:T(1,128)} %param.11) | copy-start | bytes 3076
  8.7 106.1 %copy-start.1 = (bf16[1,2048,512]{2,1,0:T(8,128)(2,1)S(1)}, bf16[1,2048,512]{2,1,0:T(8,128)(2,1)}, u32[]{:S(2)}) copy-start(bf16[1,2048,512]{2,1,0:T(8,128)(2,1)} %param.8) | copy-start | bytes 6291460
  8.7 106.1 %all-to-all-start = ((bf16[32,16,4096]{2,1,0:T(8,128)(2,1)}), bf16[32,16,4096]{2,1,0:T(8,128)(2,1)}, u32[]{:S(2)}, u32[]{:S(2)}) async-start(bf16[32,16,4096]{2,1,0:T(8,128)(2,1)} %bitcast.30), calls=%async_computation | async-start | bytes 8388608 | tf_op jit(solution)/shard_map/all_to_all | solution.py:289
  20.4 5.0 %collective-permute-start = (f32[256]{0:T(256)S(1)}, f32[256]{0:T(256)S(1)}, u32[]{:S(2)}, u32[]{:S(2)}) collective-permute-start(f32[256]{0:T(256)S(1)} %bitcast.40), channel_id=1, source_target_pairs={{0,32},{32,64},{64,96},{96,0},{1,33},{33,65},{65,97},{97,1},{2,34}... | collective-permute-start | bytes 3080 | tf_op jit(solution)/shard_map/ppermute | solution.py:312
  21.0 5.1 %collective-permute-start.1 = (f32[256]{0:T(256)S(1)}, f32[256]{0:T(256)S(1)}, u32[]{:S(2)}, u32[]{:S(2)}) collective-permute-start(f32[256]{0:T(256)S(1)} %bitcast.41), channel_id=1, source_target_pairs={{0,64},{32,96},{64,0},{96,32},{1,65},{33,97},{65,1},{97,33},{2,66}... | collective-permute-start | bytes 3080 | tf_op jit(solution)/shard_map/ppermute | solution.py:312
  23.4 4.8 %collective-permute-start.2 = (f32[256]{0:T(256)S(1)}, f32[256]{0:T(256)S(1)}, u32[]{:S(2)}, u32[]{:S(2)}) collective-permute-start(f32[256]{0:T(256)S(1)} %bitcast.42), channel_id=1, source_target_pairs={{0,96},{32,0},{64,32},{96,64},{1,97},{33,1},{65,33},{97,65},{2,98}... | collective-permute-start | bytes 3080 | tf_op jit(solution)/shard_map/ppermute | solution.py:312
  128.0 7.5 %collective-permute-start.4 = (bf16[2048,256]{1,0:T(8,128)(2,1)}, bf16[2048,256]{1,0:T(8,128)(2,1)}, u32[]{:S(2)}, u32[]{:S(2)}) collective-permute-start(bf16[2048,256]{1,0:T(8,128)(2,1)} %get-tuple-element.62), channel_id=1, source_target_pairs={{0,128},{128,0},{1,129},{129,1},{2,130},{130,2},{3,131},{131,3},{4... | collective-permute-start | bytes 3145736 | tf_op jit(solution)/shard_map/ppermute | solution.py:324
  128.0 9.8 %collective-permute-start.3 = (bf16[256,2048]{1,0:T(8,128)(2,1)}, bf16[256,2048]{1,0:T(8,128)(2,1)}, u32[]{:S(2)}, u32[]{:S(2)}) collective-permute-start(bf16[256,2048]{1,0:T(8,128)(2,1)} %get-tuple-element.60), channel_id=1, source_target_pairs={{0,128},{128,0},{1,129},{129,1},{2,130},{130,2},{3,131},{131,3},{4... | collective-permute-start | bytes 3145736 | tf_op jit(solution)/shard_map/ppermute | solution.py:324
  128.5 57.7 %all-to-all-start.1 = ((bf16[32,16,2048]{2,1,0:T(8,128)(2,1)}), bf16[32,16,2048]{2,1,0:T(8,128)(2,1)}, u32[]{:S(2)}, u32[]{:S(2)}) async-start(bf16[32,16,2048]{2,1,0:T(8,128)(2,1)} %bitcast.17), calls=%async_computation.1 | async-start | bytes 4194304 | tf_op jit(solution)/shard_map/all_to_all | solution.py:289
  140.4 16.2 %collective-permute-start.5 = (bf16[128,2048]{1,0:T(8,128)(2,1)}, bf16[128,2048]{1,0:T(8,128)(2,1)S(1)}, u32[]{:S(2)}, u32[]{:S(2)}) collective-permute-start(bf16[128,2048]{1,0:T(8,128)(2,1)} %get-tuple-element.63), channel_id=1, source_target_pairs={{0,32},{32,0},{64,96},{96,64},{1,33},{33,1},{65,97},{97,65},{2,34}... | collective-permute-start | bytes 1572872 | tf_op jit(solution)/shard_map/ppermute | solution.py:48
  141.2 15.4 %collective-permute-start.6 = (bf16[1024,256]{1,0:T(8,128)(2,1)}, bf16[1024,256]{1,0:T(8,128)(2,1)S(1)}, u32[]{:S(2)}, u32[]{:S(2)}) collective-permute-start(bf16[1024,256]{1,0:T(8,128)(2,1)} %get-tuple-element.64), channel_id=1, source_target_pairs={{0,96},{96,0},{32,64},{64,32},{1,97},{97,1},{33,65},{65,33},{2,98}... | collective-permute-start | bytes 1572872 | tf_op jit(solution)/shard_map/ppermute | solution.py:48
  143.0 11.2 %collective-permute-start.7 = (f32[256]{0:T(256)S(1)}, f32[256]{0:T(256)S(1)}, u32[]{:S(2)}, u32[]{:S(2)}) collective-permute-start(f32[256]{0:T(256)S(1)} %bitcast.50), channel_id=1, source_target_pairs={{0,32},{32,64},{64,96},{96,0},{1,33},{33,65},{65,97},{97,1},{2,34}... | collective-permute-start | bytes 3080 | tf_op jit(solution)/shard_map/ppermute | solution.py:336
  145.3 8.9 %collective-permute-start.8 = (f32[256]{0:T(256)S(1)}, f32[256]{0:T(256)S(1)}, u32[]{:S(2)}, u32[]{:S(2)}) collective-permute-start(f32[256]{0:T(256)S(1)} %bitcast.49), channel_id=1, source_target_pairs={{0,64},{32,96},{64,0},{96,32},{1,65},{33,97},{65,1},{97,33},{2,66}... | collective-permute-start | bytes 3080 | tf_op jit(solution)/shard_map/ppermute | solution.py:336
  145.5 10.5 %collective-permute-start.9 = (f32[256]{0:T(256)S(1)}, f32[256]{0:T(256)S(1)}, u32[]{:S(2)}, u32[]{:S(2)}) collective-permute-start(f32[256]{0:T(256)S(1)} %bitcast.48), channel_id=1, source_target_pairs={{0,96},{32,0},{64,32},{96,64},{1,97},{33,1},{65,33},{97,65},{2,98}... | collective-permute-start | bytes 3080 | tf_op jit(solution)/shard_map/ppermute | solution.py:336
  156.9 8.1 %collective-permute-start.10 = (bf16[64,2048]{1,0:T(8,128)(2,1)S(1)}, bf16[64,2048]{1,0:T(8,128)(2,1)S(1)}, u32[]{:S(2)}, u32[]{:S(2)}) collective-permute-start(bf16[64,2048]{1,0:T(8,128)(2,1)S(1)} %get-tuple-element.72), channel_id=1, source_target_pairs={{0,96},{96,0},{32,64},{64,32},{1,97},{97,1},{33,65},{65,33},{2,98}... | collective-permute-start | bytes 786440 | tf_op jit(solution)/shard_map/ppermute | solution.py:48
  158.2 6.9 %collective-permute-start.11 = (bf16[512,256]{1,0:T(8,128)(2,1)S(1)}, bf16[512,256]{1,0:T(8,128)(2,1)S(1)}, u32[]{:S(2)}, u32[]{:S(2)}) collective-permute-start(bf16[512,256]{1,0:T(8,128)(2,1)S(1)} %get-tuple-element.73), channel_id=1, source_target_pairs={{0,32},{32,0},{64,96},{96,64},{1,33},{33,1},{65,97},{97,65},{2,34}... | collective-permute-start | bytes 786440 | tf_op jit(solution)/shard_map/ppermute | solution.py:48
  165.2 10.1 %collective-permute-start.12 = (bf16[64,2048]{1,0:T(8,128)(2,1)S(1)}, bf16[64,2048]{1,0:T(8,128)(2,1)S(1)}, u32[]{:S(2)}, u32[]{:S(2)}) collective-permute-start(bf16[64,2048]{1,0:T(8,128)(2,1)S(1)} %add_convert_fusion.5.refs_0_), channel_id=1, source_target_pairs={{0,96},{96,0},{32,64},{64,32},{1,97},{97,1},{33,65},{65,33},{2,98}... | collective-permute-start | bytes 786440 | tf_op jit(solution)/shard_map/ppermute | solution.py:52
  167.0 8.3 %collective-permute-start.13 = (bf16[512,256]{1,0:T(8,128)(2,1)S(1)}, bf16[512,256]{1,0:T(8,128)(2,1)S(1)}, u32[]{:S(2)}, u32[]{:S(2)}) collective-permute-start(bf16[512,256]{1,0:T(8,128)(2,1)S(1)} %add_convert_fusion.4.refs_8_), channel_id=1, source_target_pairs={{0,32},{32,0},{64,96},{96,64},{1,33},{33,1},{65,97},{97,65},{2,34}... | collective-permute-start | bytes 786440 | tf_op jit(solution)/shard_map/ppermute | solution.py:52
  167.0 11.1 %collective-permute-start.14 = (bf16[64,2048]{1,0:T(8,128)(2,1)S(1)}, bf16[64,2048]{1,0:T(8,128)(2,1)S(1)}, u32[]{:S(2)}, u32[]{:S(2)}) collective-permute-start(bf16[64,2048]{1,0:T(8,128)(2,1)S(1)} %add_convert_fusion.5.refs_0_), channel_id=1, source_target_pairs={{0,32},{32,0},{64,96},{96,64},{1,33},{33,1},{65,97},{97,65},{2,34}... | collective-permute-start | bytes 786440 | tf_op jit(solution)/shard_map/ppermute | solution.py:53
  169.1 10.8 %collective-permute-start.20 = (bf16[512,256]{1,0:T(8,128)(2,1)S(1)}, bf16[512,256]{1,0:T(8,128)(2,1)S(1)}, u32[]{:S(2)}, u32[]{:S(2)}) collective-permute-start(bf16[512,256]{1,0:T(8,128)(2,1)S(1)} %add_convert_fusion.4.refs_8_), channel_id=1, source_target_pairs={{0,96},{96,0},{32,64},{64,32},{1,97},{97,1},{33,65},{65,33},{2,98}... | collective-permute-start | bytes 786440 | tf_op jit(solution)/shard_map/ppermute | solution.py:53
  170.6 9.4 %collective-permute-start.16 = (bf16[64,2048]{1,0:T(8,128)(2,1)S(1)}, bf16[64,2048]{1,0:T(8,128)(2,1)S(1)}, u32[]{:S(2)}, u32[]{:S(2)}) collective-permute-start(bf16[64,2048]{1,0:T(8,128)(2,1)S(1)} %add_convert_fusion.5.refs_0_), channel_id=1, source_target_pairs={{0,128},{128,0},{1,129},{129,1},{2,130},{130,2},{3,131},{131,3},{4... | collective-permute-start | bytes 786440 | tf_op jit(solution)/shard_map/ppermute | solution.py:340
  175.3 5.2 %collective-permute-start.22 = (bf16[512,256]{1,0:T(8,128)(2,1)S(1)}, bf16[512,256]{1,0:T(8,128)(2,1)S(1)}, u32[]{:S(2)}, u32[]{:S(2)}) collective-permute-start(bf16[512,256]{1,0:T(8,128)(2,1)S(1)} %add_convert_fusion.4.refs_8_), channel_id=1, source_target_pairs={{0,128},{128,0},{1,129},{129,1},{2,130},{130,2},{3,131},{131,3},{4... | collective-permute-start | bytes 786440 | tf_op jit(solution)/shard_map/ppermute | solution.py:340
  175.3 8.7 %collective-permute-start.15 = (bf16[64,2048]{1,0:T(8,128)(2,1)S(1)}, bf16[64,2048]{1,0:T(8,128)(2,1)S(1)}, u32[]{:S(2)}, u32[]{:S(2)}) collective-permute-start(bf16[64,2048]{1,0:T(8,128)(2,1)S(1)} %collective-permute-done.12.refs_1_), channel_id=1, source_target_pairs={{0,32},{32,0},{64,96},{96,64},{1,33},{33,1},{65,97},{97,65},{2,34}... | collective-permute-start | bytes 786440 | tf_op jit(solution)/shard_map/ppermute | solution.py:55
  178.1 7.6 %collective-permute-start.21 = (bf16[512,256]{1,0:T(8,128)(2,1)S(1)}, bf16[512,256]{1,0:T(8,128)(2,1)S(1)}, u32[]{:S(2)}, u32[]{:S(2)}) collective-permute-start(bf16[512,256]{1,0:T(8,128)(2,1)S(1)} %collective-permute-done.13.refs_9_), channel_id=1, source_target_pairs={{0,96},{96,0},{32,64},{64,32},{1,97},{97,1},{33,65},{65,33},{2,98}... | collective-permute-start | bytes 786440 | tf_op jit(solution)/shard_map/ppermute | solution.py:55
  179.9 5.8 %collective-permute-start.17 = (bf16[64,2048]{1,0:T(8,128)(2,1)S(1)}, bf16[64,2048]{1,0:T(8,128)(2,1)S(1)}, u32[]{:S(2)}, u32[]{:S(2)}) collective-permute-start(bf16[64,2048]{1,0:T(8,128)(2,1)S(1)} %collective-permute-done.12.refs_1_), channel_id=1, source_target_pairs={{0,128},{128,0},{1,129},{129,1},{2,130},{130,2},{3,131},{131,3},{4... | collective-permute-start | bytes 786440 | tf_op jit(solution)/shard_map/ppermute | solution.py:340
  180.0 9.1 %collective-permute-start.23 = (bf16[512,256]{1,0:T(8,128)(2,1)S(1)}, bf16[512,256]{1,0:T(8,128)(2,1)S(1)}, u32[]{:S(2)}, u32[]{:S(2)}) collective-permute-start(bf16[512,256]{1,0:T(8,128)(2,1)S(1)} %collective-permute-done.13.refs_9_), channel_id=1, source_target_pairs={{0,128},{128,0},{1,129},{129,1},{2,130},{130,2},{3,131},{131,3},{4... | collective-permute-start | bytes 786440 | tf_op jit(solution)/shard_map/ppermute | solution.py:340
  180.5 8.6 %collective-permute-start.18 = (bf16[64,2048]{1,0:T(8,128)(2,1)S(1)}, bf16[64,2048]{1,0:T(8,128)(2,1)S(1)}, u32[]{:S(2)}, u32[]{:S(2)}) collective-permute-start(bf16[64,2048]{1,0:T(8,128)(2,1)S(1)} %collective-permute-done.14.refs_2_), channel_id=1, source_target_pairs={{0,128},{128,0},{1,129},{129,1},{2,130},{130,2},{3,131},{131,3},{4... | collective-permute-start | bytes 786440 | tf_op jit(solution)/shard_map/ppermute | solution.py:340
  184.0 5.0 %collective-permute-start.24 = (bf16[512,256]{1,0:T(8,128)(2,1)S(1)}, bf16[512,256]{1,0:T(8,128)(2,1)}, u32[]{:S(2)}, u32[]{:S(2)}) collective-permute-start(bf16[512,256]{1,0:T(8,128)(2,1)S(1)} %collective-permute-done.20.refs_10_), channel_id=1, source_target_pairs={{0,128},{128,0},{1,129},{129,1},{2,130},{130,2},{3,131},{131,3},{4... | collective-permute-start | bytes 786440 | tf_op jit(solution)/shard_map/ppermute | solution.py:340
  185.7 3.4 %collective-permute-start.19 = (bf16[64,2048]{1,0:T(8,128)(2,1)S(1)}, bf16[64,2048]{1,0:T(8,128)(2,1)}, u32[]{:S(2)}, u32[]{:S(2)}) collective-permute-start(bf16[64,2048]{1,0:T(8,128)(2,1)S(1)} %collective-permute-done.15.refs_3_), channel_id=1, source_target_pairs={{0,128},{128,0},{1,129},{129,1},{2,130},{130,2},{3,131},{131,3},{4... | collective-permute-start | bytes 786440 | tf_op jit(solution)/shard_map/ppermute | solution.py:340
  185.7 3.4 %collective-permute-start.25 = (bf16[512,256]{1,0:T(8,128)(2,1)S(1)}, bf16[512,256]{1,0:T(8,128)(2,1)}, u32[]{:S(2)}, u32[]{:S(2)}) collective-permute-start(bf16[512,256]{1,0:T(8,128)(2,1)S(1)} %collective-permute-done.21.refs_11_), channel_id=1, source_target_pairs={{0,128},{128,0},{1,129},{129,1},{2,130},{130,2},{3,131},{131,3},{4... | collective-permute-start | bytes 786440 | tf_op jit(solution)/shard_map/ppermute | solution.py:340

commit v4 on v3

--- a/solution.py
+++ b/solution.py
@@ -53,13 +53,14 @@
     across = [lax.ppermute(part, "ctx", plan[0][1]) for part, plan in zip(parts, plans)]
     side = join(side)
     corner = [lax.ppermute(part, "ctx", plan[0][1]) for part, plan in zip(side, plans)]
+    across, corner = join((across, corner))
     return [tuple(four) for four in zip(parts, side, across, corner)], beside
 
 
 def dispatch_kernel(base, picks, tokens, out_grad, sent, spread, high_ref, low_ref, code_ref):
     exp_count, tok_dev = code_ref.shape
     highs, lows = high_ref.shape[0] // exp_count, low_ref.shape[0] // exp_count
-    rows = spread.shape[0]
+    rows = spread.shape[1]
     slots = rows * pl.num_programs(0) // exp_count
     iota = lax.broadcasted_iota
 
@@ -94,8 +95,9 @@
     repeat = (iota(I32, wide, 0) // slots + at == iota(I32, wide, 1)).astype(BF)
     code = dot(repeat, code_ref[...].astype(BF), ((1,), (0,)))
     slot = (iota(I32, code.shape, 0) % slots + 1).astype(F32)
-    chosen = (code == slot).astype(F32).astype(BF)
-    spread[...] = chosen
+    chosen = (code == slot).astype(F32)
+    spread[...] = chosen.T.astype(BF)
+    chosen = chosen.astype(BF)
     feat = tokens.shape[2]
     sent[:, :feat] = dot(chosen, tokens[0], ((1,), (0,))).astype(BF)
     sent[:, feat:] = dot(chosen, out_grad[0], ((1,), (0,))).astype(BF)
@@ -122,18 +124,18 @@
         ],
         out_specs=[
             pl.BlockSpec((rows, 2 * feat), lambda i: (i, 0)),
-            pl.BlockSpec((rows, tok_dev), lambda i: (i, 0)),
+            pl.BlockSpec((tok_dev, rows), lambda i: (0, i)),
         ],
         out_shape=[
             jax.ShapeDtypeStruct((exp_count * slots, 2 * feat), BF),
-            jax.ShapeDtypeStruct((exp_count * slots, tok_dev), BF),
+            jax.ShapeDtypeStruct((tok_dev, exp_count * slots), BF),
         ],
         scratch_shapes=[
             pltpu.VMEM((exp_count * tok_dev // lows, pick_total), F32),
             pltpu.VMEM((exp_count * lows, pick_total), F32),
             pltpu.VMEM((exp_count, tok_dev), F32),
         ],
-        compiler_params=pltpu.CompilerParams(vmem_limit_bytes=32 * 1024 * 1024),
+        compiler_params=pltpu.CompilerParams(vmem_limit_bytes=60 * 1024 * 1024),
         cost_estimate=pl.CostEstimate(
             flops=4 * exp_count * slots * tok_dev * feat,
             bytes_accessed=4 * exp_count * slots * feat,
@@ -238,21 +240,28 @@
 
 def assemble_kernel(where, *refs):
     out_pieces, in_pieces = refs[:8], refs[8:16]
-    out_ref, in_ref = refs[16], refs[17]
+    out_ref, in_ref, sems = refs[16:]
     core, near, far = where[0], where[1], where[2]
     out_rows, in_rows, in_cols = out_pieces[0].shape[0], in_pieces[0].shape[0], in_pieces[0].shape[1]
+    copies = []
     for k in range(8):
         half = core if k < 4 else 1 - core
         flip_b, flip_a = k % 2, (k // 2) % 2
         a = 1 - near if flip_a else near
         b = 1 - far if flip_b else far
         row = pl.multiple_of(((half * 2 + a) * 2 + b) * out_rows, out_rows)
-        out_ref[pl.ds(row, out_rows), :] = out_pieces[k][...]
+        place = out_ref.at[pl.ds(row, out_rows), :]
+        copies.append(pltpu.make_async_copy(out_pieces[k], place, sems.at[2 * k]))
         a = 1 - far if flip_a else far
         b = 1 - near if flip_b else near
         row = pl.multiple_of((a * 2 + b) * in_rows, in_rows)
         col = pl.multiple_of(half * in_cols, in_cols)
-        in_ref[pl.ds(row, in_rows), pl.ds(col, in_cols)] = in_pieces[k][...]
+        place = in_ref.at[pl.ds(row, in_rows), pl.ds(col, in_cols)]
+        copies.append(pltpu.make_async_copy(in_pieces[k], place, sems.at[2 * k + 1]))
+    for copy in copies:
+        copy.start()
+    for copy in copies:
+        copy.wait()
 
 
 def assemble(where, out_pieces, in_pieces, out_shape, in_shape):
@@ -261,8 +270,9 @@
         assemble_kernel,
         in_specs=[pl.BlockSpec(memory_space=pltpu.SMEM)]
         + [pl.BlockSpec(memory_space=pltpu.VMEM)] * 16,
-        out_specs=[pl.BlockSpec(memory_space=pltpu.VMEM)] * 2,
+        out_specs=[pl.BlockSpec(memory_space=pl.ANY)] * 2,
         out_shape=[jax.ShapeDtypeStruct(out_shape, BF), jax.ShapeDtypeStruct(in_shape, BF)],
+        scratch_shapes=[pltpu.SemaphoreType.DMA((16,))],
         compiler_params=pltpu.CompilerParams(vmem_limit_bytes=24 * 1024 * 1024),
         cost_estimate=pl.CostEstimate(flops=0, bytes_accessed=moved, transcendentals=0),
     )(where, *out_pieces, *in_pieces)
@@ -337,8 +347,8 @@
 
     near, far = bits(ctx_index)
     pieces, gate_grad = reduce_ctx(halves, near, far, gate_grad)
+    token_total = dot(spread, returned, ((1,), (0,))).astype(BF)
     pieces = [four + tuple(lax.ppermute(term, "dp", SWAP) for term in four) for four in pieces]
-    token_total = dot(spread, returned, ((0,), (0,))).astype(BF)
     pieces, token_total = lax.optimization_barrier((pieces, token_total))
     out_total, in_total = assemble(
         jnp.stack((core, near, far)).astype(I32), *pieces, (hid, feat), (feat, hid)

time: 195 us -> 190 us (0.974); the launches traced: 193 us -> 190 us
  local copies, waits for them, and re-layouts: 7.19 us -> 1.41 us
  Pallas kernels: 19.7 us -> 22.3 us
  waiting for transfers between devices: 117 us -> 119 us
    unnamed x13 -> x7, local copies, waits for them, and re-layouts: 5.01 us -> 0.02 us
    all_to_all x2, waiting for transfers between devices: 86 us -> 88.9 us  [swap(): out = lax.all_to_all(out, 'expert', split_axis=0, concat_axis=0, tiled=True)]
    pallas_call x1, Pallas kernels: 3.02 us -> 5.84 us  [dispatch(): pl.pallas_call(dispatch_kernel, grid=(steps,), in_specs=[pl.BlockSpec(mem...]
    ppermute x4, waiting for transfers between devices: 7.6 us -> 5.51 us  [reduce_ctx(): lax.ppermute(part, 'ctx', plan[0][1])]
  transfers between devices with their start and end apart: 28 -> 28, of which waited for: 10 -> 12; matrix products, arithmetic and copies ran while one was open for 6% -> 5% of each run, Pallas kernels for 0% -> 0%
where the time goes in v4:
time: 190 us
  waiting for transfers between devices  119 us (63%)
  starting transfers between devices  37.6 us (20%)
  Pallas kernels  22.3 us (12%)
  other arithmetic  4.67 us (2%)
  matrix products  3.95 us (2%)
    all_to_all x2, waiting for transfers between devices, swap(): out = lax.all_to_all(out, 'expert', split_axis=0, concat_axis=0, tiled=True)  88.9 us
    all_to_all x2, starting transfers between devices, swap(): out = lax.all_to_all(out, 'expert', split_axis=0, concat_axis=0, tiled=True)  18.7 us
    ppermute x3, waiting for transfers between devices, shards(): gate_grad = gate_grad + lax.ppermute(term, 'ctx', ring(ctx_count, step))  9.18 us
    pallas_call x1, Pallas kernels, expert_pass(): pl.pallas_call(pass_kernel, grid=(count // size,), in_specs=[block(feat),...  7.62 us
    ppermute x4, waiting for transfers between devices, reduce_ctx(): lax.ppermute(part, 'ctx', plan[step][1])  6.88 us
    pallas_call x1, Pallas kernels, dispatch(): pl.pallas_call(dispatch_kernel, grid=(steps,), in_specs=[pl.BlockSpec(mem...  5.84 us
    ppermute x2, waiting for transfers between devices, reduce_ctx(): lax.ppermute(part, 'ctx', plan[1][1])  5.72 us
    pallas_call x1, Pallas kernels, outer(): pl.pallas_call(functools.partial(outer_kernel, scale), grid_spec=pltpu.Pr...  5.61 us
  transfers between devices with their start and end apart: 28, of which 12 were waited for; matrix products, arithmetic and copies ran while one was open for 5% of the time, Pallas kernels for 0%

profile of v4, /device:TPU:6, one launch (start us, length us, event | category | flops | bytes accessed | tf_op | source)
XLA Modules:
  0.0 189.9 jit_solution(9376401336434163027)
XLA Ops:
  0.6 5.8 %shard_map.93 = (bf16[512,4096]{1,0:T(8,128)(2,1)}, bf16[128,512]{1,0:T(8,128)(2,1)}) custom-call(s32[1]{0:T(128)} %bitcast.1.base, s32[1,32,1024]{2,1,0:T(8,128)} %picks.1, bf16[1,128,2048]{2,1,0:T(8,128)(2,1)} %tokens.1, bf16[1,128,2048]{2,1,0:T(8,128)(2,1)} %out_grad.1), custom_call_target="tpu_custom_call" | custom-call | flops 536870912 | bytes 4194304 | tf_op jit(solution)/shard_map/pallas_call | solution.py:116
  6.5 11.8 %all-to-all-start = ((bf16[32,16,4096]{2,1,0:T(8,128)(2,1)}), bf16[32,16,4096]{2,1,0:T(8,128)(2,1)}, u32[]{:S(2)}, u32[]{:S(2)}) async-start(bf16[32,16,4096]{2,1,0:T(8,128)(2,1)} %bitcast.31), calls=%async_computation | async-start | bytes 8388608 | tf_op jit(solution)/shard_map/all_to_all | solution.py:299
  18.3 0.6 collective-permute-start
  18.8 2.4 %collective-permute-start.1 = (f32[256]{0:T(256)S(1)}, f32[256]{0:T(256)S(1)}, u32[]{:S(2)}, u32[]{:S(2)}) collective-permute-start(f32[256]{0:T(256)S(1)} %bitcast.41), channel_id=1, source_target_pairs={{0,64},{32,96},{64,0},{96,32},{1,65},{33,97},{65,1},{97,33},{2,66}... | collective-permute-start | bytes 3080 | tf_op jit(solution)/shard_map/ppermute | solution.py:322
  21.2 0.8 dynamic-slice_subtract_fusion
  22.0 0.5 convolution_convert_fusion.2
  22.6 0.6 fusion
  23.3 0.6 collective-permute-done.1
  23.9 2.1 %collective-permute-done.2 = f32[256]{0:T(256)S(1)} collective-permute-done((f32[256]{0:T(256)S(1)}, f32[256]{0:T(256)S(1)}, u32[]{:S(2)}, u32[]{:S(2)}) %collective-permute-start.2) | collective-permute-done | bytes 1056 | tf_op jit(solution)/shard_map/ppermute | solution.py:322
  26.1 0.3 select_reduce_fusion.1
  26.4 0.2 copy.11.gate
  26.6 86.0 %all-to-all-done = bf16[32,16,4096]{2,1,0:T(8,128)(2,1)} async-done(((bf16[32,16,4096]{2,1,0:T(8,128)(2,1)}), bf16[32,16,4096]{2,1,0:T(8,128)(2,1)}, u32[]{:S(2)}, u32[]{:S(2)}) %all-to-all-start) | async-done | bytes 4194336 | tf_op jit(solution)/shard_map/all_to_all | solution.py:299
  112.6 7.6 %shard_map.94 = (bf16[512,2048]{1,0:T(8,128)(2,1)}, bf16[512,512]{1,0:T(8,128)(2,1)S(1)}, bf16[512,512]{1,0:T(8,128)(2,1)S(1)}, f32[512,1]{1,0:T(8,128)S(1)}) custom-call(bf16[512,4096]{1,0:T(8,128)(2,1)} %bitcast.3.rows_in.rows_grad, bf16[512,4096]{1,0:T(8,128)(2,1)} %bitcast.3.rows_in.rows_grad, bf16[2048,512]{1,0:T(8,128)(2,1)S(1)} %bitcast.30, ...), custom_call_target="tpu_custom_call" | custom-call | flops 3221225472 | bytes 10485760 | tf_op jit(solution)/shard_map/pallas_call | solution.py:169
  120.2 5.6 %shard_map.95 = (bf16[256,2048]{1,0:T(8,128)(2,1)}, bf16[2048,256]{1,0:T(8,128)(2,1)}, bf16[256,2048]{1,0:T(8,128)(2,1)S(1)}, bf16[2048,256]{1,0:T(8,128)(2,1)S(1)}) custom-call(s32[1]{0:T(128)} %bitcast.where, bf16[512,4096]{1,0:T(8,128)(2,1)} %bitcast.3.rows_in.rows_grad, bf16[512,4096]{1,0:T(8,128)(2,1)} %bitcast.3.rows_in.rows_grad, ...), custom_call_target="tpu_custom_call" | custom-call | flops 2147483648 | bytes 8388608 | tf_op jit(solution)/shard_map/pallas_call | solution.py:215
  125.8 0.5 collective-permute-start.3
  126.3 6.9 %all-to-all-start.1 = ((bf16[32,16,2048]{2,1,0:T(8,128)(2,1)}), bf16[32,16,2048]{2,1,0:T(8,128)(2,1)}, u32[]{:S(2)}, u32[]{:S(2)}) async-start(bf16[32,16,2048]{2,1,0:T(8,128)(2,1)} %bitcast.17), calls=%async_computation.1 | async-start | bytes 4194304 | tf_op jit(solution)/shard_map/all_to_all | solution.py:299
  133.3 1.5 add_convert_fusion
  134.8 0.9 constant_dynamic-slice_fusion.8
  135.7 0.4 add_convert_fusion.1
  136.2 0.9 collective-permute-start.5
  137.1 1.1 collective-permute-start.6
  138.2 0.1 reduce
  138.4 0.5 select_reduce_fusion
  138.9 2.4 %collective-permute-start.7 = (f32[256]{0:T(256)S(1)}, f32[256]{0:T(256)S(1)}, u32[]{:S(2)}, u32[]{:S(2)}) collective-permute-start(f32[256]{0:T(256)S(1)} %bitcast.50), channel_id=1, source_target_pairs={{0,32},{32,64},{64,96},{96,0},{1,33},{33,65},{65,97},{97,1},{2,34}... | collective-permute-start | bytes 3080 | tf_op jit(solution)/shard_map/ppermute | solution.py:346
  141.2 0.1 collective-permute-start.8
  141.4 1.3 collective-permute-start.9
  142.7 7.2 %collective-permute-done.7 = f32[256]{0:T(256)S(1)} collective-permute-done((f32[256]{0:T(256)S(1)}, f32[256]{0:T(256)S(1)}, u32[]{:S(2)}, u32[]{:S(2)}) %collective-permute-start.7) | collective-permute-done | bytes 1056 | tf_op jit(solution)/shard_map/ppermute | solution.py:346
  149.9 2.0 %collective-permute-done.9 = f32[256]{0:T(256)S(1)} collective-permute-done((f32[256]{0:T(256)S(1)}, f32[256]{0:T(256)S(1)}, u32[]{:S(2)}, u32[]{:S(2)}) %collective-permute-start.9) | collective-permute-done | bytes 1056 | tf_op jit(solution)/shard_map/ppermute | solution.py:346
  151.9 0.6 add_add_fusion
  152.8 1.2 collective-permute-start.10
  154.1 6.9 %collective-permute-done.10 = bf16[64,2048]{1,0:T(8,128)(2,1)S(1)} collective-permute-done((bf16[64,2048]{1,0:T(8,128)(2,1)S(1)}, bf16[64,2048]{1,0:T(8,128)(2,1)S(1)}, u32[]{:S(2)}, u32[]{:S(2)}) %collective-permute-start.10) | collective-permute-done | bytes 262176 | tf_op jit(solution)/shard_map/ppermute | solution.py:48
  161.1 1.8 collective-permute-start.12
  162.9 2.0 %collective-permute-start.14 = (bf16[64,2048]{1,0:T(8,128)(2,1)S(1)}, bf16[64,2048]{1,0:T(8,128)(2,1)S(1)}, u32[]{:S(2)}, u32[]{:S(2)}) collective-permute-start(bf16[64,2048]{1,0:T(8,128)(2,1)S(1)} %add_convert_fusion.5.refs_0_), channel_id=1, source_target_pairs={{0,32},{32,0},{64,96},{96,64},{1,33},{33,1},{65,97},{97,65},{2,34}... | collective-permute-start | bytes 786440 | tf_op jit(solution)/shard_map/ppermute | solution.py:53
  164.9 1.5 collective-permute-start.15
  166.4 5.2 %collective-permute-done.12.refs_1_ = bf16[64,2048]{1,0:T(8,128)(2,1)S(1)} collective-permute-done((bf16[64,2048]{1,0:T(8,128)(2,1)S(1)}, bf16[64,2048]{1,0:T(8,128)(2,1)S(1)}, u32[]{:S(2)}, u32[]{:S(2)}) %collective-permute-start.12) | collective-permute-done | bytes 262176 | tf_op jit(solution)/shard_map/ppermute | solution.py:52
  171.6 0.5 collective-permute-done.13.refs_9_
  172.2 1.5 collective-permute-start.17
  173.7 3.1 %collective-permute-done.14.refs_2_ = bf16[64,2048]{1,0:T(8,128)(2,1)S(1)} collective-permute-done((bf16[64,2048]{1,0:T(8,128)(2,1)S(1)}, bf16[64,2048]{1,0:T(8,128)(2,1)S(1)}, u32[]{:S(2)}, u32[]{:S(2)}) %collective-permute-start.14) | collective-permute-done | bytes 262176 | tf_op jit(solution)/shard_map/ppermute | solution.py:53
  176.8 0.5 collective-permute-start.19
  177.3 2.2 %collective-permute-done.16.refs_3_ = bf16[64,2048]{1,0:T(8,128)(2,1)S(1)} collective-permute-done((bf16[64,2048]{1,0:T(8,128)(2,1)S(1)}, bf16[64,2048]{1,0:T(8,128)(2,1)S(1)}, u32[]{:S(2)}, u32[]{:S(2)}) %collective-permute-start.16) | collective-permute-done | bytes 262176 | tf_op jit(solution)/shard_map/ppermute | solution.py:55
  179.6 0.2 collective-permute-done.17.refs_11_
  179.7 0.3 collective-permute-start.20
  180.1 0.2 collective-permute-start.21
  180.3 0.3 collective-permute-start.24
  180.6 0.2 collective-permute-start.25
  180.8 2.8 %all-to-all-done.1 = bf16[32,16,2048]{2,1,0:T(8,128)(2,1)} async-done(((bf16[32,16,2048]{2,1,0:T(8,128)(2,1)}), bf16[32,16,2048]{2,1,0:T(8,128)(2,1)}, u32[]{:S(2)}, u32[]{:S(2)}) %all-to-all-start.1) | async-done | bytes 2097184 | tf_op jit(solution)/shard_map/all_to_all | solution.py:299
  183.6 2.9 %convolution_convert_fusion = bf16[128,2048]{1,0:T(8,128)(2,1)} fusion(bf16[128,512]{1,0:T(8,128)(2,1)S(1)} %copy-done.1, bf16[512,2048]{1,0:T(8,128)(2,1)} %bitcast.18), kind=kOutput, calls=%fused_computation | convolution fusion | flops 268697600 | bytes 2752512 | tf_op jit(solution)/shard_map/dot_general | solution.py:19
  186.5 3.3 %shard_map.96 = (bf16[512,2048]{1,0:T(8,128)(2,1)}, bf16[2048,512]{1,0:T(8,128)(2,1)}) custom-call(s32[3]{0:T(128)S(1)} %pad_add_fusion.where, bf16[64,2048]{1,0:T(8,128)(2,1)S(1)} %add_convert_fusion.5.refs_0_, bf16[64,2048]{1,0:T(8,128)(2,1)S(1)} %collective-permute-done.12.refs_1_, bf16[64,2048]{1,0:T(8,128)(2,1)S(1)} %collective-permute-done.14.refs_2_, ...), custom_call_target="tpu_custom_call" | custom-call | bytes 8388608 | tf_op jit(solution)/shard_map/pallas_call | solution.py:269
  (49 shorter events, 1.0 us)
Async XLA Ops:
  6.5 11.8 %copy-start.2 = (f32[1,1,256]{2,1,0:T(1,128)S(1)}, f32[1,1,256]{2,1,0:T(1,128)}, u32[]{:S(2)}) copy-start(f32[1,1,256]{2,1,0:T(1,128)} %param.11) | copy-start | bytes 3076
  6.5 106.1 %copy-start = (bf16[1,2048,512]{2,1,0:T(8,128)(2,1)S(1)}, bf16[1,2048,512]{2,1,0:T(8,128)(2,1)}, u32[]{:S(2)}) copy-start(bf16[1,2048,512]{2,1,0:T(8,128)(2,1)} %param.8) | copy-start | bytes 6291460
  6.5 106.1 %all-to-all-start = ((bf16[32,16,4096]{2,1,0:T(8,128)(2,1)}), bf16[32,16,4096]{2,1,0:T(8,128)(2,1)}, u32[]{:S(2)}, u32[]{:S(2)}) async-start(bf16[32,16,4096]{2,1,0:T(8,128)(2,1)} %bitcast.31), calls=%async_computation | async-start | bytes 8388608 | tf_op jit(solution)/shard_map/all_to_all | solution.py:299
  18.3 5.0 %collective-permute-start = (f32[256]{0:T(256)S(1)}, f32[256]{0:T(256)S(1)}, u32[]{:S(2)}, u32[]{:S(2)}) collective-permute-start(f32[256]{0:T(256)S(1)} %bitcast.40), channel_id=1, source_target_pairs={{0,32},{32,64},{64,96},{96,0},{1,33},{33,65},{65,97},{97,1},{2,34}... | collective-permute-start | bytes 3080 | tf_op jit(solution)/shard_map/ppermute | solution.py:322
  18.8 5.1 %collective-permute-start.1 = (f32[256]{0:T(256)S(1)}, f32[256]{0:T(256)S(1)}, u32[]{:S(2)}, u32[]{:S(2)}) collective-permute-start(f32[256]{0:T(256)S(1)} %bitcast.41), channel_id=1, source_target_pairs={{0,64},{32,96},{64,0},{96,32},{1,65},{33,97},{65,1},{97,33},{2,66}... | collective-permute-start | bytes 3080 | tf_op jit(solution)/shard_map/ppermute | solution.py:322
  21.2 4.8 %collective-permute-start.2 = (f32[256]{0:T(256)S(1)}, f32[256]{0:T(256)S(1)}, u32[]{:S(2)}, u32[]{:S(2)}) collective-permute-start(f32[256]{0:T(256)S(1)} %bitcast.42), channel_id=1, source_target_pairs={{0,96},{32,0},{64,32},{96,64},{1,97},{33,1},{65,33},{97,65},{2,98}... | collective-permute-start | bytes 3080 | tf_op jit(solution)/shard_map/ppermute | solution.py:322
  125.8 7.5 %collective-permute-start.4 = (bf16[2048,256]{1,0:T(8,128)(2,1)}, bf16[2048,256]{1,0:T(8,128)(2,1)}, u32[]{:S(2)}, u32[]{:S(2)}) collective-permute-start(bf16[2048,256]{1,0:T(8,128)(2,1)} %get-tuple-element.66), channel_id=1, source_target_pairs={{0,128},{128,0},{1,129},{129,1},{2,130},{130,2},{3,131},{131,3},{4... | collective-permute-start | bytes 3145736 | tf_op jit(solution)/shard_map/ppermute | solution.py:334
  125.8 9.8 %collective-permute-start.3 = (bf16[256,2048]{1,0:T(8,128)(2,1)}, bf16[256,2048]{1,0:T(8,128)(2,1)S(1)}, u32[]{:S(2)}, u32[]{:S(2)}) collective-permute-start(bf16[256,2048]{1,0:T(8,128)(2,1)} %get-tuple-element.64), channel_id=1, source_target_pairs={{0,128},{128,0},{1,129},{129,1},{2,130},{130,2},{3,131},{131,3},{4... | collective-permute-start | bytes 3145736 | tf_op jit(solution)/shard_map/ppermute | solution.py:334
  126.3 57.3 %all-to-all-start.1 = ((bf16[32,16,2048]{2,1,0:T(8,128)(2,1)}), bf16[32,16,2048]{2,1,0:T(8,128)(2,1)}, u32[]{:S(2)}, u32[]{:S(2)}) async-start(bf16[32,16,2048]{2,1,0:T(8,128)(2,1)} %bitcast.17), calls=%async_computation.1 | async-start | bytes 4194304 | tf_op jit(solution)/shard_map/all_to_all | solution.py:299
  136.2 16.3 %collective-permute-start.5 = (bf16[128,2048]{1,0:T(8,128)(2,1)S(1)}, bf16[128,2048]{1,0:T(8,128)(2,1)S(1)}, u32[]{:S(2)}, u32[]{:S(2)}) collective-permute-start(bf16[128,2048]{1,0:T(8,128)(2,1)S(1)} %get-tuple-element.67), channel_id=1, source_target_pairs={{0,32},{32,0},{64,96},{96,64},{1,33},{33,1},{65,97},{97,65},{2,34}... | collective-permute-start | bytes 1572872 | tf_op jit(solution)/shard_map/ppermute | solution.py:48
  137.1 15.3 %collective-permute-start.6 = (bf16[1024,256]{1,0:T(8,128)(2,1)}, bf16[1024,256]{1,0:T(8,128)(2,1)S(1)}, u32[]{:S(2)}, u32[]{:S(2)}) collective-permute-start(bf16[1024,256]{1,0:T(8,128)(2,1)} %get-tuple-element.68), channel_id=1, source_target_pairs={{0,96},{96,0},{32,64},{64,32},{1,97},{97,1},{33,65},{65,33},{2,98}... | collective-permute-start | bytes 1572872 | tf_op jit(solution)/shard_map/ppermute | solution.py:48
  138.9 11.0 %collective-permute-start.7 = (f32[256]{0:T(256)S(1)}, f32[256]{0:T(256)S(1)}, u32[]{:S(2)}, u32[]{:S(2)}) collective-permute-start(f32[256]{0:T(256)S(1)} %bitcast.50), channel_id=1, source_target_pairs={{0,32},{32,64},{64,96},{96,0},{1,33},{33,65},{65,97},{97,1},{2,34}... | collective-permute-start | bytes 3080 | tf_op jit(solution)/shard_map/ppermute | solution.py:346
  141.2 8.7 %collective-permute-start.8 = (f32[256]{0:T(256)S(1)}, f32[256]{0:T(256)S(1)}, u32[]{:S(2)}, u32[]{:S(2)}) collective-permute-start(f32[256]{0:T(256)S(1)} %bitcast.49), channel_id=1, source_target_pairs={{0,64},{32,96},{64,0},{96,32},{1,65},{33,97},{65,1},{97,33},{2,66}... | collective-permute-start | bytes 3080 | tf_op jit(solution)/shard_map/ppermute | solution.py:346
  141.4 10.5 %collective-permute-start.9 = (f32[256]{0:T(256)S(1)}, f32[256]{0:T(256)S(1)}, u32[]{:S(2)}, u32[]{:S(2)}) collective-permute-start(f32[256]{0:T(256)S(1)} %bitcast.48), channel_id=1, source_target_pairs={{0,96},{32,0},{64,32},{96,64},{1,97},{33,1},{65,33},{97,65},{2,98}... | collective-permute-start | bytes 3080 | tf_op jit(solution)/shard_map/ppermute | solution.py:346
  152.6 31.0 %copy-start.1 = (bf16[128,512]{1,0:T(8,128)(2,1)S(1)}, bf16[128,512]{1,0:T(8,128)(2,1)}, u32[]{:S(2)}) copy-start(bf16[128,512]{1,0:T(8,128)(2,1)} %get-tuple-element.93) | copy-start | bytes 393220
  152.8 8.1 %collective-permute-start.10 = (bf16[64,2048]{1,0:T(8,128)(2,1)S(1)}, bf16[64,2048]{1,0:T(8,128)(2,1)S(1)}, u32[]{:S(2)}, u32[]{:S(2)}) collective-permute-start(bf16[64,2048]{1,0:T(8,128)(2,1)S(1)} %get-tuple-element.76), channel_id=1, source_target_pairs={{0,96},{96,0},{32,64},{64,32},{1,97},{97,1},{33,65},{65,33},{2,98}... | collective-permute-start | bytes 786440 | tf_op jit(solution)/shard_map/ppermute | solution.py:48
  154.1 6.9 %collective-permute-start.11 = (bf16[512,256]{1,0:T(8,128)(2,1)S(1)}, bf16[512,256]{1,0:T(8,128)(2,1)S(1)}, u32[]{:S(2)}, u32[]{:S(2)}) collective-permute-start(bf16[512,256]{1,0:T(8,128)(2,1)S(1)} %get-tuple-element.77), channel_id=1, source_target_pairs={{0,32},{32,0},{64,96},{96,64},{1,33},{33,1},{65,97},{97,65},{2,34}... | collective-permute-start | bytes 786440 | tf_op jit(solution)/shard_map/ppermute | solution.py:48
  161.1 10.5 %collective-permute-start.12 = (bf16[64,2048]{1,0:T(8,128)(2,1)S(1)}, bf16[64,2048]{1,0:T(8,128)(2,1)S(1)}, u32[]{:S(2)}, u32[]{:S(2)}) collective-permute-start(bf16[64,2048]{1,0:T(8,128)(2,1)S(1)} %add_convert_fusion.5.refs_0_), channel_id=1, source_target_pairs={{0,96},{96,0},{32,64},{64,32},{1,97},{97,1},{33,65},{65,33},{2,98}... | collective-permute-start | bytes 786440 | tf_op jit(solution)/shard_map/ppermute | solution.py:52
  162.9 9.2 %collective-permute-start.13 = (bf16[512,256]{1,0:T(8,128)(2,1)S(1)}, bf16[512,256]{1,0:T(8,128)(2,1)S(1)}, u32[]{:S(2)}, u32[]{:S(2)}) collective-permute-start(bf16[512,256]{1,0:T(8,128)(2,1)S(1)} %add_convert_fusion.4.refs_8_), channel_id=1, source_target_pairs={{0,32},{32,0},{64,96},{96,64},{1,33},{33,1},{65,97},{97,65},{2,34}... | collective-permute-start | bytes 786440 | tf_op jit(solution)/shard_map/ppermute | solution.py:52
  162.9 13.8 %collective-permute-start.14 = (bf16[64,2048]{1,0:T(8,128)(2,1)S(1)}, bf16[64,2048]{1,0:T(8,128)(2,1)S(1)}, u32[]{:S(2)}, u32[]{:S(2)}) collective-permute-start(bf16[64,2048]{1,0:T(8,128)(2,1)S(1)} %add_convert_fusion.5.refs_0_), channel_id=1, source_target_pairs={{0,32},{32,0},{64,96},{96,64},{1,33},{33,1},{65,97},{97,65},{2,34}... | collective-permute-start | bytes 786440 | tf_op jit(solution)/shard_map/ppermute | solution.py:53
  164.9 11.8 %collective-permute-start.15 = (bf16[512,256]{1,0:T(8,128)(2,1)S(1)}, bf16[512,256]{1,0:T(8,128)(2,1)S(1)}, u32[]{:S(2)}, u32[]{:S(2)}) collective-permute-start(bf16[512,256]{1,0:T(8,128)(2,1)S(1)} %add_convert_fusion.4.refs_8_), channel_id=1, source_target_pairs={{0,96},{96,0},{32,64},{64,32},{1,97},{97,1},{33,65},{65,33},{2,98}... | collective-permute-start | bytes 786440 | tf_op jit(solution)/shard_map/ppermute | solution.py:53
  172.2 7.4 %collective-permute-start.16 = (bf16[64,2048]{1,0:T(8,128)(2,1)S(1)}, bf16[64,2048]{1,0:T(8,128)(2,1)S(1)}, u32[]{:S(2)}, u32[]{:S(2)}) collective-permute-start(bf16[64,2048]{1,0:T(8,128)(2,1)S(1)} %collective-permute-done.12.refs_1_), channel_id=1, source_target_pairs={{0,32},{32,0},{64,96},{96,64},{1,33},{33,1},{65,97},{97,65},{2,34}... | collective-permute-start | bytes 786440 | tf_op jit(solution)/shard_map/ppermute | solution.py:55
  172.2 7.6 %collective-permute-start.17 = (bf16[512,256]{1,0:T(8,128)(2,1)S(1)}, bf16[512,256]{1,0:T(8,128)(2,1)S(1)}, u32[]{:S(2)}, u32[]{:S(2)}) collective-permute-start(bf16[512,256]{1,0:T(8,128)(2,1)S(1)} %collective-permute-done.13.refs_9_), channel_id=1, source_target_pairs={{0,96},{96,0},{32,64},{64,32},{1,97},{97,1},{33,65},{65,33},{2,98}... | collective-permute-start | bytes 786440 | tf_op jit(solution)/shard_map/ppermute | solution.py:55
  173.7 6.4 %collective-permute-start.18 = (bf16[64,2048]{1,0:T(8,128)(2,1)S(1)}, bf16[64,2048]{1,0:T(8,128)(2,1)S(1)}, u32[]{:S(2)}, u32[]{:S(2)}) collective-permute-start(bf16[64,2048]{1,0:T(8,128)(2,1)S(1)} %add_convert_fusion.5.refs_0_), channel_id=1, source_target_pairs={{0,128},{128,0},{1,129},{129,1},{2,130},{130,2},{3,131},{131,3},{4... | collective-permute-start | bytes 786440 | tf_op jit(solution)/shard_map/ppermute | solution.py:351
  176.8 3.5 %collective-permute-start.22 = (bf16[512,256]{1,0:T(8,128)(2,1)S(1)}, bf16[512,256]{1,0:T(8,128)(2,1)S(1)}, u32[]{:S(2)}, u32[]{:S(2)}) collective-permute-start(bf16[512,256]{1,0:T(8,128)(2,1)S(1)} %add_convert_fusion.4.refs_8_), channel_id=1, source_target_pairs={{0,128},{128,0},{1,129},{129,1},{2,130},{130,2},{3,131},{131,3},{4... | collective-permute-start | bytes 786440 | tf_op jit(solution)/shard_map/ppermute | solution.py:351
  176.8 3.8 %collective-permute-start.19 = (bf16[64,2048]{1,0:T(8,128)(2,1)S(1)}, bf16[64,2048]{1,0:T(8,128)(2,1)S(1)}, u32[]{:S(2)}, u32[]{:S(2)}) collective-permute-start(bf16[64,2048]{1,0:T(8,128)(2,1)S(1)} %collective-permute-done.12.refs_1_), channel_id=1, source_target_pairs={{0,128},{128,0},{1,129},{129,1},{2,130},{130,2},{3,131},{131,3},{4... | collective-permute-start | bytes 786440 | tf_op jit(solution)/shard_map/ppermute | solution.py:351
  179.6 6.9 %collective-permute-start.23 = (bf16[512,256]{1,0:T(8,128)(2,1)S(1)}, bf16[512,256]{1,0:T(8,128)(2,1)S(1)}, u32[]{:S(2)}, u32[]{:S(2)}) collective-permute-start(bf16[512,256]{1,0:T(8,128)(2,1)S(1)} %collective-permute-done.13.refs_9_), channel_id=1, source_target_pairs={{0,128},{128,0},{1,129},{129,1},{2,130},{130,2},{3,131},{131,3},{4... | collective-permute-start | bytes 786440 | tf_op jit(solution)/shard_map/ppermute | solution.py:351
  179.7 6.7 %collective-permute-start.20 = (bf16[64,2048]{1,0:T(8,128)(2,1)S(1)}, bf16[64,2048]{1,0:T(8,128)(2,1)S(1)}, u32[]{:S(2)}, u32[]{:S(2)}) collective-permute-start(bf16[64,2048]{1,0:T(8,128)(2,1)S(1)} %collective-permute-done.14.refs_2_), channel_id=1, source_target_pairs={{0,128},{128,0},{1,129},{129,1},{2,130},{130,2},{3,131},{131,3},{4... | collective-permute-start | bytes 786440 | tf_op jit(solution)/shard_map/ppermute | solution.py:351
  180.1 6.4 %collective-permute-start.21 = (bf16[64,2048]{1,0:T(8,128)(2,1)S(1)}, bf16[64,2048]{1,0:T(8,128)(2,1)}, u32[]{:S(2)}, u32[]{:S(2)}) collective-permute-start(bf16[64,2048]{1,0:T(8,128)(2,1)S(1)} %collective-permute-done.16.refs_3_), channel_id=1, source_target_pairs={{0,128},{128,0},{1,129},{129,1},{2,130},{130,2},{3,131},{131,3},{4... | collective-permute-start | bytes 786440 | tf_op jit(solution)/shard_map/ppermute | solution.py:351
  180.3 6.2 %collective-permute-start.24 = (bf16[512,256]{1,0:T(8,128)(2,1)S(1)}, bf16[512,256]{1,0:T(8,128)(2,1)}, u32[]{:S(2)}, u32[]{:S(2)}) collective-permute-start(bf16[512,256]{1,0:T(8,128)(2,1)S(1)} %collective-permute-done.15.refs_10_), channel_id=1, source_target_pairs={{0,128},{128,0},{1,129},{129,1},{2,130},{130,2},{3,131},{131,3},{4... | collective-permute-start | bytes 786440 | tf_op jit(solution)/shard_map/ppermute | solution.py:351
  180.6 5.9 %collective-permute-start.25 = (bf16[512,256]{1,0:T(8,128)(2,1)S(1)}, bf16[512,256]{1,0:T(8,128)(2,1)}, u32[]{:S(2)}, u32[]{:S(2)}) collective-permute-start(bf16[512,256]{1,0:T(8,128)(2,1)S(1)} %collective-permute-done.17.refs_11_), channel_id=1, source_target_pairs={{0,128},{128,0},{1,129},{129,1},{2,130},{130,2},{3,131},{131,3},{4... | collective-permute-start | bytes 786440 | tf_op jit(solution)/shard_map/ppermute | solution.py:351

commit v5 on v4

--- a/solution.py
+++ b/solution.py
@@ -144,98 +144,107 @@
     )(jnp.reshape(base, (1,)).astype(I32), picks, tokens, out_grad)
 
 
-def pass_kernel(rows_in, rows_grad, weight_in, weight_out, gate, grads, pre, gated, gate_slot):
-    pre_act = dot(rows_in[...], weight_in[...], ((1,), (0,)))
-    back = dot(rows_grad[...], weight_out[...], ((1,), (1,)))
-    sig = 1.0 / (1.0 + jnp.exp(-pre_act))
-    activation = (pre_act * sig).astype(BF).astype(F32)
-    pre_grad = (gate[...] * back * (sig * (1.0 + pre_act * (1.0 - sig)))).astype(BF)
-    gate_slot[...] = jnp.sum(activation * back, axis=1, keepdims=True)
-    gated[...] = (gate[...] * activation).astype(BF)
-    pre[...] = pre_grad
-    grads[...] = dot(pre_grad, weight_in[...], ((1,), (1,))).astype(BF)
-
-
-def expert_pass(rows, weight_in, weight_out, gate):
+def expert_kernel(scale, core, gate, in_hbm, out_hbm, rows, gate_slot, *refs):
+    outs, refs = refs[:5], refs[5:]
+    weight_in, in_turned, weight_out, out_turned, held = refs[:5]
+    grads, out_theirs, in_theirs, out_mine, in_mine, pre, gated, in_sems, out_sems = refs[5:]
+    count, feat = grads.shape
+    hid = pre.shape[1]
+    chunks = 2
+    size = count // chunks
+    copy_of = pltpu.make_async_copy
+
+    def chunk(i, part):
+        at = (pl.ds(i * size, size), pl.ds(part * feat, feat))
+        return copy_of(rows.at[at], held.at[at], in_sems.at[2 * i + part])
+
+    loads = [
+        copy_of(out_hbm, weight_out, in_sems.at[2 * chunks]),
+        copy_of(in_hbm, weight_in, in_sems.at[2 * chunks + 1]),
+        chunk(0, 0),
+        chunk(0, 1),
+        chunk(1, 0),
+        chunk(1, 1),
+    ]
+    for load in loads:
+        load.start()
+    sent = []
+
+    def send(source, target):
+        sent.append(copy_of(source, target, out_sems.at[len(sent)]))
+        sent[-1].start()
+
+    lanes = 128
+    wide = jnp.broadcast_to(gate[...], (lanes, count)).T
+    wide = jnp.concatenate([wide] * (hid // lanes), axis=1)
+    loads[0].wait()
+    out_turned[...] = weight_out[...].T
+    loads[1].wait()
+    in_turned[...] = weight_in[...].T
+    for i in range(chunks):
+        at = slice(i * size, (i + 1) * size)
+        loads[2 + 2 * i].wait()
+        pre_act = dot(held[at, :feat], weight_in[...], ((1,), (0,)))
+        loads[3 + 2 * i].wait()
+        back = dot(held[at, feat:], out_turned[...], ((1,), (0,)))
+        sig = 1.0 / (1.0 + jnp.exp(-pre_act))
+        activation = (pre_act * sig).astype(BF).astype(F32)
+        terms = activation * back
+        terms = sum(terms[:, k : k + lanes] for k in range(0, hid, lanes))
+        gate_slot[:, at] = jnp.sum(terms.T, axis=0, keepdims=True)
+        gated[at, :] = (wide[at, :] * activation).astype(BF)
+        pre_grad = (wide[at, :] * back * (sig * (1.0 + pre_act * (1.0 - sig)))).astype(BF)
+        pre[at, :] = pre_grad
+        grads[at, :] = dot(pre_grad, in_turned[...], ((1,), (0,))).astype(BF)
+        place = pl.ds(i * size, size)
+        send(grads.at[place, :], outs[0].at[place, :])
+
+    def theirs_first(ref):
+        low, high = ref[:, : hid // 2], ref[:, hid // 2 :]
+        first = core[0] == 0
+        return jnp.concatenate((jnp.where(first, high, low), jnp.where(first, low, high)), axis=1)
+
+    gated_pair, pre_pair = theirs_first(gated), theirs_first(pre)
+    width = 512
+    for first in range(0, feat, width):
+        at = slice(first, first + width)
+        grad_at = slice(feat + first, feat + first + width)
+        out = (dot(gated_pair, held[:, grad_at], ((0,), (0,))) * scale).astype(BF)
+        out_theirs[:, at], out_mine[:, at] = out[: hid // 2], out[hid // 2 :]
+        inn = (dot(held[:, at], pre_pair, ((0,), (0,))) * scale).astype(BF)
+        in_theirs[at, :], in_mine[at, :] = inn[:, : hid // 2], inn[:, hid // 2 :]
+        place = pl.ds(first, width)
+        send(out_theirs.at[:, place], outs[1].at[:, place])
+        send(in_theirs.at[place, :], outs[2].at[place, :])
+        send(out_mine.at[:, place], outs[3].at[:, place])
+        send(in_mine.at[place, :], outs[4].at[place, :])
+    for copy in sent:
+        copy.wait()
+
+
+def expert_pass(rows, weight_in, weight_out, gate, core, scale):
     count, feat, hid = rows.shape[0], weight_in.shape[0], weight_in.shape[1]
-    size = min(256, count)
-
-    def block(cols, at=0):
-        return pl.BlockSpec((size, cols), lambda i: (i, at))
-
-    def whole(shape):
-        return pl.BlockSpec(shape, lambda i: (0, 0))
-
-    return pl.pallas_call(
-        pass_kernel,
-        grid=(count // size,),
-        in_specs=[
-            block(feat),
-            block(feat, 1),
-            whole((feat, hid)),
-            whole((hid, feat)),
-            block(1),
-        ],
-        out_specs=[block(feat), block(hid), block(hid), block(1)],
-        out_shape=[
-            jax.ShapeDtypeStruct((count, feat), BF),
-            jax.ShapeDtypeStruct((count, hid), BF),
-            jax.ShapeDtypeStruct((count, hid), BF),
-            jax.ShapeDtypeStruct((count, 1), F32),
-        ],
-        compiler_params=pltpu.CompilerParams(vmem_limit_bytes=48 * 1024 * 1024),
+    vmem = pl.BlockSpec(memory_space=pltpu.VMEM)
+    anywhere = pl.BlockSpec(memory_space=pl.ANY)
+    shapes = [(count, feat)] + [(hid // 2, feat), (feat, hid // 2)] * 2
+    held = [(feat, hid), (hid, feat), (hid, feat), (feat, hid), rows.shape]
+    held += shapes + [(count, hid)] * 2
+    gate_slot, grads, *parts = pl.pallas_call(
+        functools.partial(expert_kernel, scale),
+        in_specs=[pl.BlockSpec(memory_space=pltpu.SMEM), vmem] + [anywhere] * 3,
+        out_specs=[vmem] + [anywhere] * 5,
+        out_shape=[jax.ShapeDtypeStruct((1, count), F32)]
+        + [jax.ShapeDtypeStruct(shape, BF) for shape in shapes],
+        scratch_shapes=[pltpu.VMEM(shape, BF) for shape in held]
+        + [pltpu.SemaphoreType.DMA((6,)), pltpu.SemaphoreType.DMA((18,))],
+        compiler_params=pltpu.CompilerParams(vmem_limit_bytes=58 * 1024 * 1024),
         cost_estimate=pl.CostEstimate(
-            flops=6 * count * feat * hid,
-            bytes_accessed=2 * (3 * count * feat + 2 * feat * hid),
+            flops=10 * count * feat * hid,
+            bytes_accessed=4 * (count * feat + feat * hid),
             transcendentals=count * hid,
         ),
-    )(rows, rows, weight_in, weight_out, gate)
-
-
-def outer_kernel(scale, where, rows_in, rows_grad, pre_a, pre_b, gated_a, gated_b, *refs):
-    half = pre_a.shape[1]
-    gated = jnp.concatenate((gated_a[...], gated_b[...]), axis=1)
-    pre = jnp.concatenate((pre_a[...], pre_b[...]), axis=1)
-    out = (dot(gated, rows_grad[...], ((0,), (0,))) * scale).astype(BF)
-    inn = (dot(rows_in[...], pre, ((0,), (0,))) * scale).astype(BF)
-    refs[0][...], refs[2][...] = out[:half], out[half:]
-    refs[1][...], refs[3][...] = inn[:, :half], inn[:, half:]
-
-
-def outer(rows, pre, gated, core, scale):
-    count, feat, hid = rows.shape[0], rows.shape[1] // 2, pre.shape[1] // 2
-    steps = 4
-    size = feat // steps
-    out_block = pl.BlockSpec((hid, size), lambda i, at: (0, i))
-    in_block = pl.BlockSpec((size, hid), lambda i, at: (i, 0))
-    theirs = pl.BlockSpec((count, hid), lambda i, at: (0, 1 - at[0]))
-    mine = pl.BlockSpec((count, hid), lambda i, at: (0, at[0]))
-    out_type = jax.ShapeDtypeStruct((hid, feat), BF)
-    in_type = jax.ShapeDtypeStruct((feat, hid), BF)
-    parts = pl.pallas_call(
-        functools.partial(outer_kernel, scale),
-        grid_spec=pltpu.PrefetchScalarGridSpec(
-            num_scalar_prefetch=1,
-            grid=(steps,),
-            in_specs=[
-                pl.BlockSpec((count, size), lambda i, at: (0, i)),
-                pl.BlockSpec((count, size), lambda i, at: (0, i + steps)),
-                theirs,
-                mine,
-                theirs,
-                mine,
-            ],
-            out_specs=[out_block, in_block] * 2,
-        ),
-        out_shape=[out_type, in_type] * 2,
-        compiler_params=pltpu.CompilerParams(vmem_limit_bytes=48 * 1024 * 1024),
-        cost_estimate=pl.CostEstimate(
-            flops=8 * count * feat * hid,
-            bytes_accessed=4 * (count * feat + 2 * feat * hid),
-            transcendentals=0,
-        ),
-    )(jnp.reshape(core, (1,)).astype(I32), rows, rows, pre, pre, gated, gated)
-    return parts[:2], parts[2:]
+    )(jnp.reshape(core, (1,)).astype(I32), gate, weight_in, weight_out, rows)
+    return grads, gate_slot, parts[:2], parts[2:]
 
 
 def assemble_kernel(where, *refs):
@@ -327,16 +336,17 @@
 
     place = jnp.where(inside, block * slots + rank_pick, -1)
     at_slot = place[:, None] == jnp.arange(exp_count * slots, dtype=I32)[None, :]
-    slot_gate = jnp.sum(jnp.where(at_slot, gate_all[:, None], 0.0), axis=0)[:, None]
-
-    row_grads, pre_grad, gated, gate_slot = expert_pass(arrived, w_in[0], w_out[0], slot_gate)
-    theirs, mine = outer(arrived, pre_grad, gated, core, grad_scale)
+    slot_gate = jnp.sum(jnp.where(at_slot, gate_all[:, None], 0.0), axis=0)[None, :]
+
+    row_grads, gate_slot, theirs, mine = expert_pass(
+        arrived, w_in[0], w_out[0], slot_gate, core, grad_scale
+    )
     got = [lax.ppermute(part, "dp", SWAP) for part in theirs]
     row_grads, _ = lax.optimization_barrier((row_grads, theirs))
     returned = swap(row_grads)
     halves = [(a.astype(F32) + b.astype(F32)).astype(BF) for a, b in zip(mine, got)]
 
-    gate_pick = jnp.sum(jnp.where(at_slot, gate_slot[:, 0][None, :], 0.0), axis=1)
+    gate_pick = jnp.sum(jnp.where(at_slot, gate_slot, 0.0), axis=1)
     gate_rows = gate_pick.reshape(ctx_count, share)
     gate_grad = lax.dynamic_index_in_dim(gate_rows, ctx_index, 0, keepdims=False)
     for step in range(1, ctx_count):

time: 190 us -> 189 us (level)
    pallas_call x2 -> x1, Pallas kernels: 13.2 us -> 11.8 us  [expert_pass(): pl.pallas_call(functools.partial(expert_kernel, scale), in_specs=[pl.Bloc...]
  transfers between devices with their start and end apart: 28 -> 28, of which waited for: 12 -> 11; matrix products, arithmetic and copies ran while one was open for 5% -> 4% of each run, Pallas kernels for 0% -> 0%
where the time goes in v5:
time: 189 us
  waiting for transfers between devices  120 us (63%)
  starting transfers between devices  37.7 us (20%)
  Pallas kernels  20.9 us (11%)
  matrix products  3.95 us (2%)
  other arithmetic  3.87 us (2%)
    all_to_all x2, waiting for transfers between devices, swap(): out = lax.all_to_all(out, 'expert', split_axis=0, concat_axis=0, tiled=True)  89.3 us
    all_to_all x2, starting transfers between devices, swap(): out = lax.all_to_all(out, 'expert', split_axis=0, concat_axis=0, tiled=True)  18.8 us
    pallas_call x1, Pallas kernels, expert_pass(): pl.pallas_call(functools.partial(expert_kernel, scale), in_specs=[pl.Bloc...  11.8 us
    ppermute x3, waiting for transfers between devices, shards(): gate_grad = gate_grad + lax.ppermute(term, 'ctx', ring(ctx_count, step))  9.56 us
    ppermute x4, waiting for transfers between devices, reduce_ctx(): lax.ppermute(part, 'ctx', plan[step][1])  7.17 us
    pallas_call x1, Pallas kernels, dispatch(): pl.pallas_call(dispatch_kernel, grid=(steps,), in_specs=[pl.BlockSpec(mem...  5.87 us
    ppermute x2, waiting for transfers between devices, reduce_ctx(): lax.ppermute(part, 'ctx', plan[1][1])  5.72 us
    ppermute x4, waiting for transfers between devices, reduce_ctx(): lax.ppermute(part, 'ctx', plan[0][1])  5.67 us
  transfers between devices with their start and end apart: 28, of which 11 were waited for; matrix products, arithmetic and copies ran while one was open for 4% of the time, Pallas kernels for 0%

profile of v5, /device:TPU:6, one launch (start us, length us, event | category | flops | bytes accessed | tf_op | source)
XLA Modules:
  0.0 189.0 jit_solution(4387445636887938596)
XLA Ops:
  0.6 5.9 %shard_map.93 = (bf16[512,4096]{1,0:T(8,128)(2,1)}, bf16[128,512]{1,0:T(8,128)(2,1)}) custom-call(s32[1]{0:T(128)} %bitcast.10.base, s32[1,32,1024]{2,1,0:T(8,128)} %picks.1, bf16[1,128,2048]{2,1,0:T(8,128)(2,1)} %tokens.1, bf16[1,128,2048]{2,1,0:T(8,128)(2,1)} %out_grad.1), custom_call_target="tpu_custom_call" | custom-call | flops 536870912 | bytes 4194304 | tf_op jit(solution)/shard_map/pallas_call | solution.py:116
  6.5 11.8 %all-to-all-start = ((bf16[32,16,4096]{2,1,0:T(8,128)(2,1)}), bf16[32,16,4096]{2,1,0:T(8,128)(2,1)}, u32[]{:S(2)}, u32[]{:S(2)}) async-start(bf16[32,16,4096]{2,1,0:T(8,128)(2,1)} %bitcast.31), calls=%async_computation | async-start | bytes 8388608 | tf_op jit(solution)/shard_map/all_to_all | solution.py:308
  18.3 0.6 collective-permute-start
  18.8 2.4 %collective-permute-start.1 = (f32[256]{0:T(256)S(1)}, f32[256]{0:T(256)S(1)}, u32[]{:S(2)}, u32[]{:S(2)}) collective-permute-start(f32[256]{0:T(256)S(1)} %bitcast.42), channel_id=1, source_target_pairs={{0,64},{32,96},{64,0},{96,32},{1,65},{33,97},{65,1},{97,33},{2,66}... | collective-permute-start | bytes 3080 | tf_op jit(solution)/shard_map/ppermute | solution.py:331
  21.3 0.8 dynamic-slice_subtract_fusion
  22.0 0.5 convolution_convert_fusion.2
  22.6 0.6 fusion
  23.3 0.6 collective-permute-done.1
  24.0 2.1 %collective-permute-done.2 = f32[256]{0:T(256)S(1)} collective-permute-done((f32[256]{0:T(256)S(1)}, f32[256]{0:T(256)S(1)}, u32[]{:S(2)}, u32[]{:S(2)}) %collective-permute-start.2) | collective-permute-done | bytes 1056 | tf_op jit(solution)/shard_map/ppermute | solution.py:331
  26.1 0.9 select_reduce_fusion.1
  27.0 85.6 %all-to-all-done = bf16[32,16,4096]{2,1,0:T(8,128)(2,1)} async-done(((bf16[32,16,4096]{2,1,0:T(8,128)(2,1)}), bf16[32,16,4096]{2,1,0:T(8,128)(2,1)}, u32[]{:S(2)}, u32[]{:S(2)}) %all-to-all-start) | async-done | bytes 4194336 | tf_op jit(solution)/shard_map/all_to_all | solution.py:308
  112.6 11.8 %shard_map.94 = (f32[1,512]{1,0:T(1,128)}, bf16[512,2048]{1,0:T(8,128)(2,1)}, bf16[256,2048]{1,0:T(8,128)(2,1)}, bf16[2048,256]{1,0:T(8,128)(2,1)}, bf16[256,204...) custom-call(s32[1]{0:T(128)} %bitcast.core, f32[1,512]{1,0:T(1,128)} %bitcast.40, bf16[2048,512]{1,0:T(8,128)(2,1)} %bitcast.52, ...), custom_call_target="tpu_custom_call" | custom-call | flops 5368709120 | bytes 8388608 | tf_op jit(solution)/shard_map/pallas_call | solution.py:232
  124.4 0.1 collective-permute-start.4
  124.5 0.5 collective-permute-start.3
  125.0 7.0 %all-to-all-start.1 = ((bf16[32,16,2048]{2,1,0:T(8,128)(2,1)}), bf16[32,16,2048]{2,1,0:T(8,128)(2,1)}, u32[]{:S(2)}, u32[]{:S(2)}) async-start(bf16[32,16,2048]{2,1,0:T(8,128)(2,1)} %bitcast.32), calls=%async_computation.1 | async-start | bytes 4194304 | tf_op jit(solution)/shard_map/all_to_all | solution.py:308
  132.1 0.3 add_convert_fusion
  132.5 0.8 copy-done
  133.3 0.4 add_convert_fusion.1
  133.7 0.1 constant_dynamic-slice_fusion.9
  133.8 0.9 collective-permute-start.5
  134.7 1.1 collective-permute-start.6
  135.9 0.5 select_reduce_fusion
  136.4 2.2 %collective-permute-start.7 = (f32[256]{0:T(256)S(1)}, f32[256]{0:T(256)S(1)}, u32[]{:S(2)}, u32[]{:S(2)}) collective-permute-start(f32[256]{0:T(256)S(1)} %bitcast.51), channel_id=1, source_target_pairs={{0,32},{32,64},{64,96},{96,0},{1,33},{33,65},{65,97},{97,1},{2,34}... | collective-permute-start | bytes 3080 | tf_op jit(solution)/shard_map/ppermute | solution.py:356
  138.5 0.1 collective-permute-start.8
  138.7 1.3 collective-permute-start.9
  140.0 7.8 %collective-permute-done.7 = f32[256]{0:T(256)S(1)} collective-permute-done((f32[256]{0:T(256)S(1)}, f32[256]{0:T(256)S(1)}, u32[]{:S(2)}, u32[]{:S(2)}) %collective-permute-start.7) | collective-permute-done | bytes 1056 | tf_op jit(solution)/shard_map/ppermute | solution.py:356
  147.8 1.8 collective-permute-done.9
  149.6 0.6 add_add_fusion
  150.1 0.1 add_convert_fusion.2
  150.3 0.1 add_convert_fusion.3
  150.5 1.2 collective-permute-start.10
  151.8 7.2 %collective-permute-done.10 = bf16[64,2048]{1,0:T(8,128)(2,1)S(1)} collective-permute-done((bf16[64,2048]{1,0:T(8,128)(2,1)S(1)}, bf16[64,2048]{1,0:T(8,128)(2,1)S(1)}, u32[]{:S(2)}, u32[]{:S(2)}) %collective-permute-start.10) | collective-permute-done | bytes 262176 | tf_op jit(solution)/shard_map/ppermute | solution.py:48
  159.1 1.8 collective-permute-start.12
  160.9 2.0 %collective-permute-start.14 = (bf16[64,2048]{1,0:T(8,128)(2,1)S(1)}, bf16[64,2048]{1,0:T(8,128)(2,1)S(1)}, u32[]{:S(2)}, u32[]{:S(2)}) collective-permute-start(bf16[64,2048]{1,0:T(8,128)(2,1)S(1)} %add_convert_fusion.5.refs_0_), channel_id=1, source_target_pairs={{0,32},{32,0},{64,96},{96,64},{1,33},{33,1},{65,97},{97,65},{2,34}... | collective-permute-start | bytes 786440 | tf_op jit(solution)/shard_map/ppermute | solution.py:53
  162.9 1.5 collective-permute-start.15
  164.4 5.2 %collective-permute-done.12.refs_1_ = bf16[64,2048]{1,0:T(8,128)(2,1)S(1)} collective-permute-done((bf16[64,2048]{1,0:T(8,128)(2,1)S(1)}, bf16[64,2048]{1,0:T(8,128)(2,1)S(1)}, u32[]{:S(2)}, u32[]{:S(2)}) %collective-permute-start.12) | collective-permute-done | bytes 262176 | tf_op jit(solution)/shard_map/ppermute | solution.py:52
  169.6 0.5 collective-permute-done.13.refs_9_
  170.1 1.5 collective-permute-start.17
  171.6 3.4 %collective-permute-done.14.refs_2_ = bf16[64,2048]{1,0:T(8,128)(2,1)S(1)} collective-permute-done((bf16[64,2048]{1,0:T(8,128)(2,1)S(1)}, bf16[64,2048]{1,0:T(8,128)(2,1)S(1)}, u32[]{:S(2)}, u32[]{:S(2)}) %collective-permute-start.14) | collective-permute-done | bytes 262176 | tf_op jit(solution)/shard_map/ppermute | solution.py:53
  175.1 0.5 collective-permute-start.19
  175.6 2.2 %collective-permute-done.16.refs_3_ = bf16[64,2048]{1,0:T(8,128)(2,1)S(1)} collective-permute-done((bf16[64,2048]{1,0:T(8,128)(2,1)S(1)}, bf16[64,2048]{1,0:T(8,128)(2,1)S(1)}, u32[]{:S(2)}, u32[]{:S(2)}) %collective-permute-start.16) | collective-permute-done | bytes 262176 | tf_op jit(solution)/shard_map/ppermute | solution.py:55
  177.9 0.5 collective-permute-start.20
  178.4 0.1 collective-permute-start.21
  178.5 0.4 collective-permute-start.24
  178.9 0.1 collective-permute-start.25
  179.0 3.6 %all-to-all-done.1 = bf16[32,16,2048]{2,1,0:T(8,128)(2,1)} async-done(((bf16[32,16,2048]{2,1,0:T(8,128)(2,1)}), bf16[32,16,2048]{2,1,0:T(8,128)(2,1)}, u32[]{:S(2)}, u32[]{:S(2)}) %all-to-all-start.1) | async-done | bytes 2097184 | tf_op jit(solution)/shard_map/all_to_all | solution.py:308
  182.6 2.9 %convolution_convert_fusion = bf16[128,2048]{1,0:T(8,128)(2,1)} fusion(bf16[128,512]{1,0:T(8,128)(2,1)S(1)} %copy-done.2, bf16[512,2048]{1,0:T(8,128)(2,1)} %bitcast.19), kind=kOutput, calls=%fused_computation | convolution fusion | flops 268697600 | bytes 2752512 | tf_op jit(solution)/shard_map/dot_general | solution.py:19
  185.5 3.3 %shard_map.95 = (bf16[512,2048]{1,0:T(8,128)(2,1)}, bf16[2048,512]{1,0:T(8,128)(2,1)}) custom-call(s32[3]{0:T(128)S(1)} %pad_add_fusion.where, bf16[64,2048]{1,0:T(8,128)(2,1)S(1)} %add_convert_fusion.5.refs_0_, bf16[64,2048]{1,0:T(8,128)(2,1)S(1)} %collective-permute-done.12.refs_1_, bf16[64,2048]{1,0:T(8,128)(2,1)S(1)} %collective-permute-done.14.refs_2_, ...), custom_call_target="tpu_custom_call" | custom-call | bytes 8388608 | tf_op jit(solution)/shard_map/pallas_call | solution.py:278
  (50 shorter events, 0.7 us)
Async XLA Ops:
  6.5 11.8 %copy-start.4 = (f32[1,1,256]{2,1,0:T(1,128)S(1)}, f32[1,1,256]{2,1,0:T(1,128)}, u32[]{:S(2)}) copy-start(f32[1,1,256]{2,1,0:T(1,128)} %param.11) | copy-start | bytes 3076
  6.5 106.1 %all-to-all-start = ((bf16[32,16,4096]{2,1,0:T(8,128)(2,1)}), bf16[32,16,4096]{2,1,0:T(8,128)(2,1)}, u32[]{:S(2)}, u32[]{:S(2)}) async-start(bf16[32,16,4096]{2,1,0:T(8,128)(2,1)} %bitcast.31), calls=%async_computation | async-start | bytes 8388608 | tf_op jit(solution)/shard_map/all_to_all | solution.py:308
  18.3 5.0 %collective-permute-start = (f32[256]{0:T(256)S(1)}, f32[256]{0:T(256)S(1)}, u32[]{:S(2)}, u32[]{:S(2)}) collective-permute-start(f32[256]{0:T(256)S(1)} %bitcast.41), channel_id=1, source_target_pairs={{0,32},{32,64},{64,96},{96,0},{1,33},{33,65},{65,97},{97,1},{2,34}... | collective-permute-start | bytes 3080 | tf_op jit(solution)/shard_map/ppermute | solution.py:331
  18.8 5.1 %collective-permute-start.1 = (f32[256]{0:T(256)S(1)}, f32[256]{0:T(256)S(1)}, u32[]{:S(2)}, u32[]{:S(2)}) collective-permute-start(f32[256]{0:T(256)S(1)} %bitcast.42), channel_id=1, source_target_pairs={{0,64},{32,96},{64,0},{96,32},{1,65},{33,97},{65,1},{97,33},{2,66}... | collective-permute-start | bytes 3080 | tf_op jit(solution)/shard_map/ppermute | solution.py:331
  21.3 4.8 %collective-permute-start.2 = (f32[256]{0:T(256)S(1)}, f32[256]{0:T(256)S(1)}, u32[]{:S(2)}, u32[]{:S(2)}) collective-permute-start(f32[256]{0:T(256)S(1)} %bitcast.43), channel_id=1, source_target_pairs={{0,96},{32,0},{64,32},{96,64},{1,97},{33,1},{65,33},{97,65},{2,98}... | collective-permute-start | bytes 3080 | tf_op jit(solution)/shard_map/ppermute | solution.py:331
  124.4 7.7 %collective-permute-start.4 = (bf16[2048,256]{1,0:T(8,128)(2,1)}, bf16[2048,256]{1,0:T(8,128)(2,1)S(1)}, u32[]{:S(2)}, u32[]{:S(2)}) collective-permute-start(bf16[2048,256]{1,0:T(8,128)(2,1)} %get-tuple-element.62), channel_id=1, source_target_pairs={{0,128},{128,0},{1,129},{129,1},{2,130},{130,2},{3,131},{131,3},{4... | collective-permute-start | bytes 3145736 | tf_op jit(solution)/shard_map/ppermute | solution.py:344
  124.5 7.9 %collective-permute-start.3 = (bf16[256,2048]{1,0:T(8,128)(2,1)}, bf16[256,2048]{1,0:T(8,128)(2,1)S(1)}, u32[]{:S(2)}, u32[]{:S(2)}) collective-permute-start(bf16[256,2048]{1,0:T(8,128)(2,1)} %get-tuple-element.60), channel_id=1, source_target_pairs={{0,128},{128,0},{1,129},{129,1},{2,130},{130,2},{3,131},{131,3},{4... | collective-permute-start | bytes 3145736 | tf_op jit(solution)/shard_map/ppermute | solution.py:344
  125.0 7.1 %copy-start.1 = (bf16[2048,256]{1,0:T(8,128)(2,1)S(1)}, bf16[2048,256]{1,0:T(8,128)(2,1)}, u32[]{:S(2)}) copy-start(bf16[2048,256]{1,0:T(8,128)(2,1)} %get-tuple-element.61) | copy-start | bytes 3145732
  125.0 57.6 %all-to-all-start.1 = ((bf16[32,16,2048]{2,1,0:T(8,128)(2,1)}), bf16[32,16,2048]{2,1,0:T(8,128)(2,1)}, u32[]{:S(2)}, u32[]{:S(2)}) async-start(bf16[32,16,2048]{2,1,0:T(8,128)(2,1)} %bitcast.32), calls=%async_computation.1 | async-start | bytes 4194304 | tf_op jit(solution)/shard_map/all_to_all | solution.py:308
  132.1 1.2 copy-start
  133.3 2.6 %copy-start.3 = (f32[1,512]{1,0:T(1,128)S(1)}, f32[1,512]{1,0:T(1,128)}, u32[]{:S(2)}) copy-start(f32[1,512]{1,0:T(1,128)} %get-tuple-element.67) | copy-start | bytes 6148
  133.8 16.3 %collective-permute-start.5 = (bf16[128,2048]{1,0:T(8,128)(2,1)S(1)}, bf16[128,2048]{1,0:T(8,128)(2,1)S(1)}, u32[]{:S(2)}, u32[]{:S(2)}) collective-permute-start(bf16[128,2048]{1,0:T(8,128)(2,1)S(1)} %get-tuple-element.63), channel_id=1, source_target_pairs={{0,32},{32,0},{64,96},{96,64},{1,33},{33,1},{65,97},{97,65},{2,34}... | collective-permute-start | bytes 1572872 | tf_op jit(solution)/shard_map/ppermute | solution.py:48
  134.7 15.4 %collective-permute-start.6 = (bf16[1024,256]{1,0:T(8,128)(2,1)S(1)}, bf16[1024,256]{1,0:T(8,128)(2,1)S(1)}, u32[]{:S(2)}, u32[]{:S(2)}) collective-permute-start(bf16[1024,256]{1,0:T(8,128)(2,1)S(1)} %get-tuple-element.64), channel_id=1, source_target_pairs={{0,96},{96,0},{32,64},{64,32},{1,97},{97,1},{33,65},{65,33},{2,98}... | collective-permute-start | bytes 1572872 | tf_op jit(solution)/shard_map/ppermute | solution.py:48
  136.4 11.4 %collective-permute-start.7 = (f32[256]{0:T(256)S(1)}, f32[256]{0:T(256)S(1)}, u32[]{:S(2)}, u32[]{:S(2)}) collective-permute-start(f32[256]{0:T(256)S(1)} %bitcast.51), channel_id=1, source_target_pairs={{0,32},{32,64},{64,96},{96,0},{1,33},{33,65},{65,97},{97,1},{2,34}... | collective-permute-start | bytes 3080 | tf_op jit(solution)/shard_map/ppermute | solution.py:356
  138.5 9.3 %collective-permute-start.8 = (f32[256]{0:T(256)S(1)}, f32[256]{0:T(256)S(1)}, u32[]{:S(2)}, u32[]{:S(2)}) collective-permute-start(f32[256]{0:T(256)S(1)} %bitcast.50), channel_id=1, source_target_pairs={{0,64},{32,96},{64,0},{96,32},{1,65},{33,97},{65,1},{97,33},{2,66}... | collective-permute-start | bytes 3080 | tf_op jit(solution)/shard_map/ppermute | solution.py:356
  138.7 10.9 %collective-permute-start.9 = (f32[256]{0:T(256)S(1)}, f32[256]{0:T(256)S(1)}, u32[]{:S(2)}, u32[]{:S(2)}) collective-permute-start(f32[256]{0:T(256)S(1)} %bitcast.49), channel_id=1, source_target_pairs={{0,96},{32,0},{64,32},{96,64},{1,97},{33,1},{65,33},{97,65},{2,98}... | collective-permute-start | bytes 3080 | tf_op jit(solution)/shard_map/ppermute | solution.py:356
  150.3 32.3 %copy-start.2 = (bf16[128,512]{1,0:T(8,128)(2,1)S(1)}, bf16[128,512]{1,0:T(8,128)(2,1)}, u32[]{:S(2)}) copy-start(bf16[128,512]{1,0:T(8,128)(2,1)} %get-tuple-element.89) | copy-start | bytes 393220
  150.5 8.4 %collective-permute-start.10 = (bf16[64,2048]{1,0:T(8,128)(2,1)S(1)}, bf16[64,2048]{1,0:T(8,128)(2,1)S(1)}, u32[]{:S(2)}, u32[]{:S(2)}) collective-permute-start(bf16[64,2048]{1,0:T(8,128)(2,1)S(1)} %get-tuple-element.72), channel_id=1, source_target_pairs={{0,96},{96,0},{32,64},{64,32},{1,97},{97,1},{33,65},{65,33},{2,98}... | collective-permute-start | bytes 786440 | tf_op jit(solution)/shard_map/ppermute | solution.py:48
  151.8 7.2 %collective-permute-start.11 = (bf16[512,256]{1,0:T(8,128)(2,1)S(1)}, bf16[512,256]{1,0:T(8,128)(2,1)S(1)}, u32[]{:S(2)}, u32[]{:S(2)}) collective-permute-start(bf16[512,256]{1,0:T(8,128)(2,1)S(1)} %get-tuple-element.73), channel_id=1, source_target_pairs={{0,32},{32,0},{64,96},{96,64},{1,33},{33,1},{65,97},{97,65},{2,34}... | collective-permute-start | bytes 786440 | tf_op jit(solution)/shard_map/ppermute | solution.py:48
  159.1 10.5 %collective-permute-start.12 = (bf16[64,2048]{1,0:T(8,128)(2,1)S(1)}, bf16[64,2048]{1,0:T(8,128)(2,1)S(1)}, u32[]{:S(2)}, u32[]{:S(2)}) collective-permute-start(bf16[64,2048]{1,0:T(8,128)(2,1)S(1)} %add_convert_fusion.5.refs_0_), channel_id=1, source_target_pairs={{0,96},{96,0},{32,64},{64,32},{1,97},{97,1},{33,65},{65,33},{2,98}... | collective-permute-start | bytes 786440 | tf_op jit(solution)/shard_map/ppermute | solution.py:52
  160.9 9.2 %collective-permute-start.13 = (bf16[512,256]{1,0:T(8,128)(2,1)S(1)}, bf16[512,256]{1,0:T(8,128)(2,1)S(1)}, u32[]{:S(2)}, u32[]{:S(2)}) collective-permute-start(bf16[512,256]{1,0:T(8,128)(2,1)S(1)} %add_convert_fusion.4.refs_8_), channel_id=1, source_target_pairs={{0,32},{32,0},{64,96},{96,64},{1,33},{33,1},{65,97},{97,65},{2,34}... | collective-permute-start | bytes 786440 | tf_op jit(solution)/shard_map/ppermute | solution.py:52
  160.9 14.2 %collective-permute-start.14 = (bf16[64,2048]{1,0:T(8,128)(2,1)S(1)}, bf16[64,2048]{1,0:T(8,128)(2,1)S(1)}, u32[]{:S(2)}, u32[]{:S(2)}) collective-permute-start(bf16[64,2048]{1,0:T(8,128)(2,1)S(1)} %add_convert_fusion.5.refs_0_), channel_id=1, source_target_pairs={{0,32},{32,0},{64,96},{96,64},{1,33},{33,1},{65,97},{97,65},{2,34}... | collective-permute-start | bytes 786440 | tf_op jit(solution)/shard_map/ppermute | solution.py:53
  162.9 12.2 %collective-permute-start.15 = (bf16[512,256]{1,0:T(8,128)(2,1)S(1)}, bf16[512,256]{1,0:T(8,128)(2,1)S(1)}, u32[]{:S(2)}, u32[]{:S(2)}) collective-permute-start(bf16[512,256]{1,0:T(8,128)(2,1)S(1)} %add_convert_fusion.4.refs_8_), channel_id=1, source_target_pairs={{0,96},{96,0},{32,64},{64,32},{1,97},{97,1},{33,65},{65,33},{2,98}... | collective-permute-start | bytes 786440 | tf_op jit(solution)/shard_map/ppermute | solution.py:53
  170.1 7.7 %collective-permute-start.16 = (bf16[64,2048]{1,0:T(8,128)(2,1)S(1)}, bf16[64,2048]{1,0:T(8,128)(2,1)S(1)}, u32[]{:S(2)}, u32[]{:S(2)}) collective-permute-start(bf16[64,2048]{1,0:T(8,128)(2,1)S(1)} %collective-permute-done.12.refs_1_), channel_id=1, source_target_pairs={{0,32},{32,0},{64,96},{96,64},{1,33},{33,1},{65,97},{97,65},{2,34}... | collective-permute-start | bytes 786440 | tf_op jit(solution)/shard_map/ppermute | solution.py:55
  170.1 7.7 %collective-permute-start.17 = (bf16[512,256]{1,0:T(8,128)(2,1)S(1)}, bf16[512,256]{1,0:T(8,128)(2,1)S(1)}, u32[]{:S(2)}, u32[]{:S(2)}) collective-permute-start(bf16[512,256]{1,0:T(8,128)(2,1)S(1)} %collective-permute-done.13.refs_9_), channel_id=1, source_target_pairs={{0,96},{96,0},{32,64},{64,32},{1,97},{97,1},{33,65},{65,33},{2,98}... | collective-permute-start | bytes 786440 | tf_op jit(solution)/shard_map/ppermute | solution.py:55
  171.6 6.7 %collective-permute-start.18 = (bf16[64,2048]{1,0:T(8,128)(2,1)S(1)}, bf16[64,2048]{1,0:T(8,128)(2,1)S(1)}, u32[]{:S(2)}, u32[]{:S(2)}) collective-permute-start(bf16[64,2048]{1,0:T(8,128)(2,1)S(1)} %add_convert_fusion.5.refs_0_), channel_id=1, source_target_pairs={{0,128},{128,0},{1,129},{129,1},{2,130},{130,2},{3,131},{131,3},{4... | collective-permute-start | bytes 786440 | tf_op jit(solution)/shard_map/ppermute | solution.py:361
  175.1 3.4 %collective-permute-start.22 = (bf16[512,256]{1,0:T(8,128)(2,1)S(1)}, bf16[512,256]{1,0:T(8,128)(2,1)S(1)}, u32[]{:S(2)}, u32[]{:S(2)}) collective-permute-start(bf16[512,256]{1,0:T(8,128)(2,1)S(1)} %add_convert_fusion.4.refs_8_), channel_id=1, source_target_pairs={{0,128},{128,0},{1,129},{129,1},{2,130},{130,2},{3,131},{131,3},{4... | collective-permute-start | bytes 786440 | tf_op jit(solution)/shard_map/ppermute | solution.py:361
  175.1 3.8 %collective-permute-start.19 = (bf16[64,2048]{1,0:T(8,128)(2,1)S(1)}, bf16[64,2048]{1,0:T(8,128)(2,1)S(1)}, u32[]{:S(2)}, u32[]{:S(2)}) collective-permute-start(bf16[64,2048]{1,0:T(8,128)(2,1)S(1)} %collective-permute-done.12.refs_1_), channel_id=1, source_target_pairs={{0,128},{128,0},{1,129},{129,1},{2,130},{130,2},{3,131},{131,3},{4... | collective-permute-start | bytes 786440 | tf_op jit(solution)/shard_map/ppermute | solution.py:361
  177.9 7.6 %collective-permute-start.23 = (bf16[512,256]{1,0:T(8,128)(2,1)S(1)}, bf16[512,256]{1,0:T(8,128)(2,1)S(1)}, u32[]{:S(2)}, u32[]{:S(2)}) collective-permute-start(bf16[512,256]{1,0:T(8,128)(2,1)S(1)} %collective-permute-done.13.refs_9_), channel_id=1, source_target_pairs={{0,128},{128,0},{1,129},{129,1},{2,130},{130,2},{3,131},{131,3},{4... | collective-permute-start | bytes 786440 | tf_op jit(solution)/shard_map/ppermute | solution.py:361
  177.9 7.6 %collective-permute-start.20 = (bf16[64,2048]{1,0:T(8,128)(2,1)S(1)}, bf16[64,2048]{1,0:T(8,128)(2,1)S(1)}, u32[]{:S(2)}, u32[]{:S(2)}) collective-permute-start(bf16[64,2048]{1,0:T(8,128)(2,1)S(1)} %collective-permute-done.14.refs_2_), channel_id=1, source_target_pairs={{0,128},{128,0},{1,129},{129,1},{2,130},{130,2},{3,131},{131,3},{4... | collective-permute-start | bytes 786440 | tf_op jit(solution)/shard_map/ppermute | solution.py:361
  178.4 7.1 %collective-permute-start.21 = (bf16[64,2048]{1,0:T(8,128)(2,1)S(1)}, bf16[64,2048]{1,0:T(8,128)(2,1)}, u32[]{:S(2)}, u32[]{:S(2)}) collective-permute-start(bf16[64,2048]{1,0:T(8,128)(2,1)S(1)} %collective-permute-done.16.refs_3_), channel_id=1, source_target_pairs={{0,128},{128,0},{1,129},{129,1},{2,130},{130,2},{3,131},{131,3},{4... | collective-permute-start | bytes 786440 | tf_op jit(solution)/shard_map/ppermute | solution.py:361
  178.5 7.0 %collective-permute-start.24 = (bf16[512,256]{1,0:T(8,128)(2,1)S(1)}, bf16[512,256]{1,0:T(8,128)(2,1)}, u32[]{:S(2)}, u32[]{:S(2)}) collective-permute-start(bf16[512,256]{1,0:T(8,128)(2,1)S(1)} %collective-permute-done.15.refs_10_), channel_id=1, source_target_pairs={{0,128},{128,0},{1,129},{129,1},{2,130},{130,2},{3,131},{131,3},{4... | collective-permute-start | bytes 786440 | tf_op jit(solution)/shard_map/ppermute | solution.py:361
  178.9 6.6 %collective-permute-start.25 = (bf16[512,256]{1,0:T(8,128)(2,1)S(1)}, bf16[512,256]{1,0:T(8,128)(2,1)}, u32[]{:S(2)}, u32[]{:S(2)}) collective-permute-start(bf16[512,256]{1,0:T(8,128)(2,1)S(1)} %collective-permute-done.17.refs_11_), channel_id=1, source_target_pairs={{0,128},{128,0},{1,129},{129,1},{2,130},{130,2},{3,131},{131,3},{4... | collective-permute-start | bytes 786440 | tf_op jit(solution)/shard_map/ppermute | solution.py:361

commit v6 on v5

--- a/solution.py
+++ b/solution.py
@@ -107,7 +107,7 @@
     exp_count, pick_total = picks.shape[1:]
     tok_dev, feat = tokens.shape[1:]
     lows = 16
-    steps = 4
+    steps = 2
     rows = exp_count * slots // steps
 
     def whole(shape):

time: 189 us -> 189 us (level)
  transfers between devices with their start and end apart: 28 -> 28, of which waited for: 11 -> 12; matrix products, arithmetic and copies ran while one was open for 4% -> 4% of each run, Pallas kernels for 0% -> 0%
where the time goes in v6:
time: 189 us; the launch traced here: 188 us
  waiting for transfers between devices  120 us (63%)
  starting transfers between devices  37.9 us (20%)
  Pallas kernels  20.2 us (11%)
  matrix products  3.95 us (2%)
  other arithmetic  3.87 us (2%)
    all_to_all x2, waiting for transfers between devices, swap(): out = lax.all_to_all(out, 'expert', split_axis=0, concat_axis=0, tiled=True)  89.7 us
    all_to_all x2, starting transfers between devices, swap(): out = lax.all_to_all(out, 'expert', split_axis=0, concat_axis=0, tiled=True)  18.8 us
    pallas_call x1, Pallas kernels, expert_pass(): pl.pallas_call(functools.partial(expert_kernel, scale), in_specs=[pl.Bloc...  11.8 us
    ppermute x3, waiting for transfers between devices, shards(): gate_grad = gate_grad + lax.ppermute(term, 'ctx', ring(ctx_count, step))  9.39 us
    ppermute x4, waiting for transfers between devices, reduce_ctx(): lax.ppermute(part, 'ctx', plan[step][1])  6.96 us
    ppermute x2, waiting for transfers between devices, reduce_ctx(): lax.ppermute(part, 'ctx', plan[1][1])  5.72 us
    ppermute x4, waiting for transfers between devices, reduce_ctx(): lax.ppermute(part, 'ctx', plan[0][1])  5.49 us
    pallas_call x1, Pallas kernels, dispatch(): pl.pallas_call(dispatch_kernel, grid=(steps,), in_specs=[pl.BlockSpec(mem...  5.16 us
  transfers between devices with their start and end apart: 28, of which 12 were waited for; matrix products, arithmetic and copies ran while one was open for 4% of the time, Pallas kernels for 0%

profile of v6, /device:TPU:6, one launch (start us, length us, event | category | flops | bytes accessed | tf_op | source)
XLA Modules:
  0.0 188.3 jit_solution(16430312296627109831)
XLA Ops:
  0.6 5.2 %shard_map.93 = (bf16[512,4096]{1,0:T(8,128)(2,1)}, bf16[128,512]{1,0:T(8,128)(2,1)}) custom-call(s32[1]{0:T(128)} %bitcast.10.base, s32[1,32,1024]{2,1,0:T(8,128)} %picks.1, bf16[1,128,2048]{2,1,0:T(8,128)(2,1)} %tokens.1, bf16[1,128,2048]{2,1,0:T(8,128)(2,1)} %out_grad.1), custom_call_target="tpu_custom_call" | custom-call | flops 536870912 | bytes 4194304 | tf_op jit(solution)/shard_map/pallas_call | solution.py:116
  5.8 11.7 %all-to-all-start = ((bf16[32,16,4096]{2,1,0:T(8,128)(2,1)}), bf16[32,16,4096]{2,1,0:T(8,128)(2,1)}, u32[]{:S(2)}, u32[]{:S(2)}) async-start(bf16[32,16,4096]{2,1,0:T(8,128)(2,1)} %bitcast.31), calls=%async_computation | async-start | bytes 8388608 | tf_op jit(solution)/shard_map/all_to_all | solution.py:308
  17.6 0.6 collective-permute-start
  18.1 2.4 %collective-permute-start.1 = (f32[256]{0:T(256)S(1)}, f32[256]{0:T(256)S(1)}, u32[]{:S(2)}, u32[]{:S(2)}) collective-permute-start(f32[256]{0:T(256)S(1)} %bitcast.42), channel_id=1, source_target_pairs={{0,64},{32,96},{64,0},{96,32},{1,65},{33,97},{65,1},{97,33},{2,66}... | collective-permute-start | bytes 3080 | tf_op jit(solution)/shard_map/ppermute | solution.py:331
  20.5 0.8 dynamic-slice_subtract_fusion
  21.3 0.5 convolution_convert_fusion.2
  21.9 0.6 fusion
  22.6 0.6 collective-permute-done.1
  23.2 2.1 %collective-permute-done.2 = f32[256]{0:T(256)S(1)} collective-permute-done((f32[256]{0:T(256)S(1)}, f32[256]{0:T(256)S(1)}, u32[]{:S(2)}, u32[]{:S(2)}) %collective-permute-start.2) | collective-permute-done | bytes 1056 | tf_op jit(solution)/shard_map/ppermute | solution.py:331
  25.4 0.9 select_reduce_fusion.1
  26.3 85.6 %all-to-all-done = bf16[32,16,4096]{2,1,0:T(8,128)(2,1)} async-done(((bf16[32,16,4096]{2,1,0:T(8,128)(2,1)}), bf16[32,16,4096]{2,1,0:T(8,128)(2,1)}, u32[]{:S(2)}, u32[]{:S(2)}) %all-to-all-start) | async-done | bytes 4194336 | tf_op jit(solution)/shard_map/all_to_all | solution.py:308
  111.9 11.8 %shard_map.94 = (f32[1,512]{1,0:T(1,128)}, bf16[512,2048]{1,0:T(8,128)(2,1)}, bf16[256,2048]{1,0:T(8,128)(2,1)}, bf16[2048,256]{1,0:T(8,128)(2,1)}, bf16[256,204...) custom-call(s32[1]{0:T(128)} %bitcast.core, f32[1,512]{1,0:T(1,128)} %bitcast.40, bf16[2048,512]{1,0:T(8,128)(2,1)} %bitcast.52, ...), custom_call_target="tpu_custom_call" | custom-call | flops 5368709120 | bytes 8388608 | tf_op jit(solution)/shard_map/pallas_call | solution.py:232
  123.7 0.3 collective-permute-start.4
  124.0 0.5 collective-permute-start.3
  124.5 7.0 %all-to-all-start.1 = ((bf16[32,16,2048]{2,1,0:T(8,128)(2,1)}), bf16[32,16,2048]{2,1,0:T(8,128)(2,1)}, u32[]{:S(2)}, u32[]{:S(2)}) async-start(bf16[32,16,2048]{2,1,0:T(8,128)(2,1)} %bitcast.32), calls=%async_computation.1 | async-start | bytes 4194304 | tf_op jit(solution)/shard_map/all_to_all | solution.py:308
  131.5 0.3 add_convert_fusion
  131.9 0.8 copy-done
  132.8 0.4 add_convert_fusion.1
  133.2 0.1 constant_dynamic-slice_fusion.9
  133.3 0.9 collective-permute-start.5
  134.2 1.1 collective-permute-start.6
  135.3 0.5 select_reduce_fusion
  135.8 2.2 %collective-permute-start.7 = (f32[256]{0:T(256)S(1)}, f32[256]{0:T(256)S(1)}, u32[]{:S(2)}, u32[]{:S(2)}) collective-permute-start(f32[256]{0:T(256)S(1)} %bitcast.51), channel_id=1, source_target_pairs={{0,32},{32,64},{64,96},{96,0},{1,33},{33,65},{65,97},{97,1},{2,34}... | collective-permute-start | bytes 3080 | tf_op jit(solution)/shard_map/ppermute | solution.py:356
  138.0 0.1 collective-permute-start.8
  138.1 1.3 collective-permute-start.9
  139.5 7.6 %collective-permute-done.7 = f32[256]{0:T(256)S(1)} collective-permute-done((f32[256]{0:T(256)S(1)}, f32[256]{0:T(256)S(1)}, u32[]{:S(2)}, u32[]{:S(2)}) %collective-permute-start.7) | collective-permute-done | bytes 1056 | tf_op jit(solution)/shard_map/ppermute | solution.py:356
  147.1 1.8 collective-permute-done.9
  148.8 0.6 add_add_fusion
  149.4 0.1 add_convert_fusion.2
  149.6 0.1 add_convert_fusion.3
  149.8 1.2 collective-permute-start.10
  151.0 7.0 %collective-permute-done.10 = bf16[64,2048]{1,0:T(8,128)(2,1)S(1)} collective-permute-done((bf16[64,2048]{1,0:T(8,128)(2,1)S(1)}, bf16[64,2048]{1,0:T(8,128)(2,1)S(1)}, u32[]{:S(2)}, u32[]{:S(2)}) %collective-permute-start.10) | collective-permute-done | bytes 262176 | tf_op jit(solution)/shard_map/ppermute | solution.py:48
  158.2 1.8 collective-permute-start.12
  160.0 2.0 %collective-permute-start.14 = (bf16[64,2048]{1,0:T(8,128)(2,1)S(1)}, bf16[64,2048]{1,0:T(8,128)(2,1)S(1)}, u32[]{:S(2)}, u32[]{:S(2)}) collective-permute-start(bf16[64,2048]{1,0:T(8,128)(2,1)S(1)} %add_convert_fusion.5.refs_0_), channel_id=1, source_target_pairs={{0,32},{32,0},{64,96},{96,64},{1,33},{33,1},{65,97},{97,65},{2,34}... | collective-permute-start | bytes 786440 | tf_op jit(solution)/shard_map/ppermute | solution.py:53
  162.0 1.5 collective-permute-start.15
  163.5 5.2 %collective-permute-done.12.refs_1_ = bf16[64,2048]{1,0:T(8,128)(2,1)S(1)} collective-permute-done((bf16[64,2048]{1,0:T(8,128)(2,1)S(1)}, bf16[64,2048]{1,0:T(8,128)(2,1)S(1)}, u32[]{:S(2)}, u32[]{:S(2)}) %collective-permute-start.12) | collective-permute-done | bytes 262176 | tf_op jit(solution)/shard_map/ppermute | solution.py:52
  168.7 0.5 collective-permute-done.13.refs_9_
  169.2 1.5 collective-permute-start.17
  170.7 3.2 %collective-permute-done.14.refs_2_ = bf16[64,2048]{1,0:T(8,128)(2,1)S(1)} collective-permute-done((bf16[64,2048]{1,0:T(8,128)(2,1)S(1)}, bf16[64,2048]{1,0:T(8,128)(2,1)S(1)}, u32[]{:S(2)}, u32[]{:S(2)}) %collective-permute-start.14) | collective-permute-done | bytes 262176 | tf_op jit(solution)/shard_map/ppermute | solution.py:53
  173.9 0.5 collective-permute-start.19
  174.5 2.2 %collective-permute-done.16.refs_3_ = bf16[64,2048]{1,0:T(8,128)(2,1)S(1)} collective-permute-done((bf16[64,2048]{1,0:T(8,128)(2,1)S(1)}, bf16[64,2048]{1,0:T(8,128)(2,1)S(1)}, u32[]{:S(2)}, u32[]{:S(2)}) %collective-permute-start.16) | collective-permute-done | bytes 262176 | tf_op jit(solution)/shard_map/ppermute | solution.py:55
  176.8 0.4 collective-permute-start.20
  177.3 0.1 collective-permute-start.21
  177.4 0.4 collective-permute-start.24
  177.8 0.1 collective-permute-start.25
  177.9 4.1 %all-to-all-done.1 = bf16[32,16,2048]{2,1,0:T(8,128)(2,1)} async-done(((bf16[32,16,2048]{2,1,0:T(8,128)(2,1)}), bf16[32,16,2048]{2,1,0:T(8,128)(2,1)}, u32[]{:S(2)}, u32[]{:S(2)}) %all-to-all-start.1) | async-done | bytes 2097184 | tf_op jit(solution)/shard_map/all_to_all | solution.py:308
  181.9 2.8 %convolution_convert_fusion = bf16[128,2048]{1,0:T(8,128)(2,1)} fusion(bf16[128,512]{1,0:T(8,128)(2,1)S(1)} %copy-done.2, bf16[512,2048]{1,0:T(8,128)(2,1)} %bitcast.19), kind=kOutput, calls=%fused_computation | convolution fusion | flops 268697600 | bytes 2752512 | tf_op jit(solution)/shard_map/dot_general | solution.py:19
  184.8 3.3 %shard_map.95 = (bf16[512,2048]{1,0:T(8,128)(2,1)}, bf16[2048,512]{1,0:T(8,128)(2,1)}) custom-call(s32[3]{0:T(128)S(1)} %pad_add_fusion.where, bf16[64,2048]{1,0:T(8,128)(2,1)S(1)} %add_convert_fusion.5.refs_0_, bf16[64,2048]{1,0:T(8,128)(2,1)S(1)} %collective-permute-done.12.refs_1_, bf16[64,2048]{1,0:T(8,128)(2,1)S(1)} %collective-permute-done.14.refs_2_, ...), custom_call_target="tpu_custom_call" | custom-call | bytes 8388608 | tf_op jit(solution)/shard_map/pallas_call | solution.py:278
  (50 shorter events, 0.7 us)
Async XLA Ops:
  5.8 11.8 %copy-start.4 = (f32[1,1,256]{2,1,0:T(1,128)S(1)}, f32[1,1,256]{2,1,0:T(1,128)}, u32[]{:S(2)}) copy-start(f32[1,1,256]{2,1,0:T(1,128)} %param.11) | copy-start | bytes 3076
  5.8 106.1 %all-to-all-start = ((bf16[32,16,4096]{2,1,0:T(8,128)(2,1)}), bf16[32,16,4096]{2,1,0:T(8,128)(2,1)}, u32[]{:S(2)}, u32[]{:S(2)}) async-start(bf16[32,16,4096]{2,1,0:T(8,128)(2,1)} %bitcast.31), calls=%async_computation | async-start | bytes 8388608 | tf_op jit(solution)/shard_map/all_to_all | solution.py:308
  17.6 5.0 %collective-permute-start = (f32[256]{0:T(256)S(1)}, f32[256]{0:T(256)S(1)}, u32[]{:S(2)}, u32[]{:S(2)}) collective-permute-start(f32[256]{0:T(256)S(1)} %bitcast.41), channel_id=1, source_target_pairs={{0,32},{32,64},{64,96},{96,0},{1,33},{33,65},{65,97},{97,1},{2,34}... | collective-permute-start | bytes 3080 | tf_op jit(solution)/shard_map/ppermute | solution.py:331
  18.1 5.1 %collective-permute-start.1 = (f32[256]{0:T(256)S(1)}, f32[256]{0:T(256)S(1)}, u32[]{:S(2)}, u32[]{:S(2)}) collective-permute-start(f32[256]{0:T(256)S(1)} %bitcast.42), channel_id=1, source_target_pairs={{0,64},{32,96},{64,0},{96,32},{1,65},{33,97},{65,1},{97,33},{2,66}... | collective-permute-start | bytes 3080 | tf_op jit(solution)/shard_map/ppermute | solution.py:331
  20.5 4.8 %collective-permute-start.2 = (f32[256]{0:T(256)S(1)}, f32[256]{0:T(256)S(1)}, u32[]{:S(2)}, u32[]{:S(2)}) collective-permute-start(f32[256]{0:T(256)S(1)} %bitcast.43), channel_id=1, source_target_pairs={{0,96},{32,0},{64,32},{96,64},{1,97},{33,1},{65,33},{97,65},{2,98}... | collective-permute-start | bytes 3080 | tf_op jit(solution)/shard_map/ppermute | solution.py:331
  123.7 7.8 %collective-permute-start.4 = (bf16[2048,256]{1,0:T(8,128)(2,1)}, bf16[2048,256]{1,0:T(8,128)(2,1)S(1)}, u32[]{:S(2)}, u32[]{:S(2)}) collective-permute-start(bf16[2048,256]{1,0:T(8,128)(2,1)} %get-tuple-element.62), channel_id=1, source_target_pairs={{0,128},{128,0},{1,129},{129,1},{2,130},{130,2},{3,131},{131,3},{4... | collective-permute-start | bytes 3145736 | tf_op jit(solution)/shard_map/ppermute | solution.py:344
  124.0 8.0 %collective-permute-start.3 = (bf16[256,2048]{1,0:T(8,128)(2,1)}, bf16[256,2048]{1,0:T(8,128)(2,1)S(1)}, u32[]{:S(2)}, u32[]{:S(2)}) collective-permute-start(bf16[256,2048]{1,0:T(8,128)(2,1)} %get-tuple-element.60), channel_id=1, source_target_pairs={{0,128},{128,0},{1,129},{129,1},{2,130},{130,2},{3,131},{131,3},{4... | collective-permute-start | bytes 3145736 | tf_op jit(solution)/shard_map/ppermute | solution.py:344
  124.5 7.1 %copy-start.1 = (bf16[2048,256]{1,0:T(8,128)(2,1)S(1)}, bf16[2048,256]{1,0:T(8,128)(2,1)}, u32[]{:S(2)}) copy-start(bf16[2048,256]{1,0:T(8,128)(2,1)} %get-tuple-element.61) | copy-start | bytes 3145732
  124.5 57.5 %all-to-all-start.1 = ((bf16[32,16,2048]{2,1,0:T(8,128)(2,1)}), bf16[32,16,2048]{2,1,0:T(8,128)(2,1)}, u32[]{:S(2)}, u32[]{:S(2)}) async-start(bf16[32,16,2048]{2,1,0:T(8,128)(2,1)} %bitcast.32), calls=%async_computation.1 | async-start | bytes 4194304 | tf_op jit(solution)/shard_map/all_to_all | solution.py:308
  131.5 1.2 copy-start
  132.8 2.6 %copy-start.3 = (f32[1,512]{1,0:T(1,128)S(1)}, f32[1,512]{1,0:T(1,128)}, u32[]{:S(2)}) copy-start(f32[1,512]{1,0:T(1,128)} %get-tuple-element.67) | copy-start | bytes 6148
  133.3 16.1 %collective-permute-start.5 = (bf16[128,2048]{1,0:T(8,128)(2,1)S(1)}, bf16[128,2048]{1,0:T(8,128)(2,1)S(1)}, u32[]{:S(2)}, u32[]{:S(2)}) collective-permute-start(bf16[128,2048]{1,0:T(8,128)(2,1)S(1)} %get-tuple-element.63), channel_id=1, source_target_pairs={{0,32},{32,0},{64,96},{96,64},{1,33},{33,1},{65,97},{97,65},{2,34}... | collective-permute-start | bytes 1572872 | tf_op jit(solution)/shard_map/ppermute | solution.py:48
  134.2 15.2 %collective-permute-start.6 = (bf16[1024,256]{1,0:T(8,128)(2,1)S(1)}, bf16[1024,256]{1,0:T(8,128)(2,1)S(1)}, u32[]{:S(2)}, u32[]{:S(2)}) collective-permute-start(bf16[1024,256]{1,0:T(8,128)(2,1)S(1)} %get-tuple-element.64), channel_id=1, source_target_pairs={{0,96},{96,0},{32,64},{64,32},{1,97},{97,1},{33,65},{65,33},{2,98}... | collective-permute-start | bytes 1572872 | tf_op jit(solution)/shard_map/ppermute | solution.py:48
  135.8 11.3 %collective-permute-start.7 = (f32[256]{0:T(256)S(1)}, f32[256]{0:T(256)S(1)}, u32[]{:S(2)}, u32[]{:S(2)}) collective-permute-start(f32[256]{0:T(256)S(1)} %bitcast.51), channel_id=1, source_target_pairs={{0,32},{32,64},{64,96},{96,0},{1,33},{33,65},{65,97},{97,1},{2,34}... | collective-permute-start | bytes 3080 | tf_op jit(solution)/shard_map/ppermute | solution.py:356
  138.0 9.1 %collective-permute-start.8 = (f32[256]{0:T(256)S(1)}, f32[256]{0:T(256)S(1)}, u32[]{:S(2)}, u32[]{:S(2)}) collective-permute-start(f32[256]{0:T(256)S(1)} %bitcast.50), channel_id=1, source_target_pairs={{0,64},{32,96},{64,0},{96,32},{1,65},{33,97},{65,1},{97,33},{2,66}... | collective-permute-start | bytes 3080 | tf_op jit(solution)/shard_map/ppermute | solution.py:356
  138.1 10.7 %collective-permute-start.9 = (f32[256]{0:T(256)S(1)}, f32[256]{0:T(256)S(1)}, u32[]{:S(2)}, u32[]{:S(2)}) collective-permute-start(f32[256]{0:T(256)S(1)} %bitcast.49), channel_id=1, source_target_pairs={{0,96},{32,0},{64,32},{96,64},{1,97},{33,1},{65,33},{97,65},{2,98}... | collective-permute-start | bytes 3080 | tf_op jit(solution)/shard_map/ppermute | solution.py:356
  149.6 32.3 %copy-start.2 = (bf16[128,512]{1,0:T(8,128)(2,1)S(1)}, bf16[128,512]{1,0:T(8,128)(2,1)}, u32[]{:S(2)}) copy-start(bf16[128,512]{1,0:T(8,128)(2,1)} %get-tuple-element.89) | copy-start | bytes 393220
  149.8 8.2 %collective-permute-start.10 = (bf16[64,2048]{1,0:T(8,128)(2,1)S(1)}, bf16[64,2048]{1,0:T(8,128)(2,1)S(1)}, u32[]{:S(2)}, u32[]{:S(2)}) collective-permute-start(bf16[64,2048]{1,0:T(8,128)(2,1)S(1)} %get-tuple-element.72), channel_id=1, source_target_pairs={{0,96},{96,0},{32,64},{64,32},{1,97},{97,1},{33,65},{65,33},{2,98}... | collective-permute-start | bytes 786440 | tf_op jit(solution)/shard_map/ppermute | solution.py:48
  151.0 7.0 %collective-permute-start.11 = (bf16[512,256]{1,0:T(8,128)(2,1)S(1)}, bf16[512,256]{1,0:T(8,128)(2,1)S(1)}, u32[]{:S(2)}, u32[]{:S(2)}) collective-permute-start(bf16[512,256]{1,0:T(8,128)(2,1)S(1)} %get-tuple-element.73), channel_id=1, source_target_pairs={{0,32},{32,0},{64,96},{96,64},{1,33},{33,1},{65,97},{97,65},{2,34}... | collective-permute-start | bytes 786440 | tf_op jit(solution)/shard_map/ppermute | solution.py:48
  158.2 10.5 %collective-permute-start.12 = (bf16[64,2048]{1,0:T(8,128)(2,1)S(1)}, bf16[64,2048]{1,0:T(8,128)(2,1)S(1)}, u32[]{:S(2)}, u32[]{:S(2)}) collective-permute-start(bf16[64,2048]{1,0:T(8,128)(2,1)S(1)} %add_convert_fusion.5.refs_0_), channel_id=1, source_target_pairs={{0,96},{96,0},{32,64},{64,32},{1,97},{97,1},{33,65},{65,33},{2,98}... | collective-permute-start | bytes 786440 | tf_op jit(solution)/shard_map/ppermute | solution.py:52
  160.0 9.2 %collective-permute-start.13 = (bf16[512,256]{1,0:T(8,128)(2,1)S(1)}, bf16[512,256]{1,0:T(8,128)(2,1)S(1)}, u32[]{:S(2)}, u32[]{:S(2)}) collective-permute-start(bf16[512,256]{1,0:T(8,128)(2,1)S(1)} %add_convert_fusion.4.refs_8_), channel_id=1, source_target_pairs={{0,32},{32,0},{64,96},{96,64},{1,33},{33,1},{65,97},{97,65},{2,34}... | collective-permute-start | bytes 786440 | tf_op jit(solution)/shard_map/ppermute | solution.py:52
  160.0 13.9 %collective-permute-start.14 = (bf16[64,2048]{1,0:T(8,128)(2,1)S(1)}, bf16[64,2048]{1,0:T(8,128)(2,1)S(1)}, u32[]{:S(2)}, u32[]{:S(2)}) collective-permute-start(bf16[64,2048]{1,0:T(8,128)(2,1)S(1)} %add_convert_fusion.5.refs_0_), channel_id=1, source_target_pairs={{0,32},{32,0},{64,96},{96,64},{1,33},{33,1},{65,97},{97,65},{2,34}... | collective-permute-start | bytes 786440 | tf_op jit(solution)/shard_map/ppermute | solution.py:53
  162.0 11.9 %collective-permute-start.15 = (bf16[512,256]{1,0:T(8,128)(2,1)S(1)}, bf16[512,256]{1,0:T(8,128)(2,1)S(1)}, u32[]{:S(2)}, u32[]{:S(2)}) collective-permute-start(bf16[512,256]{1,0:T(8,128)(2,1)S(1)} %add_convert_fusion.4.refs_8_), channel_id=1, source_target_pairs={{0,96},{96,0},{32,64},{64,32},{1,97},{97,1},{33,65},{65,33},{2,98}... | collective-permute-start | bytes 786440 | tf_op jit(solution)/shard_map/ppermute | solution.py:53
  169.2 7.5 %collective-permute-start.16 = (bf16[64,2048]{1,0:T(8,128)(2,1)S(1)}, bf16[64,2048]{1,0:T(8,128)(2,1)S(1)}, u32[]{:S(2)}, u32[]{:S(2)}) collective-permute-start(bf16[64,2048]{1,0:T(8,128)(2,1)S(1)} %collective-permute-done.12.refs_1_), channel_id=1, source_target_pairs={{0,32},{32,0},{64,96},{96,64},{1,33},{33,1},{65,97},{97,65},{2,34}... | collective-permute-start | bytes 786440 | tf_op jit(solution)/shard_map/ppermute | solution.py:55
  169.2 7.6 %collective-permute-start.17 = (bf16[512,256]{1,0:T(8,128)(2,1)S(1)}, bf16[512,256]{1,0:T(8,128)(2,1)S(1)}, u32[]{:S(2)}, u32[]{:S(2)}) collective-permute-start(bf16[512,256]{1,0:T(8,128)(2,1)S(1)} %collective-permute-done.13.refs_9_), channel_id=1, source_target_pairs={{0,96},{96,0},{32,64},{64,32},{1,97},{97,1},{33,65},{65,33},{2,98}... | collective-permute-start | bytes 786440 | tf_op jit(solution)/shard_map/ppermute | solution.py:55
  170.7 6.5 %collective-permute-start.18 = (bf16[64,2048]{1,0:T(8,128)(2,1)S(1)}, bf16[64,2048]{1,0:T(8,128)(2,1)S(1)}, u32[]{:S(2)}, u32[]{:S(2)}) collective-permute-start(bf16[64,2048]{1,0:T(8,128)(2,1)S(1)} %add_convert_fusion.5.refs_0_), channel_id=1, source_target_pairs={{0,128},{128,0},{1,129},{129,1},{2,130},{130,2},{3,131},{131,3},{4... | collective-permute-start | bytes 786440 | tf_op jit(solution)/shard_map/ppermute | solution.py:361
  173.9 3.4 %collective-permute-start.22 = (bf16[512,256]{1,0:T(8,128)(2,1)S(1)}, bf16[512,256]{1,0:T(8,128)(2,1)S(1)}, u32[]{:S(2)}, u32[]{:S(2)}) collective-permute-start(bf16[512,256]{1,0:T(8,128)(2,1)S(1)} %add_convert_fusion.4.refs_8_), channel_id=1, source_target_pairs={{0,128},{128,0},{1,129},{129,1},{2,130},{130,2},{3,131},{131,3},{4... | collective-permute-start | bytes 786440 | tf_op jit(solution)/shard_map/ppermute | solution.py:361
  173.9 3.8 %collective-permute-start.19 = (bf16[64,2048]{1,0:T(8,128)(2,1)S(1)}, bf16[64,2048]{1,0:T(8,128)(2,1)S(1)}, u32[]{:S(2)}, u32[]{:S(2)}) collective-permute-start(bf16[64,2048]{1,0:T(8,128)(2,1)S(1)} %collective-permute-done.12.refs_1_), channel_id=1, source_target_pairs={{0,128},{128,0},{1,129},{129,1},{2,130},{130,2},{3,131},{131,3},{4... | collective-permute-start | bytes 786440 | tf_op jit(solution)/shard_map/ppermute | solution.py:361
  176.7 8.0 %collective-permute-start.23 = (bf16[512,256]{1,0:T(8,128)(2,1)S(1)}, bf16[512,256]{1,0:T(8,128)(2,1)S(1)}, u32[]{:S(2)}, u32[]{:S(2)}) collective-permute-start(bf16[512,256]{1,0:T(8,128)(2,1)S(1)} %collective-permute-done.13.refs_9_), channel_id=1, source_target_pairs={{0,128},{128,0},{1,129},{129,1},{2,130},{130,2},{3,131},{131,3},{4... | collective-permute-start | bytes 786440 | tf_op jit(solution)/shard_map/ppermute | solution.py:361
  176.8 8.0 %collective-permute-start.20 = (bf16[64,2048]{1,0:T(8,128)(2,1)S(1)}, bf16[64,2048]{1,0:T(8,128)(2,1)S(1)}, u32[]{:S(2)}, u32[]{:S(2)}) collective-permute-start(bf16[64,2048]{1,0:T(8,128)(2,1)S(1)} %collective-permute-done.14.refs_2_), channel_id=1, source_target_pairs={{0,128},{128,0},{1,129},{129,1},{2,130},{130,2},{3,131},{131,3},{4... | collective-permute-start | bytes 786440 | tf_op jit(solution)/shard_map/ppermute | solution.py:361
  177.3 7.5 %collective-permute-start.21 = (bf16[64,2048]{1,0:T(8,128)(2,1)S(1)}, bf16[64,2048]{1,0:T(8,128)(2,1)}, u32[]{:S(2)}, u32[]{:S(2)}) collective-permute-start(bf16[64,2048]{1,0:T(8,128)(2,1)S(1)} %collective-permute-done.16.refs_3_), channel_id=1, source_target_pairs={{0,128},{128,0},{1,129},{129,1},{2,130},{130,2},{3,131},{131,3},{4... | collective-permute-start | bytes 786440 | tf_op jit(solution)/shard_map/ppermute | solution.py:361
  177.4 7.4 %collective-permute-start.24 = (bf16[512,256]{1,0:T(8,128)(2,1)S(1)}, bf16[512,256]{1,0:T(8,128)(2,1)}, u32[]{:S(2)}, u32[]{:S(2)}) collective-permute-start(bf16[512,256]{1,0:T(8,128)(2,1)S(1)} %collective-permute-done.15.refs_10_), channel_id=1, source_target_pairs={{0,128},{128,0},{1,129},{129,1},{2,130},{130,2},{3,131},{131,3},{4... | collective-permute-start | bytes 786440 | tf_op jit(solution)/shard_map/ppermute | solution.py:361
  177.8 7.0 %collective-permute-start.25 = (bf16[512,256]{1,0:T(8,128)(2,1)S(1)}, bf16[512,256]{1,0:T(8,128)(2,1)}, u32[]{:S(2)}, u32[]{:S(2)}) collective-permute-start(bf16[512,256]{1,0:T(8,128)(2,1)S(1)} %collective-permute-done.17.refs_11_), channel_id=1, source_target_pairs={{0,128},{128,0},{1,129},{129,1},{2,130},{130,2},{3,131},{131,3},{4... | collective-permute-start | bytes 786440 | tf_op jit(solution)/shard_map/ppermute | solution.py:361

commit v7 on v6

--- a/solution.py
+++ b/solution.py
@@ -150,7 +150,7 @@
     grads, out_theirs, in_theirs, out_mine, in_mine, pre, gated, in_sems, out_sems = refs[5:]
     count, feat = grads.shape
     hid = pre.shape[1]
-    chunks = 2
+    chunks = 1
     size = count // chunks
     copy_of = pltpu.make_async_copy
 
@@ -161,11 +161,8 @@
     loads = [
         copy_of(out_hbm, weight_out, in_sems.at[2 * chunks]),
         copy_of(in_hbm, weight_in, in_sems.at[2 * chunks + 1]),
-        chunk(0, 0),
-        chunk(0, 1),
-        chunk(1, 0),
-        chunk(1, 1),
     ]
+    loads += [chunk(i, part) for i in range(chunks) for part in range(2)]
     for load in loads:
         load.start()
     sent = []
@@ -236,7 +233,7 @@
         out_shape=[jax.ShapeDtypeStruct((1, count), F32)]
         + [jax.ShapeDtypeStruct(shape, BF) for shape in shapes],
         scratch_shapes=[pltpu.VMEM(shape, BF) for shape in held]
-        + [pltpu.SemaphoreType.DMA((6,)), pltpu.SemaphoreType.DMA((18,))],
+        + [pltpu.SemaphoreType.DMA((4,)), pltpu.SemaphoreType.DMA((17,))],
         compiler_params=pltpu.CompilerParams(vmem_limit_bytes=58 * 1024 * 1024),
         cost_estimate=pl.CostEstimate(
             flops=10 * count * feat * hid,

time: 189 us -> 188 us (level)
  transfers between devices with their start and end apart: 28 -> 28, of which waited for: 12 -> 11; matrix products, arithmetic and copies ran while one was open for 4% -> 4% of each run, Pallas kernels for 0% -> 0%
where the time goes in v7:
time: 188 us
  waiting for transfers between devices  120 us (64%)
  starting transfers between devices  37.7 us (20%)
  Pallas kernels  19.7 us (10%)
  matrix products  3.95 us (2%)
  other arithmetic  3.87 us (2%)
    all_to_all x2, waiting for transfers between devices, swap(): out = lax.all_to_all(out, 'expert', split_axis=0, concat_axis=0, tiled=True)  89.2 us
    all_to_all x2, starting transfers between devices, swap(): out = lax.all_to_all(out, 'expert', split_axis=0, concat_axis=0, tiled=True)  18.8 us
    pallas_call x1, Pallas kernels, expert_pass(): pl.pallas_call(functools.partial(expert_kernel, scale), in_specs=[pl.Bloc...  11.3 us
    ppermute x3, waiting for transfers between devices, shards(): gate_grad = gate_grad + lax.ppermute(term, 'ctx', ring(ctx_count, step))  9.57 us
    ppermute x4, waiting for transfers between devices, reduce_ctx(): lax.ppermute(part, 'ctx', plan[step][1])  7.17 us
    ppermute x2, waiting for transfers between devices, reduce_ctx(): lax.ppermute(part, 'ctx', plan[1][1])  5.72 us
    ppermute x4, waiting for transfers between devices, reduce_ctx(): lax.ppermute(part, 'ctx', plan[0][1])  5.67 us
    pallas_call x1, Pallas kernels, dispatch(): pl.pallas_call(dispatch_kernel, grid=(steps,), in_specs=[pl.BlockSpec(mem...  5.16 us
  transfers between devices with their start and end apart: 28, of which 11 were waited for; matrix products, arithmetic and copies ran while one was open for 4% of the time, Pallas kernels for 0%

profile of v7, /device:TPU:6, one launch (start us, length us, event | category | flops | bytes accessed | tf_op | source)
XLA Modules:
  0.0 187.8 jit_solution(10749392098937913161)
XLA Ops:
  0.6 5.2 %shard_map.93 = (bf16[512,4096]{1,0:T(8,128)(2,1)}, bf16[128,512]{1,0:T(8,128)(2,1)}) custom-call(s32[1]{0:T(128)} %bitcast.10.base, s32[1,32,1024]{2,1,0:T(8,128)} %picks.1, bf16[1,128,2048]{2,1,0:T(8,128)(2,1)} %tokens.1, bf16[1,128,2048]{2,1,0:T(8,128)(2,1)} %out_grad.1), custom_call_target="tpu_custom_call" | custom-call | flops 536870912 | bytes 4194304 | tf_op jit(solution)/shard_map/pallas_call | solution.py:116
  5.8 11.7 %all-to-all-start = ((bf16[32,16,4096]{2,1,0:T(8,128)(2,1)}), bf16[32,16,4096]{2,1,0:T(8,128)(2,1)}, u32[]{:S(2)}, u32[]{:S(2)}) async-start(bf16[32,16,4096]{2,1,0:T(8,128)(2,1)} %bitcast.31), calls=%async_computation | async-start | bytes 8388608 | tf_op jit(solution)/shard_map/all_to_all | solution.py:305
  17.6 0.6 collective-permute-start
  18.1 2.4 %collective-permute-start.1 = (f32[256]{0:T(256)S(1)}, f32[256]{0:T(256)S(1)}, u32[]{:S(2)}, u32[]{:S(2)}) collective-permute-start(f32[256]{0:T(256)S(1)} %bitcast.42), channel_id=1, source_target_pairs={{0,64},{32,96},{64,0},{96,32},{1,65},{33,97},{65,1},{97,33},{2,66}... | collective-permute-start | bytes 3080 | tf_op jit(solution)/shard_map/ppermute | solution.py:328
  20.5 0.8 dynamic-slice_subtract_fusion
  21.3 0.5 convolution_convert_fusion.2
  21.9 0.6 fusion
  22.6 0.6 collective-permute-done.1
  23.2 2.1 %collective-permute-done.2 = f32[256]{0:T(256)S(1)} collective-permute-done((f32[256]{0:T(256)S(1)}, f32[256]{0:T(256)S(1)}, u32[]{:S(2)}, u32[]{:S(2)}) %collective-permute-start.2) | collective-permute-done | bytes 1056 | tf_op jit(solution)/shard_map/ppermute | solution.py:328
  25.4 0.9 select_reduce_fusion.1
  26.3 85.6 %all-to-all-done = bf16[32,16,4096]{2,1,0:T(8,128)(2,1)} async-done(((bf16[32,16,4096]{2,1,0:T(8,128)(2,1)}), bf16[32,16,4096]{2,1,0:T(8,128)(2,1)}, u32[]{:S(2)}, u32[]{:S(2)}) %all-to-all-start) | async-done | bytes 4194336 | tf_op jit(solution)/shard_map/all_to_all | solution.py:305
  111.9 11.3 %shard_map.94 = (f32[1,512]{1,0:T(1,128)}, bf16[512,2048]{1,0:T(8,128)(2,1)}, bf16[256,2048]{1,0:T(8,128)(2,1)}, bf16[2048,256]{1,0:T(8,128)(2,1)}, bf16[256,204...) custom-call(s32[1]{0:T(128)} %bitcast.core, f32[1,512]{1,0:T(1,128)} %bitcast.40, bf16[2048,512]{1,0:T(8,128)(2,1)} %bitcast.52, ...), custom_call_target="tpu_custom_call" | custom-call | flops 5368709120 | bytes 8388608 | tf_op jit(solution)/shard_map/pallas_call | solution.py:229
  123.2 0.1 collective-permute-start.4
  123.3 0.5 collective-permute-start.3
  123.8 7.0 %all-to-all-start.1 = ((bf16[32,16,2048]{2,1,0:T(8,128)(2,1)}), bf16[32,16,2048]{2,1,0:T(8,128)(2,1)}, u32[]{:S(2)}, u32[]{:S(2)}) async-start(bf16[32,16,2048]{2,1,0:T(8,128)(2,1)} %bitcast.32), calls=%async_computation.1 | async-start | bytes 4194304 | tf_op jit(solution)/shard_map/all_to_all | solution.py:305
  130.9 0.3 add_convert_fusion
  131.3 0.8 copy-done
  132.1 0.4 add_convert_fusion.1
  132.5 0.1 constant_dynamic-slice_fusion.9
  132.6 0.9 collective-permute-start.5
  133.5 1.1 collective-permute-start.6
  134.7 0.5 select_reduce_fusion
  135.2 2.2 %collective-permute-start.7 = (f32[256]{0:T(256)S(1)}, f32[256]{0:T(256)S(1)}, u32[]{:S(2)}, u32[]{:S(2)}) collective-permute-start(f32[256]{0:T(256)S(1)} %bitcast.51), channel_id=1, source_target_pairs={{0,32},{32,64},{64,96},{96,0},{1,33},{33,65},{65,97},{97,1},{2,34}... | collective-permute-start | bytes 3080 | tf_op jit(solution)/shard_map/ppermute | solution.py:353
  137.3 0.1 collective-permute-start.8
  137.5 1.3 collective-permute-start.9
  138.8 7.8 %collective-permute-done.7 = f32[256]{0:T(256)S(1)} collective-permute-done((f32[256]{0:T(256)S(1)}, f32[256]{0:T(256)S(1)}, u32[]{:S(2)}, u32[]{:S(2)}) %collective-permute-start.7) | collective-permute-done | bytes 1056 | tf_op jit(solution)/shard_map/ppermute | solution.py:353
  146.6 1.8 collective-permute-done.9
  148.4 0.6 add_add_fusion
  148.9 0.1 add_convert_fusion.2
  149.1 0.1 add_convert_fusion.3
  149.3 1.2 collective-permute-start.10
  150.6 7.2 %collective-permute-done.10 = bf16[64,2048]{1,0:T(8,128)(2,1)S(1)} collective-permute-done((bf16[64,2048]{1,0:T(8,128)(2,1)S(1)}, bf16[64,2048]{1,0:T(8,128)(2,1)S(1)}, u32[]{:S(2)}, u32[]{:S(2)}) %collective-permute-start.10) | collective-permute-done | bytes 262176 | tf_op jit(solution)/shard_map/ppermute | solution.py:48
  157.9 1.8 collective-permute-start.12
  159.7 2.0 %collective-permute-start.14 = (bf16[64,2048]{1,0:T(8,128)(2,1)S(1)}, bf16[64,2048]{1,0:T(8,128)(2,1)S(1)}, u32[]{:S(2)}, u32[]{:S(2)}) collective-permute-start(bf16[64,2048]{1,0:T(8,128)(2,1)S(1)} %add_convert_fusion.5.refs_0_), channel_id=1, source_target_pairs={{0,32},{32,0},{64,96},{96,64},{1,33},{33,1},{65,97},{97,65},{2,34}... | collective-permute-start | bytes 786440 | tf_op jit(solution)/shard_map/ppermute | solution.py:53
  161.7 1.5 collective-permute-start.15
  163.2 5.2 %collective-permute-done.12.refs_1_ = bf16[64,2048]{1,0:T(8,128)(2,1)S(1)} collective-permute-done((bf16[64,2048]{1,0:T(8,128)(2,1)S(1)}, bf16[64,2048]{1,0:T(8,128)(2,1)S(1)}, u32[]{:S(2)}, u32[]{:S(2)}) %collective-permute-start.12) | collective-permute-done | bytes 262176 | tf_op jit(solution)/shard_map/ppermute | solution.py:52
  168.4 0.5 collective-permute-done.13.refs_9_
  169.0 1.5 collective-permute-start.17
  170.5 3.4 %collective-permute-done.14.refs_2_ = bf16[64,2048]{1,0:T(8,128)(2,1)S(1)} collective-permute-done((bf16[64,2048]{1,0:T(8,128)(2,1)S(1)}, bf16[64,2048]{1,0:T(8,128)(2,1)S(1)}, u32[]{:S(2)}, u32[]{:S(2)}) %collective-permute-start.14) | collective-permute-done | bytes 262176 | tf_op jit(solution)/shard_map/ppermute | solution.py:53
  173.9 0.5 collective-permute-start.19
  174.5 2.2 %collective-permute-done.16.refs_3_ = bf16[64,2048]{1,0:T(8,128)(2,1)S(1)} collective-permute-done((bf16[64,2048]{1,0:T(8,128)(2,1)S(1)}, bf16[64,2048]{1,0:T(8,128)(2,1)S(1)}, u32[]{:S(2)}, u32[]{:S(2)}) %collective-permute-start.16) | collective-permute-done | bytes 262176 | tf_op jit(solution)/shard_map/ppermute | solution.py:55
  176.7 0.5 collective-permute-start.20
  177.2 0.1 collective-permute-start.21
  177.3 0.4 collective-permute-start.24
  177.7 0.1 collective-permute-start.25
  177.8 3.6 %all-to-all-done.1 = bf16[32,16,2048]{2,1,0:T(8,128)(2,1)} async-done(((bf16[32,16,2048]{2,1,0:T(8,128)(2,1)}), bf16[32,16,2048]{2,1,0:T(8,128)(2,1)}, u32[]{:S(2)}, u32[]{:S(2)}) %all-to-all-start.1) | async-done | bytes 2097184 | tf_op jit(solution)/shard_map/all_to_all | solution.py:305
  181.4 2.9 %convolution_convert_fusion = bf16[128,2048]{1,0:T(8,128)(2,1)} fusion(bf16[128,512]{1,0:T(8,128)(2,1)S(1)} %copy-done.2, bf16[512,2048]{1,0:T(8,128)(2,1)} %bitcast.19), kind=kOutput, calls=%fused_computation | convolution fusion | flops 268697600 | bytes 2752512 | tf_op jit(solution)/shard_map/dot_general | solution.py:19
  184.3 3.3 %shard_map.95 = (bf16[512,2048]{1,0:T(8,128)(2,1)}, bf16[2048,512]{1,0:T(8,128)(2,1)}) custom-call(s32[3]{0:T(128)S(1)} %pad_add_fusion.where, bf16[64,2048]{1,0:T(8,128)(2,1)S(1)} %add_convert_fusion.5.refs_0_, bf16[64,2048]{1,0:T(8,128)(2,1)S(1)} %collective-permute-done.12.refs_1_, bf16[64,2048]{1,0:T(8,128)(2,1)S(1)} %collective-permute-done.14.refs_2_, ...), custom_call_target="tpu_custom_call" | custom-call | bytes 8388608 | tf_op jit(solution)/shard_map/pallas_call | solution.py:275
  (50 shorter events, 0.7 us)
Async XLA Ops:
  5.8 11.8 %copy-start.4 = (f32[1,1,256]{2,1,0:T(1,128)S(1)}, f32[1,1,256]{2,1,0:T(1,128)}, u32[]{:S(2)}) copy-start(f32[1,1,256]{2,1,0:T(1,128)} %param.11) | copy-start | bytes 3076
  5.8 106.1 %all-to-all-start = ((bf16[32,16,4096]{2,1,0:T(8,128)(2,1)}), bf16[32,16,4096]{2,1,0:T(8,128)(2,1)}, u32[]{:S(2)}, u32[]{:S(2)}) async-start(bf16[32,16,4096]{2,1,0:T(8,128)(2,1)} %bitcast.31), calls=%async_computation | async-start | bytes 8388608 | tf_op jit(solution)/shard_map/all_to_all | solution.py:305
  17.6 5.0 %collective-permute-start = (f32[256]{0:T(256)S(1)}, f32[256]{0:T(256)S(1)}, u32[]{:S(2)}, u32[]{:S(2)}) collective-permute-start(f32[256]{0:T(256)S(1)} %bitcast.41), channel_id=1, source_target_pairs={{0,32},{32,64},{64,96},{96,0},{1,33},{33,65},{65,97},{97,1},{2,34}... | collective-permute-start | bytes 3080 | tf_op jit(solution)/shard_map/ppermute | solution.py:328
  18.1 5.1 %collective-permute-start.1 = (f32[256]{0:T(256)S(1)}, f32[256]{0:T(256)S(1)}, u32[]{:S(2)}, u32[]{:S(2)}) collective-permute-start(f32[256]{0:T(256)S(1)} %bitcast.42), channel_id=1, source_target_pairs={{0,64},{32,96},{64,0},{96,32},{1,65},{33,97},{65,1},{97,33},{2,66}... | collective-permute-start | bytes 3080 | tf_op jit(solution)/shard_map/ppermute | solution.py:328
  20.5 4.8 %collective-permute-start.2 = (f32[256]{0:T(256)S(1)}, f32[256]{0:T(256)S(1)}, u32[]{:S(2)}, u32[]{:S(2)}) collective-permute-start(f32[256]{0:T(256)S(1)} %bitcast.43), channel_id=1, source_target_pairs={{0,96},{32,0},{64,32},{96,64},{1,97},{33,1},{65,33},{97,65},{2,98}... | collective-permute-start | bytes 3080 | tf_op jit(solution)/shard_map/ppermute | solution.py:328
  123.2 7.7 %collective-permute-start.4 = (bf16[2048,256]{1,0:T(8,128)(2,1)}, bf16[2048,256]{1,0:T(8,128)(2,1)S(1)}, u32[]{:S(2)}, u32[]{:S(2)}) collective-permute-start(bf16[2048,256]{1,0:T(8,128)(2,1)} %get-tuple-element.62), channel_id=1, source_target_pairs={{0,128},{128,0},{1,129},{129,1},{2,130},{130,2},{3,131},{131,3},{4... | collective-permute-start | bytes 3145736 | tf_op jit(solution)/shard_map/ppermute | solution.py:341
  123.3 7.9 %collective-permute-start.3 = (bf16[256,2048]{1,0:T(8,128)(2,1)}, bf16[256,2048]{1,0:T(8,128)(2,1)S(1)}, u32[]{:S(2)}, u32[]{:S(2)}) collective-permute-start(bf16[256,2048]{1,0:T(8,128)(2,1)} %get-tuple-element.60), channel_id=1, source_target_pairs={{0,128},{128,0},{1,129},{129,1},{2,130},{130,2},{3,131},{131,3},{4... | collective-permute-start | bytes 3145736 | tf_op jit(solution)/shard_map/ppermute | solution.py:341
  123.8 7.1 %copy-start.1 = (bf16[2048,256]{1,0:T(8,128)(2,1)S(1)}, bf16[2048,256]{1,0:T(8,128)(2,1)}, u32[]{:S(2)}) copy-start(bf16[2048,256]{1,0:T(8,128)(2,1)} %get-tuple-element.61) | copy-start | bytes 3145732
  123.8 57.6 %all-to-all-start.1 = ((bf16[32,16,2048]{2,1,0:T(8,128)(2,1)}), bf16[32,16,2048]{2,1,0:T(8,128)(2,1)}, u32[]{:S(2)}, u32[]{:S(2)}) async-start(bf16[32,16,2048]{2,1,0:T(8,128)(2,1)} %bitcast.32), calls=%async_computation.1 | async-start | bytes 4194304 | tf_op jit(solution)/shard_map/all_to_all | solution.py:305
  130.9 1.2 copy-start
  132.1 2.6 %copy-start.3 = (f32[1,512]{1,0:T(1,128)S(1)}, f32[1,512]{1,0:T(1,128)}, u32[]{:S(2)}) copy-start(f32[1,512]{1,0:T(1,128)} %get-tuple-element.67) | copy-start | bytes 6148
  132.6 16.3 %collective-permute-start.5 = (bf16[128,2048]{1,0:T(8,128)(2,1)S(1)}, bf16[128,2048]{1,0:T(8,128)(2,1)S(1)}, u32[]{:S(2)}, u32[]{:S(2)}) collective-permute-start(bf16[128,2048]{1,0:T(8,128)(2,1)S(1)} %get-tuple-element.63), channel_id=1, source_target_pairs={{0,32},{32,0},{64,96},{96,64},{1,33},{33,1},{65,97},{97,65},{2,34}... | collective-permute-start | bytes 1572872 | tf_op jit(solution)/shard_map/ppermute | solution.py:48
  133.5 15.4 %collective-permute-start.6 = (bf16[1024,256]{1,0:T(8,128)(2,1)S(1)}, bf16[1024,256]{1,0:T(8,128)(2,1)S(1)}, u32[]{:S(2)}, u32[]{:S(2)}) collective-permute-start(bf16[1024,256]{1,0:T(8,128)(2,1)S(1)} %get-tuple-element.64), channel_id=1, source_target_pairs={{0,96},{96,0},{32,64},{64,32},{1,97},{97,1},{33,65},{65,33},{2,98}... | collective-permute-start | bytes 1572872 | tf_op jit(solution)/shard_map/ppermute | solution.py:48
  135.2 11.4 %collective-permute-start.7 = (f32[256]{0:T(256)S(1)}, f32[256]{0:T(256)S(1)}, u32[]{:S(2)}, u32[]{:S(2)}) collective-permute-start(f32[256]{0:T(256)S(1)} %bitcast.51), channel_id=1, source_target_pairs={{0,32},{32,64},{64,96},{96,0},{1,33},{33,65},{65,97},{97,1},{2,34}... | collective-permute-start | bytes 3080 | tf_op jit(solution)/shard_map/ppermute | solution.py:353
  137.3 9.3 %collective-permute-start.8 = (f32[256]{0:T(256)S(1)}, f32[256]{0:T(256)S(1)}, u32[]{:S(2)}, u32[]{:S(2)}) collective-permute-start(f32[256]{0:T(256)S(1)} %bitcast.50), channel_id=1, source_target_pairs={{0,64},{32,96},{64,0},{96,32},{1,65},{33,97},{65,1},{97,33},{2,66}... | collective-permute-start | bytes 3080 | tf_op jit(solution)/shard_map/ppermute | solution.py:353
  137.5 10.9 %collective-permute-start.9 = (f32[256]{0:T(256)S(1)}, f32[256]{0:T(256)S(1)}, u32[]{:S(2)}, u32[]{:S(2)}) collective-permute-start(f32[256]{0:T(256)S(1)} %bitcast.49), channel_id=1, source_target_pairs={{0,96},{32,0},{64,32},{96,64},{1,97},{33,1},{65,33},{97,65},{2,98}... | collective-permute-start | bytes 3080 | tf_op jit(solution)/shard_map/ppermute | solution.py:353
  149.1 32.3 %copy-start.2 = (bf16[128,512]{1,0:T(8,128)(2,1)S(1)}, bf16[128,512]{1,0:T(8,128)(2,1)}, u32[]{:S(2)}) copy-start(bf16[128,512]{1,0:T(8,128)(2,1)} %get-tuple-element.89) | copy-start | bytes 393220
  149.3 8.4 %collective-permute-start.10 = (bf16[64,2048]{1,0:T(8,128)(2,1)S(1)}, bf16[64,2048]{1,0:T(8,128)(2,1)S(1)}, u32[]{:S(2)}, u32[]{:S(2)}) collective-permute-start(bf16[64,2048]{1,0:T(8,128)(2,1)S(1)} %get-tuple-element.72), channel_id=1, source_target_pairs={{0,96},{96,0},{32,64},{64,32},{1,97},{97,1},{33,65},{65,33},{2,98}... | collective-permute-start | bytes 786440 | tf_op jit(solution)/shard_map/ppermute | solution.py:48
  150.6 7.2 %collective-permute-start.11 = (bf16[512,256]{1,0:T(8,128)(2,1)S(1)}, bf16[512,256]{1,0:T(8,128)(2,1)S(1)}, u32[]{:S(2)}, u32[]{:S(2)}) collective-permute-start(bf16[512,256]{1,0:T(8,128)(2,1)S(1)} %get-tuple-element.73), channel_id=1, source_target_pairs={{0,32},{32,0},{64,96},{96,64},{1,33},{33,1},{65,97},{97,65},{2,34}... | collective-permute-start | bytes 786440 | tf_op jit(solution)/shard_map/ppermute | solution.py:48
  157.9 10.5 %collective-permute-start.12 = (bf16[64,2048]{1,0:T(8,128)(2,1)S(1)}, bf16[64,2048]{1,0:T(8,128)(2,1)S(1)}, u32[]{:S(2)}, u32[]{:S(2)}) collective-permute-start(bf16[64,2048]{1,0:T(8,128)(2,1)S(1)} %add_convert_fusion.5.refs_0_), channel_id=1, source_target_pairs={{0,96},{96,0},{32,64},{64,32},{1,97},{97,1},{33,65},{65,33},{2,98}... | collective-permute-start | bytes 786440 | tf_op jit(solution)/shard_map/ppermute | solution.py:52
  159.7 9.2 %collective-permute-start.13 = (bf16[512,256]{1,0:T(8,128)(2,1)S(1)}, bf16[512,256]{1,0:T(8,128)(2,1)S(1)}, u32[]{:S(2)}, u32[]{:S(2)}) collective-permute-start(bf16[512,256]{1,0:T(8,128)(2,1)S(1)} %add_convert_fusion.4.refs_8_), channel_id=1, source_target_pairs={{0,32},{32,0},{64,96},{96,64},{1,33},{33,1},{65,97},{97,65},{2,34}... | collective-permute-start | bytes 786440 | tf_op jit(solution)/shard_map/ppermute | solution.py:52
  159.7 14.2 %collective-permute-start.14 = (bf16[64,2048]{1,0:T(8,128)(2,1)S(1)}, bf16[64,2048]{1,0:T(8,128)(2,1)S(1)}, u32[]{:S(2)}, u32[]{:S(2)}) collective-permute-start(bf16[64,2048]{1,0:T(8,128)(2,1)S(1)} %add_convert_fusion.5.refs_0_), channel_id=1, source_target_pairs={{0,32},{32,0},{64,96},{96,64},{1,33},{33,1},{65,97},{97,65},{2,34}... | collective-permute-start | bytes 786440 | tf_op jit(solution)/shard_map/ppermute | solution.py:53
  161.7 12.2 %collective-permute-start.15 = (bf16[512,256]{1,0:T(8,128)(2,1)S(1)}, bf16[512,256]{1,0:T(8,128)(2,1)S(1)}, u32[]{:S(2)}, u32[]{:S(2)}) collective-permute-start(bf16[512,256]{1,0:T(8,128)(2,1)S(1)} %add_convert_fusion.4.refs_8_), channel_id=1, source_target_pairs={{0,96},{96,0},{32,64},{64,32},{1,97},{97,1},{33,65},{65,33},{2,98}... | collective-permute-start | bytes 786440 | tf_op jit(solution)/shard_map/ppermute | solution.py:53
  169.0 7.7 %collective-permute-start.16 = (bf16[64,2048]{1,0:T(8,128)(2,1)S(1)}, bf16[64,2048]{1,0:T(8,128)(2,1)S(1)}, u32[]{:S(2)}, u32[]{:S(2)}) collective-permute-start(bf16[64,2048]{1,0:T(8,128)(2,1)S(1)} %collective-permute-done.12.refs_1_), channel_id=1, source_target_pairs={{0,32},{32,0},{64,96},{96,64},{1,33},{33,1},{65,97},{97,65},{2,34}... | collective-permute-start | bytes 786440 | tf_op jit(solution)/shard_map/ppermute | solution.py:55
  169.0 7.7 %collective-permute-start.17 = (bf16[512,256]{1,0:T(8,128)(2,1)S(1)}, bf16[512,256]{1,0:T(8,128)(2,1)S(1)}, u32[]{:S(2)}, u32[]{:S(2)}) collective-permute-start(bf16[512,256]{1,0:T(8,128)(2,1)S(1)} %collective-permute-done.13.refs_9_), channel_id=1, source_target_pairs={{0,96},{96,0},{32,64},{64,32},{1,97},{97,1},{33,65},{65,33},{2,98}... | collective-permute-start | bytes 786440 | tf_op jit(solution)/shard_map/ppermute | solution.py:55
  170.5 6.7 %collective-permute-start.18 = (bf16[64,2048]{1,0:T(8,128)(2,1)S(1)}, bf16[64,2048]{1,0:T(8,128)(2,1)S(1)}, u32[]{:S(2)}, u32[]{:S(2)}) collective-permute-start(bf16[64,2048]{1,0:T(8,128)(2,1)S(1)} %add_convert_fusion.5.refs_0_), channel_id=1, source_target_pairs={{0,128},{128,0},{1,129},{129,1},{2,130},{130,2},{3,131},{131,3},{4... | collective-permute-start | bytes 786440 | tf_op jit(solution)/shard_map/ppermute | solution.py:358
  173.9 3.4 %collective-permute-start.22 = (bf16[512,256]{1,0:T(8,128)(2,1)S(1)}, bf16[512,256]{1,0:T(8,128)(2,1)S(1)}, u32[]{:S(2)}, u32[]{:S(2)}) collective-permute-start(bf16[512,256]{1,0:T(8,128)(2,1)S(1)} %add_convert_fusion.4.refs_8_), channel_id=1, source_target_pairs={{0,128},{128,0},{1,129},{129,1},{2,130},{130,2},{3,131},{131,3},{4... | collective-permute-start | bytes 786440 | tf_op jit(solution)/shard_map/ppermute | solution.py:358
  173.9 3.8 %collective-permute-start.19 = (bf16[64,2048]{1,0:T(8,128)(2,1)S(1)}, bf16[64,2048]{1,0:T(8,128)(2,1)S(1)}, u32[]{:S(2)}, u32[]{:S(2)}) collective-permute-start(bf16[64,2048]{1,0:T(8,128)(2,1)S(1)} %collective-permute-done.12.refs_1_), channel_id=1, source_target_pairs={{0,128},{128,0},{1,129},{129,1},{2,130},{130,2},{3,131},{131,3},{4... | collective-permute-start | bytes 786440 | tf_op jit(solution)/shard_map/ppermute | solution.py:358
  176.7 7.6 %collective-permute-start.23 = (bf16[512,256]{1,0:T(8,128)(2,1)S(1)}, bf16[512,256]{1,0:T(8,128)(2,1)S(1)}, u32[]{:S(2)}, u32[]{:S(2)}) collective-permute-start(bf16[512,256]{1,0:T(8,128)(2,1)S(1)} %collective-permute-done.13.refs_9_), channel_id=1, source_target_pairs={{0,128},{128,0},{1,129},{129,1},{2,130},{130,2},{3,131},{131,3},{4... | collective-permute-start | bytes 786440 | tf_op jit(solution)/shard_map/ppermute | solution.py:358
  176.7 7.6 %collective-permute-start.20 = (bf16[64,2048]{1,0:T(8,128)(2,1)S(1)}, bf16[64,2048]{1,0:T(8,128)(2,1)S(1)}, u32[]{:S(2)}, u32[]{:S(2)}) collective-permute-start(bf16[64,2048]{1,0:T(8,128)(2,1)S(1)} %collective-permute-done.14.refs_2_), channel_id=1, source_target_pairs={{0,128},{128,0},{1,129},{129,1},{2,130},{130,2},{3,131},{131,3},{4... | collective-permute-start | bytes 786440 | tf_op jit(solution)/shard_map/ppermute | solution.py:358
  177.2 7.1 %collective-permute-start.21 = (bf16[64,2048]{1,0:T(8,128)(2,1)S(1)}, bf16[64,2048]{1,0:T(8,128)(2,1)}, u32[]{:S(2)}, u32[]{:S(2)}) collective-permute-start(bf16[64,2048]{1,0:T(8,128)(2,1)S(1)} %collective-permute-done.16.refs_3_), channel_id=1, source_target_pairs={{0,128},{128,0},{1,129},{129,1},{2,130},{130,2},{3,131},{131,3},{4... | collective-permute-start | bytes 786440 | tf_op jit(solution)/shard_map/ppermute | solution.py:358
  177.3 7.0 %collective-permute-start.24 = (bf16[512,256]{1,0:T(8,128)(2,1)S(1)}, bf16[512,256]{1,0:T(8,128)(2,1)}, u32[]{:S(2)}, u32[]{:S(2)}) collective-permute-start(bf16[512,256]{1,0:T(8,128)(2,1)S(1)} %collective-permute-done.15.refs_10_), channel_id=1, source_target_pairs={{0,128},{128,0},{1,129},{129,1},{2,130},{130,2},{3,131},{131,3},{4... | collective-permute-start | bytes 786440 | tf_op jit(solution)/shard_map/ppermute | solution.py:358
  177.7 6.6 %collective-permute-start.25 = (bf16[512,256]{1,0:T(8,128)(2,1)S(1)}, bf16[512,256]{1,0:T(8,128)(2,1)}, u32[]{:S(2)}, u32[]{:S(2)}) collective-permute-start(bf16[512,256]{1,0:T(8,128)(2,1)S(1)} %collective-permute-done.17.refs_11_), channel_id=1, source_target_pairs={{0,128},{128,0},{1,129},{129,1},{2,130},{130,2},{3,131},{131,3},{4... | collective-permute-start | bytes 786440 | tf_op jit(solution)/shard_map/ppermute | solution.py:358
